TPU v7x, 32 devices: a whole 2x2x4 slice. The times are simulated.
32 devices in a mesh: blk: 16 (over z, x, core), rep: 2 (over y).
Axes of the slice: x: 2, y: 2, z: 4, core: 2. Of those that a mesh axis runs over, the one named last changes fastest.
Arguments:
- integrals: bfloat16 [16, 512, 1024], P('blk'), may hold values from -0.59765625 to 0.59765625
- eps_occ: float32 [16], replicated, may hold values from -2 to -0.5
- eps_vir: float32 [512], replicated, may hold values from 0.5 to 3
- offsets: int32 [8], P('rep'), may hold values from 0 to 7
Outputs:
- gamma: float32 [16, 512, 1024], P('blk', None, 'rep')
All inputs are finite; a program needn't handle non-finite values.
Results may differ from a plain program's by a relative error of at most 0.0017.
Values may be sent and summed in bfloat16 or wider, within the bound.
No kernel may reach another device: no remote copies, remote signals or barrier semaphores. Data moves between devices by JAX's collectives and lax.ppermute only.
A program may use at most 64 MiB of HBM per device.

v0:
```python
import jax
import jax.numpy as jnp
from jax import lax
from jax.sharding import PartitionSpec as P


def shifted(block, axis, distance):
    devices = range(lax.axis_size(axis))
    route = [((i - distance) % len(devices), i) for i in devices]
    return lax.ppermute(block, axis, route)


def walk_ahead(tile, offset):
    for level in range(lax.axis_size("blk").bit_length() - 2):
        moved = shifted(tile, "blk", 1 << level)
        tile = jnp.where(offset // (1 << level) % 2 == 1, moved, tile)
    return tile


def walk_back(tile, offset):
    for level in range(lax.axis_size("blk").bit_length() - 2):
        moved = shifted(tile, "blk", -(1 << level))
        tile = jnp.where(offset // (1 << level) % 2 == 1, moved, tile)
    return tile


def pair_amp(left, right, e_left, e_right, eps_vir):
    pair = lax.dot_general(
        left, right, (((1,), (1,)), ((), ())), preferred_element_type=jnp.float32
    )
    denom = eps_vir[:, None] + eps_vir[None, :] - e_left - e_right
    return (-pair / denom).astype(jnp.bfloat16)


def per_device(integrals, eps_occ, eps_vir, offsets):
    tile = integrals[0]
    occupied = eps_occ.shape[0]
    here = lax.axis_index("blk")
    e_here = lax.dynamic_index_in_dim(eps_occ, here, keepdims=False)
    total = jnp.zeros(tile.shape, jnp.float32)
    for slot in range(offsets.shape[0]):
        shift = offsets[slot]
        other = walk_ahead(tile, shift)
        e_other = lax.dynamic_index_in_dim(eps_occ, (here - shift) % occupied, keepdims=False)
        amp = pair_amp(tile, other, e_here, e_other, eps_vir)
        own = jnp.dot(amp, other, preferred_element_type=jnp.float32)
        below = walk_back(tile, shift)
        e_below = lax.dynamic_index_in_dim(eps_occ, (here + shift) % occupied, keepdims=False)
        amp_below = pair_amp(below, tile, e_below, e_here, eps_vir)
        part = lax.dot_general(
            amp_below, below, (((0,), (0,)), ((), ())), preferred_element_type=jnp.float32
        )
        part = lax.optimization_barrier(part.astype(jnp.bfloat16)).astype(jnp.float32)
        total = total + own + part
    gamma = lax.psum_scatter(total, "rep", scatter_dimension=1, tiled=True)
    return gamma[None]


def solution(mesh):
    in_specs = (P("blk", None, None), P(), P(), P("rep"))
    out_specs = P("blk", None, "rep")
    return jax.shard_map(
        per_device, mesh=mesh, in_specs=in_specs, out_specs=out_specs, check_vma=False
    )
```

profile of v0, /device:TPU:0, one launch (start us, length us, event | category | flops | bytes accessed | tf_op | source)
XLA Modules:
  0.0 434.8 jit_solution(1844439295921808852)
XLA Ops:
  6.5 5.4 %collective-permute-start.3 = (bf16[512,1024]{1,0:T(8,128)(2,1)}, bf16[512,1024]{1,0:T(8,128)(2,1)S(1)}, u32[]{:S(2)}, u32[]{:S(2)}) collective-permute-start(bf16[512,1024]{1,0:T(8,128)(2,1)} %bitcast.79), channel_id=1, source_target_pairs={{2,0},{4,2},{6,4},{8,6},{10,8},{12,10},{14,12},{16,14},{18,16},{20... | collective-permute-start | bytes 3145736 | tf_op jit(solution)/shard_map/ppermute | solution.py:10
  20.9 3.6 collective-permute-done.3
  25.6 3.7 collective-permute-done
  29.3 4.5 %broadcast_select_fusion.12 = (bf16[512,1024]{1,0:T(8,128)(2,1)}, bf16[512,1024]{1,0:T(8,128)(2,1)}, bf16[512,1024]{1,0:T(8,128)(2,1)}, bf16[512,1024]{1,0:T(8,1...) fusion(bf16[512,1024]{1,0:T(8,128)(2,1)} %copy-done.2, ...), kind=kLoop, calls=%fused_computation.76 | loop fusion | flops 4194304 | bytes 11534340 | tf_op jit(solution)/shard_map/jit(_where)/select_n | solution.py:23
  33.8 9.0 %collective-permute-start.8 = (bf16[512,1024]{1,0:T(8,128)(2,1)}, bf16[512,1024]{1,0:T(8,128)(2,1)}, u32[]{:S(2)}, u32[]{:S(2)}) collective-permute-start(bf16[512,1024]{1,0:T(8,128)(2,1)} %get-tuple-element.8), channel_id=1, source_target_pairs={{4,0},{6,2},{8,4},{10,6},{12,8},{14,10},{16,12},{18,14},{20,16},{2... | collective-permute-start | bytes 3145736 | tf_op jit(solution)/shard_map/ppermute | solution.py:10
  42.8 4.7 %collective-permute-start.4 = (bf16[512,1024]{1,0:T(8,128)(2,1)}, bf16[512,1024]{1,0:T(8,128)(2,1)}, u32[]{:S(2)}, u32[]{:S(2)}) collective-permute-start(bf16[512,1024]{1,0:T(8,128)(2,1)} %get-tuple-element.5), channel_id=1, source_target_pairs={{4,0},{6,2},{8,4},{10,6},{12,8},{14,10},{16,12},{18,14},{20,16},{2... | collective-permute-start | bytes 3145736 | tf_op jit(solution)/shard_map/ppermute | solution.py:10
  56.3 30.0 %collective-permute-done.8 = bf16[512,1024]{1,0:T(8,128)(2,1)} collective-permute-done((bf16[512,1024]{1,0:T(8,128)(2,1)}, bf16[512,1024]{1,0:T(8,128)(2,1)}, u32[]{:S(2)}, u32[]{:S(2)}) %collective-permute-start.8) | collective-permute-done | bytes 1048608 | tf_op jit(solution)/shard_map/ppermute | solution.py:10
  86.3 2.3 broadcast_select_fusion.10
  88.6 64.6 %collective-permute-done.6 = bf16[512,1024]{1,0:T(8,128)(2,1)} collective-permute-done((bf16[512,1024]{1,0:T(8,128)(2,1)}, bf16[512,1024]{1,0:T(8,128)(2,1)}, u32[]{:S(2)}, u32[]{:S(2)}) %collective-permute-start.6) | collective-permute-done | bytes 1048608 | tf_op jit(solution)/shard_map/ppermute | solution.py:10
  153.2 2.5 collective-permute-start.14
  155.6 2.3 broadcast_select_fusion.11
  159.8 2.4 collective-permute-start.5
  162.2 2.3 broadcast_select_fusion.2
  164.5 56.5 %collective-permute-done.12 = bf16[512,1024]{1,0:T(8,128)(2,1)S(1)} collective-permute-done((bf16[512,1024]{1,0:T(8,128)(2,1)}, bf16[512,1024]{1,0:T(8,128)(2,1)S(1)}, u32[]{:S(2)}, u32[]{:S(2)}) %collective-permute-start.12) | collective-permute-done | bytes 1048608 | tf_op jit(solution)/shard_map/ppermute | solution.py:10
  221.0 3.6 collective-permute-start.17
  233.2 4.1 convolution_convert_fusion.3
  237.3 11.2 %collective-permute-done.17 = bf16[512,1024]{1,0:T(8,128)(2,1)} collective-permute-done((bf16[512,1024]{1,0:T(8,128)(2,1)}, bf16[512,1024]{1,0:T(8,128)(2,1)}, u32[]{:S(2)}, u32[]{:S(2)}) %collective-permute-start.17) | collective-permute-done | bytes 1048608 | tf_op jit(solution)/shard_map/ppermute | solution.py:10
  248.9 5.3 %convolution_convert_fusion = bf16[512,1024]{1,0:T(8,128)(2,1)} fusion(bf16[512,1024]{1,0:T(8,128)(2,1)} %collective-permute-done.17, bf16[512,1024]{1,0:T(8,128)(2,1)} %broadcast_select_fusion.2, pred[]{:T(512)S(6)} %eq.90, f32[]{:T(128)} %bitcast.17, f32[]{:T(128)} %bitcast.3, f32[512]{0:T(512)S(1)} %copy-done.6, bf16[1,512,1024]{2,1,0:T(8,128)(2,1)S(1)} %copy-done.1), kind=kOutput, calls=%fused_computation.10 | convolution fusion | flops 1076887552 | bytes 4196361 | tf_op jit(solution)/shard_map/dot_general | solution.py:50
  254.1 16.8 %collective-permute-done.13 = bf16[512,1024]{1,0:T(8,128)(2,1)} collective-permute-done((bf16[512,1024]{1,0:T(8,128)(2,1)}, bf16[512,1024]{1,0:T(8,128)(2,1)}, u32[]{:S(2)}, u32[]{:S(2)}) %collective-permute-start.13) | collective-permute-done | bytes 1048608 | tf_op jit(solution)/shard_map/ppermute | solution.py:10
  271.3 5.3 %convolution_convert_fusion.1 = bf16[512,1024]{1,0:T(8,128)(2,1)} fusion(bf16[512,1024]{1,0:T(8,128)(2,1)} %collective-permute-done.13, bf16[512,1024]{1,0:T(8,128)(2,1)} %broadcast_select_fusion.6, pred[]{:T(512)S(6)} %eq.87, f32[]{:T(128)} %bitcast.13, f32[]{:T(128)} %bitcast.3, f32[512]{0:T(512)S(1)} %copy-done.6, bf16[1,512,1024]{2,1,0:T(8,128)(2,1)S(1)} %copy-done.1), kind=kOutput, calls=%fused_computation.11 | convolution fusion | flops 1076887552 | bytes 4196361 | tf_op jit(solution)/shard_map/dot_general | solution.py:50
  276.6 16.8 %collective-permute-done.9 = bf16[512,1024]{1,0:T(8,128)(2,1)} collective-permute-done((bf16[512,1024]{1,0:T(8,128)(2,1)}, bf16[512,1024]{1,0:T(8,128)(2,1)}, u32[]{:S(2)}, u32[]{:S(2)}) %collective-permute-start.9) | collective-permute-done | bytes 1048608 | tf_op jit(solution)/shard_map/ppermute | solution.py:10
  293.4 5.2 %convolution_convert_fusion.2 = bf16[512,1024]{1,0:T(8,128)(2,1)} fusion(bf16[512,1024]{1,0:T(8,128)(2,1)} %collective-permute-done.9, bf16[512,1024]{1,0:T(8,128)(2,1)} %broadcast_select_fusion.10, pred[]{:T(512)S(6)} %eq.84, f32[]{:T(128)} %bitcast.9, f32[]{:T(128)} %bitcast.3, f32[512]{0:T(512)S(1)} %copy-done.6, bf16[1,512,1024]{2,1,0:T(8,128)(2,1)S(1)} %copy-done.1), kind=kOutput, calls=%fused_computation.12 | convolution fusion | flops 1076887552 | bytes 4196361 | tf_op jit(solution)/shard_map/dot_general | solution.py:50
  298.6 18.0 %collective-permute-done.7 = bf16[512,1024]{1,0:T(8,128)(2,1)} collective-permute-done((bf16[512,1024]{1,0:T(8,128)(2,1)}, bf16[512,1024]{1,0:T(8,128)(2,1)}, u32[]{:S(2)}, u32[]{:S(2)}) %collective-permute-start.7) | collective-permute-done | bytes 1048608 | tf_op jit(solution)/shard_map/ppermute | solution.py:10
  316.7 4.6 %fusion.26 = f32[512,1024]{1,0:T(8,128)S(1)} fusion(bf16[512,1024]{1,0:T(8,128)(2,1)} %collective-permute-done.7, bf16[512,1024]{1,0:T(8,128)(2,1)} %broadcast_select_fusion.11, pred[]{:T(512)S(6)} %eq.84, f32[]{:T(128)} %bitcast.8, f32[]{:T(128)} %bitcast.3, f32[512]{0:T(512)S(1)} %copy-done.6, bf16[1,512,1024]{2,1,0:T(8,128)(2,1)} %param.4), kind=kOutput, calls=%fused_computation.44 | convolution fusion | flops 1076363264 | bytes 5244937 | tf_op jit(solution)/shard_map/dot_general | solution.py:46
  321.3 17.9 %collective-permute-done.11 = bf16[512,1024]{1,0:T(8,128)(2,1)} collective-permute-done((bf16[512,1024]{1,0:T(8,128)(2,1)}, bf16[512,1024]{1,0:T(8,128)(2,1)}, u32[]{:S(2)}, u32[]{:S(2)}) %collective-permute-start.11) | collective-permute-done | bytes 1048608 | tf_op jit(solution)/shard_map/ppermute | solution.py:10
  339.2 5.9 %fusion.25 = f32[512,1024]{1,0:T(8,128)} fusion(bf16[512,1024]{1,0:T(8,128)(2,1)} %collective-permute-done.11, bf16[512,1024]{1,0:T(8,128)(2,1)} %broadcast_select_fusion.7, pred[]{:T(512)S(6)} %eq.87, f32[]{:T(128)} %bitcast.12, f32[]{:T(128)} %bitcast.3, f32[512]{0:T(512)S(1)} %copy-done.6, bf16[1,512,1024]{2,1,0:T(8,128)(2,1)} %param.4), kind=kOutput, calls=%fused_computation.43 | convolution fusion | flops 1076363264 | bytes 5244937 | tf_op jit(solution)/shard_map/dot_general | solution.py:46
  345.1 16.5 %collective-permute-done.15 = bf16[512,1024]{1,0:T(8,128)(2,1)} collective-permute-done((bf16[512,1024]{1,0:T(8,128)(2,1)}, bf16[512,1024]{1,0:T(8,128)(2,1)}, u32[]{:S(2)}, u32[]{:S(2)}) %collective-permute-start.15) | collective-permute-done | bytes 1048608 | tf_op jit(solution)/shard_map/ppermute | solution.py:10
  361.6 5.9 %fusion.24 = f32[512,1024]{1,0:T(8,128)} fusion(bf16[512,1024]{1,0:T(8,128)(2,1)} %collective-permute-done.15, bf16[512,1024]{1,0:T(8,128)(2,1)} %broadcast_select_fusion.3, pred[]{:T(512)S(6)} %eq.90, f32[]{:T(128)} %bitcast.16, f32[]{:T(128)} %bitcast.3, f32[512]{0:T(512)S(1)} %copy-done.6, bf16[1,512,1024]{2,1,0:T(8,128)(2,1)} %param.4), kind=kOutput, calls=%fused_computation.42 | convolution fusion | flops 1076363264 | bytes 5244937 | tf_op jit(solution)/shard_map/dot_general | solution.py:46
  367.5 16.1 %collective-permute-done.2 = bf16[512,1024]{1,0:T(8,128)(2,1)} collective-permute-done((bf16[512,1024]{1,0:T(8,128)(2,1)}, bf16[512,1024]{1,0:T(8,128)(2,1)}, u32[]{:S(2)}, u32[]{:S(2)}) %collective-permute-start.2) | collective-permute-done | bytes 1048608 | tf_op jit(solution)/shard_map/ppermute | solution.py:10
  383.6 5.9 %fusion.27 = f32[512,1024]{1,0:T(8,128)} fusion(bf16[512,1024]{1,0:T(8,128)(2,1)} %collective-permute-done.2, bf16[512,1024]{1,0:T(8,128)(2,1)} %broadcast_select_fusion.15, pred[]{:T(512)S(6)} %eq.81, f32[]{:T(128)} %bitcast.4, f32[]{:T(128)} %bitcast.3, f32[512]{0:T(512)S(1)} %copy-done.6, bf16[1,512,1024]{2,1,0:T(8,128)(2,1)} %param.4), kind=kOutput, calls=%fused_computation.45 | convolution fusion | flops 1076363264 | bytes 5244937 | tf_op jit(solution)/shard_map/dot_general | solution.py:46
  389.5 6.6 %convert_add_fusion = f32[512,1024]{1,0:T(8,128)} fusion(bf16[512,1024]{1,0:T(8,128)(2,1)} %convolution_convert_fusion, f32[512,1024]{1,0:T(8,128)} %fusion.24, bf16[512,1024]{1,0:T(8,128)(2,1)} %convolution_convert_fusion.1, f32[512,1024]{1,0:T(8,128)} %fusion.25, bf16[512,1024]{1,0:T(8,128)(2,1)} %convolution_convert_fusion.2, f32[512,1024]{1,0:T(8,128)S(1)} %fusion.26, ...), kind=kLoop, calls=%fused_computation.9 | loop fusion | flops 5767168 | bytes 14680064 | tf_op jit(solution)/shard_map/add | solution.py:54
  396.2 31.8 %reduce-scatter.2.cloned.1.call-done = f32[512,512]{1,0:T(8,128)} async-done(((f32[512,1024]{1,0:T(8,128)}), f32[512,512]{1,0:T(8,128)}) %reduce-scatter.2.cloned.1.call-update) | async-done | bytes 1048592 | tf_op jit(solution)/shard_map/reduce_scatter | solution.py:55
  (41 shorter events, 14.5 us)
Async XLA Ops:
  6.5 421.4 %reduce-scatter.2.cloned.1.call-start = ((), (), s32[]{:S(2)}) async-start(), calls=%async_computation.1 | async-start | bytes 3145728 | tf_op jit(solution)/shard_map/reduce_scatter | solution.py:55
  6.5 18.0 %collective-permute-start.3 = (bf16[512,1024]{1,0:T(8,128)(2,1)}, bf16[512,1024]{1,0:T(8,128)(2,1)S(1)}, u32[]{:S(2)}, u32[]{:S(2)}) collective-permute-start(bf16[512,1024]{1,0:T(8,128)(2,1)} %bitcast.79), channel_id=1, source_target_pairs={{2,0},{4,2},{6,4},{8,6},{10,8},{12,10},{14,12},{16,14},{18,16},{20... | collective-permute-start | bytes 3145736 | tf_op jit(solution)/shard_map/ppermute | solution.py:10
  12.0 17.3 %collective-permute-start = (bf16[512,1024]{1,0:T(8,128)(2,1)}, bf16[512,1024]{1,0:T(8,128)(2,1)}, u32[]{:S(2)}, u32[]{:S(2)}) collective-permute-start(bf16[512,1024]{1,0:T(8,128)(2,1)} %bitcast.80), channel_id=1, source_target_pairs={{30,0},{0,2},{2,4},{4,6},{6,8},{8,10},{10,12},{12,14},{14,16},{16,... | collective-permute-start | bytes 3145736 | tf_op jit(solution)/shard_map/ppermute | solution.py:10
  20.9 34.5 %copy-start.4 = (f32[16]{0:T(128)S(1)}, f32[16]{0:T(128)}, u32[]{:S(2)}) copy-start(f32[16]{0:T(128)} %param.5) | copy-start | bytes 196
  24.6 1.0 copy-start.2
  33.8 52.5 %collective-permute-start.8 = (bf16[512,1024]{1,0:T(8,128)(2,1)}, bf16[512,1024]{1,0:T(8,128)(2,1)}, u32[]{:S(2)}, u32[]{:S(2)}) collective-permute-start(bf16[512,1024]{1,0:T(8,128)(2,1)} %get-tuple-element.8), channel_id=1, source_target_pairs={{4,0},{6,2},{8,4},{10,6},{12,8},{14,10},{16,12},{18,14},{20,16},{2... | collective-permute-start | bytes 3145736 | tf_op jit(solution)/shard_map/ppermute | solution.py:10
  42.8 110.4 %collective-permute-start.6 = (bf16[512,1024]{1,0:T(8,128)(2,1)}, bf16[512,1024]{1,0:T(8,128)(2,1)}, u32[]{:S(2)}, u32[]{:S(2)}) collective-permute-start(bf16[512,1024]{1,0:T(8,128)(2,1)} %get-tuple-element.13), channel_id=1, source_target_pairs={{28,0},{30,2},{0,4},{2,6},{4,8},{6,10},{8,12},{10,14},{12,16},{14,... | collective-permute-start | bytes 3145736 | tf_op jit(solution)/shard_map/ppermute | solution.py:10
  42.8 115.1 %collective-permute-start.4 = (bf16[512,1024]{1,0:T(8,128)(2,1)}, bf16[512,1024]{1,0:T(8,128)(2,1)}, u32[]{:S(2)}, u32[]{:S(2)}) collective-permute-start(bf16[512,1024]{1,0:T(8,128)(2,1)} %get-tuple-element.5), channel_id=1, source_target_pairs={{4,0},{6,2},{8,4},{10,6},{12,8},{14,10},{16,12},{18,14},{20,16},{2... | collective-permute-start | bytes 3145736 | tf_op jit(solution)/shard_map/ppermute | solution.py:10
  47.5 112.3 %collective-permute-start.16 = (bf16[512,1024]{1,0:T(8,128)(2,1)}, bf16[512,1024]{1,0:T(8,128)(2,1)}, u32[]{:S(2)}, u32[]{:S(2)}) collective-permute-start(bf16[512,1024]{1,0:T(8,128)(2,1)} %get-tuple-element.6), channel_id=1, source_target_pairs={{4,0},{6,2},{8,4},{10,6},{12,8},{14,10},{16,12},{18,14},{20,16},{2... | collective-permute-start | bytes 3145736 | tf_op jit(solution)/shard_map/ppermute | solution.py:10
  56.2 164.8 %collective-permute-start.12 = (bf16[512,1024]{1,0:T(8,128)(2,1)}, bf16[512,1024]{1,0:T(8,128)(2,1)S(1)}, u32[]{:S(2)}, u32[]{:S(2)}) collective-permute-start(bf16[512,1024]{1,0:T(8,128)(2,1)} %get-tuple-element.7), channel_id=1, source_target_pairs={{4,0},{6,2},{8,4},{10,6},{12,8},{14,10},{16,12},{18,14},{20,16},{2... | collective-permute-start | bytes 3145736 | tf_op jit(solution)/shard_map/ppermute | solution.py:10
  86.3 139.5 %collective-permute-start.10 = (bf16[512,1024]{1,0:T(8,128)(2,1)S(1)}, bf16[512,1024]{1,0:T(8,128)(2,1)S(1)}, u32[]{:S(2)}, u32[]{:S(2)}) collective-permute-start(bf16[512,1024]{1,0:T(8,128)(2,1)S(1)} %get-tuple-element.14), channel_id=1, source_target_pairs={{28,0},{30,2},{0,4},{2,6},{4,8},{6,10},{8,12},{10,14},{12,16},{14,... | collective-permute-start | bytes 3145736 | tf_op jit(solution)/shard_map/ppermute | solution.py:10
  153.2 74.1 %collective-permute-start.14 = (bf16[512,1024]{1,0:T(8,128)(2,1)S(1)}, bf16[512,1024]{1,0:T(8,128)(2,1)S(1)}, u32[]{:S(2)}, u32[]{:S(2)}) collective-permute-start(bf16[512,1024]{1,0:T(8,128)(2,1)S(1)} %get-tuple-element.15), channel_id=1, source_target_pairs={{28,0},{30,2},{0,4},{2,6},{4,8},{6,10},{8,12},{10,14},{12,16},{14,... | collective-permute-start | bytes 3145736 | tf_op jit(solution)/shard_map/ppermute | solution.py:10
  157.9 71.0 %collective-permute-start.1 = (bf16[512,1024]{1,0:T(8,128)(2,1)S(1)}, bf16[512,1024]{1,0:T(8,128)(2,1)S(1)}, u32[]{:S(2)}, u32[]{:S(2)}) collective-permute-start(bf16[512,1024]{1,0:T(8,128)(2,1)S(1)} %get-tuple-element.16), channel_id=1, source_target_pairs={{28,0},{30,2},{0,4},{2,6},{4,8},{6,10},{8,12},{10,14},{12,16},{14,... | collective-permute-start | bytes 3145736 | tf_op jit(solution)/shard_map/ppermute | solution.py:10
  159.7 66.0 %copy-start.3 = (bf16[512,1024]{1,0:T(8,128)(2,1)}, bf16[512,1024]{1,0:T(8,128)(2,1)S(1)}, u32[]{:S(2)}) copy-start(bf16[512,1024]{1,0:T(8,128)(2,1)S(1)} %broadcast_select_fusion.14) | copy-start | bytes 3145732
  159.8 64.8 %copy-start = (bf16[512,1024]{1,0:T(8,128)(2,1)S(1)}, bf16[512,1024]{1,0:T(8,128)(2,1)}, u32[]{:S(2)}) copy-start(bf16[512,1024]{1,0:T(8,128)(2,1)} %get-tuple-element.7) | copy-start | bytes 3145732
  159.8 71.8 %collective-permute-start.5 = (bf16[512,1024]{1,0:T(8,128)(2,1)S(1)}, bf16[512,1024]{1,0:T(8,128)(2,1)S(1)}, u32[]{:S(2)}, u32[]{:S(2)}) collective-permute-start(bf16[512,1024]{1,0:T(8,128)(2,1)S(1)} %broadcast_select_fusion.14), channel_id=1, source_target_pairs={{8,0},{10,2},{12,4},{14,6},{16,8},{18,10},{20,12},{22,14},{24,16},... | collective-permute-start | bytes 3145736 | tf_op jit(solution)/shard_map/ppermute | solution.py:10
  221.0 27.5 %collective-permute-start.17 = (bf16[512,1024]{1,0:T(8,128)(2,1)}, bf16[512,1024]{1,0:T(8,128)(2,1)}, u32[]{:S(2)}, u32[]{:S(2)}) collective-permute-start(bf16[512,1024]{1,0:T(8,128)(2,1)} %broadcast_select_fusion.2), channel_id=1, source_target_pairs={{8,0},{10,2},{12,4},{14,6},{16,8},{18,10},{20,12},{22,14},{24,16},... | collective-permute-start | bytes 3145736 | tf_op jit(solution)/shard_map/ppermute | solution.py:10
  225.8 45.2 %collective-permute-start.13 = (bf16[512,1024]{1,0:T(8,128)(2,1)}, bf16[512,1024]{1,0:T(8,128)(2,1)}, u32[]{:S(2)}, u32[]{:S(2)}) collective-permute-start(bf16[512,1024]{1,0:T(8,128)(2,1)} %broadcast_select_fusion.6), channel_id=1, source_target_pairs={{8,0},{10,2},{12,4},{14,6},{16,8},{18,10},{20,12},{22,14},{24,16},... | collective-permute-start | bytes 3145736 | tf_op jit(solution)/shard_map/ppermute | solution.py:10
  227.3 66.1 %collective-permute-start.9 = (bf16[512,1024]{1,0:T(8,128)(2,1)}, bf16[512,1024]{1,0:T(8,128)(2,1)}, u32[]{:S(2)}, u32[]{:S(2)}) collective-permute-start(bf16[512,1024]{1,0:T(8,128)(2,1)} %broadcast_select_fusion.10), channel_id=1, source_target_pairs={{8,0},{10,2},{12,4},{14,6},{16,8},{18,10},{20,12},{22,14},{24,16},... | collective-permute-start | bytes 3145736 | tf_op jit(solution)/shard_map/ppermute | solution.py:10
  228.9 4.3 copy-start.1
  228.9 4.3 copy-start.6
  228.9 87.8 %collective-permute-start.7 = (bf16[512,1024]{1,0:T(8,128)(2,1)}, bf16[512,1024]{1,0:T(8,128)(2,1)}, u32[]{:S(2)}, u32[]{:S(2)}) collective-permute-start(bf16[512,1024]{1,0:T(8,128)(2,1)} %broadcast_select_fusion.11), channel_id=1, source_target_pairs={{24,0},{26,2},{28,4},{30,6},{0,8},{2,10},{4,12},{6,14},{8,16},{10,... | collective-permute-start | bytes 3145736 | tf_op jit(solution)/shard_map/ppermute | solution.py:10
  231.6 1.6 copy-start.5
  231.6 107.6 %collective-permute-start.11 = (bf16[512,1024]{1,0:T(8,128)(2,1)}, bf16[512,1024]{1,0:T(8,128)(2,1)}, u32[]{:S(2)}, u32[]{:S(2)}) collective-permute-start(bf16[512,1024]{1,0:T(8,128)(2,1)} %broadcast_select_fusion.7), channel_id=1, source_target_pairs={{24,0},{26,2},{28,4},{30,6},{0,8},{2,10},{4,12},{6,14},{8,16},{10,... | collective-permute-start | bytes 3145736 | tf_op jit(solution)/shard_map/ppermute | solution.py:10
  248.5 113.2 %collective-permute-start.15 = (bf16[512,1024]{1,0:T(8,128)(2,1)}, bf16[512,1024]{1,0:T(8,128)(2,1)}, u32[]{:S(2)}, u32[]{:S(2)}) collective-permute-start(bf16[512,1024]{1,0:T(8,128)(2,1)} %broadcast_select_fusion.3), channel_id=1, source_target_pairs={{24,0},{26,2},{28,4},{30,6},{0,8},{2,10},{4,12},{6,14},{8,16},{10,... | collective-permute-start | bytes 3145736 | tf_op jit(solution)/shard_map/ppermute | solution.py:10
  270.9 112.7 %collective-permute-start.2 = (bf16[512,1024]{1,0:T(8,128)(2,1)}, bf16[512,1024]{1,0:T(8,128)(2,1)}, u32[]{:S(2)}, u32[]{:S(2)}) collective-permute-start(bf16[512,1024]{1,0:T(8,128)(2,1)} %broadcast_select_fusion.15), channel_id=1, source_target_pairs={{24,0},{26,2},{28,4},{30,6},{0,8},{2,10},{4,12},{6,14},{8,16},{10,... | collective-permute-start | bytes 3145736 | tf_op jit(solution)/shard_map/ppermute | solution.py:10
Sparse Core Ops, SparseCore 0:
  396.3 31.6 reduce-scatter.1
where the time goes:
time: 436 us; the launch traced here: 435 us
  waiting for transfers between devices  304 us (70%)
  matrix products  42.2 us (10%)
  starting transfers between devices  33 us (8%)
  between operations  28.9 us (7%)
  other arithmetic  23.9 us (5%)
    ppermute x18, waiting for transfers between devices, shifted(): return lax.ppermute(block, axis, route)  272 us
    ppermute x18, starting transfers between devices, shifted(): return lax.ppermute(block, axis, route)  33 us
    reduce_scatter x1, waiting for transfers between devices, per_device(): gamma = lax.psum_scatter(total, 'rep', scatter_dimension=1, tiled=True)  31.8 us
    dot_general x4, matrix products, per_device(): own = jnp.dot(amp, other, preferred_element_type=jnp.float32)  22.3 us
    dot_general x4, matrix products, per_device(): lax.dot_general(amp_below, below, (((0,), (0,)), ((), ())), preferred_ele...  19.9 us
    select_n x5, other arithmetic, walk_back(): tile = jnp.where(offset // (1 << level) % 2 == 1, moved, tile)  11.7 us
  transfers between devices with their start and end apart: 19, of which 13 were waited for; matrix products, arithmetic and copies ran while one was open for 12% of the time, Pallas kernels for 0%

commit v1 on v0

v1 whole, which is shorter than its diff:
```python
import functools

import jax
import jax.numpy as jnp
from jax import lax
from jax.experimental import pallas as pl
from jax.experimental.pallas import tpu as pltpu
from jax.sharding import PartitionSpec as P

CHUNK = 256


def exchange(block, axis, mask):
    devices = range(lax.axis_size(axis))
    return lax.ppermute(block, axis, [(i, i ^ mask) for i in devices])


def cut(block, pieces):
    rows = block.shape[0] // pieces
    return [block[i * rows : (i + 1) * rows] for i in range(pieces)]


def absorb_kernel(plan, sizes, place, table, e_occ, e_row, e_part, e_col, *refs):
    lefts_plan, blocks_plan, fresh, final = plan
    occupied, part_rows, width = sizes
    n_left, n_block = len(lefts_plan), len(blocks_plan)
    lefts, refs = refs[:n_left], refs[n_left:]
    blocks, refs = refs[:n_block], refs[n_block:]
    olds = [None] * n_left if fresh else refs[:n_left]
    news = refs[-n_left:]
    here, slot = place[0], place[1]
    entries = table.shape[0]

    rights, slices, rows, tags = [], [], [], []
    for block, (mask, piece) in zip(blocks, blocks_plan):
        rights.append(block[...])
        slices.append(block[:, pl.ds(pl.multiple_of(slot * width, width), width)])
        l = here ^ mask
        tags.append(l)
        if piece is None:
            row = e_row[...]
        else:
            r, p, pieces = piece
            row = e_part[pl.ds((slot ^ r) * pieces + p, 1), :]
        rows.append(row - e_occ[l])
    counts = [right.shape[0] for right in rights]
    right = jnp.concatenate(rights, axis=0) if len(rights) > 1 else rights[0]
    row = jnp.concatenate(rows, axis=1) if len(rows) > 1 else rows[0]

    groups = []
    start = 0
    for i, (mask, _) in enumerate(blocks_plan):
        if groups and groups[-1][0] == mask:
            groups[-1][2] += counts[i]
            groups[-1][3].append(slices[i])
        else:
            groups.append([mask, start, counts[i], [slices[i]]])
        start += counts[i]

    for left, old, new, mask_k in zip(lefts, olds, news, lefts_plan):
        k = here ^ mask_k
        weights = []
        for mask, _, _, _ in groups:
            ahead = (k - (here ^ mask)) & (occupied - 1)
            back = ((here ^ mask) - k) & (occupied - 1)
            total = jnp.int32(0)
            for n in range(entries):
                d = table[n] & (occupied - 1)
                total = total - (d == ahead).astype(jnp.int32) - (d == back).astype(jnp.int32)
            weights.append(total.astype(jnp.float32))
        for at in range(0, left.shape[0], CHUNK):
            pair = lax.dot_general(
                left[at : at + CHUNK], right, (((1,), (1,)), ((), ())),
                preferred_element_type=jnp.float32,
            )
            column = e_col[at : at + CHUNK, :1] - e_occ[k]
            amp = (pair / (column + row)).astype(jnp.bfloat16)
            total = None if old is None else old[at : at + CHUNK]
            for (_, start, count, parts), weight in zip(groups, weights):
                side = jnp.concatenate(parts, axis=0) if len(parts) > 1 else parts[0]
                term = weight * jnp.dot(
                    amp[:, start : start + count], side, preferred_element_type=jnp.float32
                )
                total = term if total is None else total + term
            new[at : at + CHUNK] = total.astype(new.dtype)


def in_vmem(array):
    return pltpu.with_memory_space_constraint(array, pltpu.VMEM)


def absorb(context, sizes, lefts, blocks, olds, final=False):
    plan = (
        tuple(mask for _, mask in lefts),
        tuple((mask, piece) for _, mask, piece in blocks),
        olds is None,
        final,
    )
    rows, width = lefts[0][0].shape[0], sizes[2]
    arrays = [in_vmem(a) for a, _ in lefts] + [in_vmem(b) for b, _, _ in blocks]
    arrays += [] if olds is None else [in_vmem(t) for t in olds]
    kind = jnp.bfloat16 if final else jnp.float32
    scalar = pl.BlockSpec(memory_space=pltpu.SMEM)
    whole = pl.BlockSpec(memory_space=pltpu.VMEM)
    n_in = len(context) + len(arrays)
    aliases = {}
    if olds is not None and not final:
        aliases = {n_in - len(lefts) + i: i for i in range(len(lefts))}
    depth = sum(b.shape[0] for b, _, _ in blocks)
    aux = lefts[0][0].shape[1]
    return pl.pallas_call(
        functools.partial(absorb_kernel, plan, sizes),
        out_shape=[pltpu.VMEM((rows, width), kind) for _ in lefts],
        in_specs=[scalar] * 3 + [whole] * (n_in - 3),
        out_specs=[whole] * len(lefts),
        input_output_aliases=aliases,
        compiler_params=pltpu.CompilerParams(vmem_limit_bytes=24 * 1024 * 1024),
        cost_estimate=pl.CostEstimate(
            flops=2 * len(lefts) * rows * depth * (aux + width),
            bytes_accessed=1024 * 1024,
            transcendentals=0,
        ),
    )(*context, *arrays)


def per_device(integrals, eps_occ, eps_vir, offsets):
    tile = integrals[0]
    virtuals, aux = tile.shape
    occupied = eps_occ.shape[0]
    reps = lax.axis_size("rep")
    lines = lax.axis_size("blk") // 4
    here = lax.axis_index("blk")
    slot = lax.axis_index("rep")
    part = virtuals // reps
    width = aux // reps
    pieces = max(1, 4 // reps)
    rows = part // pieces
    sizes = (occupied, rows, width)

    across = exchange(tile, "blk", 2)
    mine = lax.dynamic_slice_in_dim(tile, slot * part, part, axis=0)
    halves = cut(mine, pieces)
    table = offsets
    bit = 1
    while bit < reps:
        table = jnp.concatenate([table, exchange(table, "rep", bit)])
        bit *= 2

    line = {}
    for m in range(1, lines):
        for p in range(pieces):
            low = m & -m
            source = halves[p] if m == low else line[m ^ low, p]
            line[m, p] = exchange(source, "blk", 4 * low)
    twin = exchange(tile, "blk", 1)

    context = [
        jnp.stack([here, slot]).astype(jnp.int32),
        table,
        eps_occ,
        eps_vir[None, :],
        eps_vir.reshape(virtuals // rows, rows),
        jnp.broadcast_to(eps_vir[:, None], (virtuals, 128)),
    ]
    near, far = (tile, 0), (across, 2)
    first = [(tile, 0, None), (twin, 1, None)]
    (own,) = absorb(context, sizes, [near], first, None)

    steps = []
    for m in range(1, lines):
        for p in range(pieces):
            got = {0: line[m, p]}
            for r in range(1, reps):
                low = r & -r
                got[r] = exchange(got[r ^ low], "rep", low)
            blocks = [(got[r], 4 * m, (r, p, pieces)) for r in range(reps)]
            blocks += [
                (exchange(got[r], "blk", 1), 4 * m + 1, (r, p, pieces)) for r in range(reps)
            ]
            steps.append(blocks)

    (own,) = absorb(context, sizes, [near], steps[0], [own])
    (theirs,) = absorb(context, sizes, [far], first, None)
    (theirs,) = absorb(context, sizes, [far], steps[0], [theirs])
    for blocks in steps[1:-1]:
        own, theirs = absorb(context, sizes, [near, far], blocks, [own, theirs])
    (theirs,) = absorb(context, sizes, [far], steps[-1], [theirs], final=True)
    (own,) = absorb(context, sizes, [near], steps[-1], [own])
    gamma = own + exchange(theirs, "blk", 2).astype(jnp.float32)
    return gamma[None]


def solution(mesh):
    in_specs = (P("blk", None, None), P(), P(), P("rep"))
    out_specs = P("blk", None, "rep")
    return jax.shard_map(
        per_device, mesh=mesh, in_specs=in_specs, out_specs=out_specs, check_vma=False
    )
```

time: 436 us -> 93.2 us (0.21)
  waiting for transfers between devices: 304 us -> 39 us
  matrix products: 42.2 us -> 0 us
  between operations: 28.9 us -> 0.23 us
  Pallas kernels: 0 us -> 26.2 us
  other arithmetic: 23.9 us -> 1.28 us
  starting transfers between devices: 33 us -> 24.3 us
    ppermute x18 -> x28, waiting for transfers between devices: 272 us -> 39 us  [exchange(): return lax.ppermute(block, axis, [(i, i ^ mask) for i in devices])]
    dot_general x8 -> x0, matrix products: 42.2 us -> none  [the longest x4 22.3 us: per_device(): own = jnp.dot(amp, other, preferred_element_type=jnp.float32)]
    reduce_scatter x1 -> x0, waiting for transfers between devices: 31.8 us -> none  [per_device(): gamma = lax.psum_scatter(total, 'rep', scatter_dimension=1, tiled=True)]
    pallas_call x0 -> x10, Pallas kernels: none -> 26.2 us  [absorb(): pl.pallas_call(functools.partial(absorb_kernel, plan, sizes), out_shape=[...]
    select_n x9 -> x0, other arithmetic: 17.3 us -> none  [the longest x5 11.7 us: walk_back(): tile = jnp.where(offset // (1 << level) % 2 == 1, moved, tile)]
    ppermute x18 -> x28, starting transfers between devices: 33 us -> 24.3 us  [exchange(): return lax.ppermute(block, axis, [(i, i ^ mask) for i in devices])]
    add x1 -> x0, other arithmetic: 6.61 us -> none  [per_device(): total = total + own + part]
  transfers between devices with their start and end apart: 19 -> 28, of which waited for: 13 -> 7; matrix products, arithmetic and copies ran while one was open for 12% -> 1% of each run, Pallas kernels for 0% -> 26%
where the time goes in v1:
time: 93.2 us; the launch traced here: 92.9 us
  waiting for transfers between devices  39 us (42%)
  Pallas kernels  26.2 us (28%)
  starting transfers between devices  24.3 us (26%)
  local copies, waits for them, and re-layouts  1.85 us (2%)
  other arithmetic  1.28 us (1%)
    ppermute x28, waiting for transfers between devices, exchange(): return lax.ppermute(block, axis, [(i, i ^ mask) for i in devices])  39 us
    pallas_call x10, Pallas kernels, absorb(): pl.pallas_call(functools.partial(absorb_kernel, plan, sizes), out_shape=[...  26.2 us
    ppermute x28, starting transfers between devices, exchange(): return lax.ppermute(block, axis, [(i, i ^ mask) for i in devices])  24.3 us
  transfers between devices with their start and end apart: 28, of which 7 were waited for; matrix products, arithmetic and copies ran while one was open for 1% of the time, Pallas kernels for 26%

profile of v1, /device:TPU:0, one launch (start us, length us, event | category | flops | bytes accessed | tf_op | source)
XLA Modules:
  0.0 92.9 jit_solution(9357913375035186898)
XLA Ops:
  0.5 1.1 %dynamic-slice_bitcast_fusion = (bf16[128,1024]{1,0:T(8,128)(2,1)S(1)}, bf16[128,1024]{1,0:T(8,128)(2,1)S(1)}) fusion(bf16[1,512,1024]{2,1,0:T(8,128)(2,1)} %param.4, s32[]{:T(128)S(6)} %select_n.3, s32[]{:T(128)S(6)} %add.10), kind=kLoop, calls=%fused_computation.1 | loop fusion | bytes 1048584 | tf_op jit(solution)/shard_map/slice | solution.py:20
  1.5 2.7 %collective-permute-start.22 = (bf16[128,1024]{1,0:T(8,128)(2,1)S(1)}, bf16[128,1024]{1,0:T(8,128)(2,1)S(1)}, u32[]{:S(2)}, u32[]{:S(2)}) collective-permute-start(bf16[128,1024]{1,0:T(8,128)(2,1)S(1)} %get-tuple-element.21), channel_id=1, source_target_pairs={{0,8},{2,10},{4,12},{6,14},{8,0},{10,2},{12,4},{14,6},{16,24},{18,... | collective-permute-start | bytes 786440 | tf_op jit(solution)/shard_map/ppermute | solution.py:15
  4.3 1.5 %collective-permute-start.6 = (bf16[512,1024]{1,0:T(8,128)(2,1)S(1)}, bf16[512,1024]{1,0:T(8,128)(2,1)S(1)}, u32[]{:S(2)}, u32[]{:S(2)}) collective-permute-start(bf16[512,1024]{1,0:T(8,128)(2,1)S(1)} %bitcast.12), channel_id=1, source_target_pairs={{0,4},{2,6},{4,0},{6,2},{8,12},{10,14},{12,8},{14,10},{16,20},{18,... | collective-permute-start | bytes 3145736 | tf_op jit(solution)/shard_map/ppermute | solution.py:15
  6.2 1.5 %collective-permute-start = (s32[4]{0:T(128)S(1)}, s32[4]{0:T(128)S(1)}, u32[]{:S(2)}, u32[]{:S(2)}) collective-permute-start(s32[4]{0:T(128)S(1)} %copy-done.3), channel_id=1, source_target_pairs={{0,1},{1,0},{2,3},{3,2},{4,5},{5,4},{6,7},{7,6},{8,9},{9,8},{10,11... | collective-permute-start | bytes 56 | tf_op jit(solution)/shard_map/ppermute | solution.py:15
  7.7 2.0 %collective-permute-done = s32[4]{0:T(128)S(1)} collective-permute-done((s32[4]{0:T(128)S(1)}, s32[4]{0:T(128)S(1)}, u32[]{:S(2)}, u32[]{:S(2)}) %collective-permute-start) | collective-permute-done | bytes 48 | tf_op jit(solution)/shard_map/ppermute | solution.py:15
  9.8 2.6 %collective-permute-start.7 = (bf16[128,1024]{1,0:T(8,128)(2,1)S(1)}, bf16[128,1024]{1,0:T(8,128)(2,1)S(1)}, u32[]{:S(2)}, u32[]{:S(2)}) collective-permute-start(bf16[128,1024]{1,0:T(8,128)(2,1)S(1)} %get-tuple-element.21), channel_id=1, source_target_pairs={{0,16},{2,18},{4,20},{6,22},{8,24},{10,26},{12,28},{14,30},{16,0},... | collective-permute-start | bytes 786440 | tf_op jit(solution)/shard_map/ppermute | solution.py:15
  12.3 2.0 %collective-permute-start.1 = (bf16[128,1024]{1,0:T(8,128)(2,1)S(1)}, bf16[128,1024]{1,0:T(8,128)(2,1)S(1)}, u32[]{:S(2)}, u32[]{:S(2)}) collective-permute-start(bf16[128,1024]{1,0:T(8,128)(2,1)S(1)} %get-tuple-element.22), channel_id=1, source_target_pairs={{0,16},{2,18},{4,20},{6,22},{8,24},{10,26},{12,28},{14,30},{16,0},... | collective-permute-start | bytes 786440 | tf_op jit(solution)/shard_map/ppermute | solution.py:15
  14.4 9.5 %collective-permute-done.18.refs_2_ = bf16[128,1024]{1,0:T(8,128)(2,1)} collective-permute-done((bf16[128,1024]{1,0:T(8,128)(2,1)S(1)}, bf16[128,1024]{1,0:T(8,128)(2,1)}, u32[]{:S(2)}, u32[]{:S(2)}) %collective-permute-start.18) | collective-permute-done | bytes 262176 | tf_op jit(solution)/shard_map/ppermute | solution.py:15
  23.9 1.7 %collective-permute-start.23 = (bf16[128,1024]{1,0:T(8,128)(2,1)S(1)}, bf16[128,1024]{1,0:T(8,128)(2,1)S(1)}, u32[]{:S(2)}, u32[]{:S(2)}) collective-permute-start(bf16[128,1024]{1,0:T(8,128)(2,1)S(1)} %collective-permute-done.22.refs_1_), channel_id=1, source_target_pairs={{0,1},{1,0},{2,3},{3,2},{4,5},{5,4},{6,7},{7,6},{8,9},{9,8},{10,11... | collective-permute-start | bytes 786440 | tf_op jit(solution)/shard_map/ppermute | solution.py:15
  25.6 5.5 %collective-permute-done.7.refs_2_ = bf16[128,1024]{1,0:T(8,128)(2,1)S(1)} collective-permute-done((bf16[128,1024]{1,0:T(8,128)(2,1)S(1)}, bf16[128,1024]{1,0:T(8,128)(2,1)S(1)}, u32[]{:S(2)}, u32[]{:S(2)}) %collective-permute-start.7) | collective-permute-done | bytes 262176 | tf_op jit(solution)/shard_map/ppermute | solution.py:15
  31.1 3.4 %collective-permute-done.1.refs_2_ = bf16[128,1024]{1,0:T(8,128)(2,1)S(1)} collective-permute-done((bf16[128,1024]{1,0:T(8,128)(2,1)S(1)}, bf16[128,1024]{1,0:T(8,128)(2,1)S(1)}, u32[]{:S(2)}, u32[]{:S(2)}) %collective-permute-start.1) | collective-permute-done | bytes 262176 | tf_op jit(solution)/shard_map/ppermute | solution.py:15
  34.5 1.5 %collective-permute-start.19 = (bf16[128,1024]{1,0:T(8,128)(2,1)}, bf16[128,1024]{1,0:T(8,128)(2,1)}, u32[]{:S(2)}, u32[]{:S(2)}) collective-permute-start(bf16[128,1024]{1,0:T(8,128)(2,1)} %collective-permute-done.18.refs_2_), channel_id=1, source_target_pairs={{0,1},{1,0},{2,3},{3,2},{4,5},{5,4},{6,7},{7,6},{8,9},{9,8},{10,11... | collective-permute-start | bytes 786440 | tf_op jit(solution)/shard_map/ppermute | solution.py:15
  36.6 6.4 %collective-permute-done.19.refs_3_ = bf16[128,1024]{1,0:T(8,128)(2,1)} collective-permute-done((bf16[128,1024]{1,0:T(8,128)(2,1)}, bf16[128,1024]{1,0:T(8,128)(2,1)}, u32[]{:S(2)}, u32[]{:S(2)}) %collective-permute-start.19) | collective-permute-done | bytes 262176 | tf_op jit(solution)/shard_map/ppermute | solution.py:15
  43.1 0.8 collective-permute-start.8
  44.3 0.7 copy-done.2
  45.0 3.1 %shard_map.46.refs_5_ = f32[512,512]{1,0:T(8,128)S(1)} custom-call(s32[2]{0:T(128)S(1)} %pad_add_fusion.place, s32[8]{0:T(128)S(1)} %pad_add_fusion.1.table, f32[16]{0:T(128)S(1)} %copy-done.2, f32[1,512]{1,0:T(1,128)S(1)} %bitcast.22, f32[4,128]{1,0:T(4,128)S(1)} %bitcast.23, f32[512,128]{1,0:T(8,128)S(1)} %broadcast_in_dim.13.e_col, ...), custom_call_target="tpu_custom_call" | custom-call | flops 1610612736 | bytes 1048576 | tf_op jit(solution)/shard_map/pallas_call | solution.py:111
  48.0 2.5 %collective-permute-start.12 = (bf16[128,1024]{1,0:T(8,128)(2,1)S(1)}, bf16[128,1024]{1,0:T(8,128)(2,1)S(1)}, u32[]{:S(2)}, u32[]{:S(2)}) collective-permute-start(bf16[128,1024]{1,0:T(8,128)(2,1)S(1)} %collective-permute-done.1.refs_2_), channel_id=1, source_target_pairs={{0,1},{1,0},{2,3},{3,2},{4,5},{5,4},{6,7},{7,6},{8,9},{9,8},{10,11... | collective-permute-start | bytes 786440 | tf_op jit(solution)/shard_map/ppermute | solution.py:15
  50.5 1.2 %collective-permute-start.2 = (bf16[128,1024]{1,0:T(8,128)(2,1)S(1)}, bf16[128,1024]{1,0:T(8,128)(2,1)S(1)}, u32[]{:S(2)}, u32[]{:S(2)}) collective-permute-start(bf16[128,1024]{1,0:T(8,128)(2,1)S(1)} %collective-permute-done.1.refs_2_), channel_id=1, source_target_pairs={{0,8},{2,10},{4,12},{6,14},{8,0},{10,2},{12,4},{14,6},{16,24},{18,... | collective-permute-start | bytes 786440 | tf_op jit(solution)/shard_map/ppermute | solution.py:15
  51.8 3.1 %shard_map.48.refs_5_ = f32[512,512]{1,0:T(8,128)S(1)} custom-call(s32[2]{0:T(128)S(1)} %pad_add_fusion.place, s32[8]{0:T(128)S(1)} %pad_add_fusion.1.table, f32[16]{0:T(128)S(1)} %copy-done.2, f32[1,512]{1,0:T(1,128)S(1)} %bitcast.24, f32[4,128]{1,0:T(4,128)S(1)} %bitcast.25, f32[512,128]{1,0:T(8,128)S(1)} %broadcast_in_dim.13.e_col, ...), custom_call_target="tpu_custom_call" | custom-call | flops 1610612736 | bytes 1048576 | tf_op jit(solution)/shard_map/pallas_call | solution.py:111
  54.9 0.6 collective-permute-start.17
  55.5 1.8 %shard_map.49.refs_7_ = f32[512,512]{1,0:T(8,128)S(1)} custom-call(s32[2]{0:T(128)S(1)} %pad_add_fusion.place, s32[8]{0:T(128)S(1)} %pad_add_fusion.1.table, f32[16]{0:T(128)S(1)} %copy-done.2, f32[1,512]{1,0:T(1,128)S(1)} %bitcast.26, f32[4,128]{1,0:T(4,128)S(1)} %bitcast.27, ...), custom_call_target="tpu_custom_call", output_to_operand_aliasing={{}: (11, {})} | custom-call | flops 805306368 | bytes 1048576 | tf_op jit(solution)/shard_map/pallas_call | solution.py:111
  57.4 1.8 %shard_map.47.refs_6_ = f32[512,512]{1,0:T(8,128)S(1)} custom-call(s32[2]{0:T(128)S(1)} %pad_add_fusion.place, s32[8]{0:T(128)S(1)} %pad_add_fusion.1.table, f32[16]{0:T(128)S(1)} %copy-done.2, f32[1,512]{1,0:T(1,128)S(1)} %bitcast.28, f32[4,128]{1,0:T(4,128)S(1)} %bitcast.29, ...), custom_call_target="tpu_custom_call", output_to_operand_aliasing={{}: (11, {})} | custom-call | flops 805306368 | bytes 1048576 | tf_op jit(solution)/shard_map/pallas_call | solution.py:111
  59.8 1.9 %collective-permute-start.3 = (bf16[128,1024]{1,0:T(8,128)(2,1)S(1)}, bf16[128,1024]{1,0:T(8,128)(2,1)S(1)}, u32[]{:S(2)}, u32[]{:S(2)}) collective-permute-start(bf16[128,1024]{1,0:T(8,128)(2,1)S(1)} %collective-permute-done.2.refs_1_), channel_id=1, source_target_pairs={{0,1},{1,0},{2,3},{3,2},{4,5},{5,4},{6,7},{7,6},{8,9},{9,8},{10,11... | collective-permute-start | bytes 786440 | tf_op jit(solution)/shard_map/ppermute | solution.py:15
  61.7 3.6 %shard_map.50 = (f32[512,512]{1,0:T(8,128)S(1)}, f32[512,512]{1,0:T(8,128)S(1)}) custom-call(s32[2]{0:T(128)S(1)} %pad_add_fusion.place, s32[8]{0:T(128)S(1)} %pad_add_fusion.1.table, f32[16]{0:T(128)S(1)} %copy-done.2, f32[1,512]{1,0:T(1,128)S(1)} %bitcast.30, f32[4,128]{1,0:T(4,128)S(1)} %bitcast.31, ...), custom_call_target="tpu_custom_call", output_to_operand_aliasing={{0}: (12, {}), {1}: (13, {})} | custom-call | flops 1610612736 | bytes 1048576 | tf_op jit(solution)/shard_map/pallas_call | solution.py:111
  65.9 3.0 %shard_map.51 = (f32[512,512]{1,0:T(8,128)S(1)}, f32[512,512]{1,0:T(8,128)S(1)}) custom-call(s32[2]{0:T(128)S(1)} %pad_add_fusion.place, s32[8]{0:T(128)S(1)} %pad_add_fusion.1.table, f32[16]{0:T(128)S(1)} %copy-done.2, f32[1,512]{1,0:T(1,128)S(1)} %bitcast.32, f32[4,128]{1,0:T(4,128)S(1)} %bitcast.33, ...), custom_call_target="tpu_custom_call", output_to_operand_aliasing={{0}: (12, {}), {1}: (13, {})} | custom-call | flops 1610612736 | bytes 1048576 | tf_op jit(solution)/shard_map/pallas_call | solution.py:111
  69.5 3.2 %shard_map.52 = (f32[512,512]{1,0:T(8,128)S(1)}, f32[512,512]{1,0:T(8,128)S(1)}) custom-call(s32[2]{0:T(128)S(1)} %pad_add_fusion.place, s32[8]{0:T(128)S(1)} %pad_add_fusion.1.table, f32[16]{0:T(128)S(1)} %copy-done.2, f32[1,512]{1,0:T(1,128)S(1)} %bitcast.34, f32[4,128]{1,0:T(4,128)S(1)} %bitcast.35, ...), custom_call_target="tpu_custom_call", output_to_operand_aliasing={{0}: (12, {}), {1}: (13, {})} | custom-call | flops 1610612736 | bytes 1048576 | tf_op jit(solution)/shard_map/pallas_call | solution.py:111
  72.7 3.0 %shard_map.53 = (f32[512,512]{1,0:T(8,128)S(1)}, f32[512,512]{1,0:T(8,128)S(1)}) custom-call(s32[2]{0:T(128)S(1)} %pad_add_fusion.place, s32[8]{0:T(128)S(1)} %pad_add_fusion.1.table, f32[16]{0:T(128)S(1)} %copy-done.2, f32[1,512]{1,0:T(1,128)S(1)} %bitcast.36, f32[4,128]{1,0:T(4,128)S(1)} %bitcast.37, ...), custom_call_target="tpu_custom_call", output_to_operand_aliasing={{0}: (12, {}), {1}: (13, {})} | custom-call | flops 1610612736 | bytes 1048576 | tf_op jit(solution)/shard_map/pallas_call | solution.py:111
  75.8 1.7 %shard_map.55 = bf16[512,512]{1,0:T(8,128)(2,1)S(1)} custom-call(s32[2]{0:T(128)S(1)} %pad_add_fusion.place, s32[8]{0:T(128)S(1)} %pad_add_fusion.1.table, f32[16]{0:T(128)S(1)} %copy-done.2, f32[1,512]{1,0:T(1,128)S(1)} %bitcast.38, f32[4,128]{1,0:T(4,128)S(1)} %bitcast.39, f32[512,128]{1,0:T(8,128)S(1)} %broadcast_in_dim.13.e_col, ...), custom_call_target="tpu_custom_call" | custom-call | flops 805306368 | bytes 1048576 | tf_op jit(solution)/shard_map/pallas_call | solution.py:111
  77.5 0.5 collective-permute-start.27
  78.1 1.8 %shard_map.54 = f32[512,512]{1,0:T(8,128)S(1)} custom-call(s32[2]{0:T(128)S(1)} %pad_add_fusion.place, s32[8]{0:T(128)S(1)} %pad_add_fusion.1.table, f32[16]{0:T(128)S(1)} %copy-done.2, f32[1,512]{1,0:T(1,128)S(1)} %bitcast.40, f32[4,128]{1,0:T(4,128)S(1)} %bitcast.41, f32[512,128]{1,0:T(8,128)S(1)} %broadcast_in_dim.13.e_col, ...), custom_call_target="tpu_custom_call", output_to_operand_aliasing={{}: (11, {})} | custom-call | flops 805306368 | bytes 1048576 | tf_op jit(solution)/shard_map/pallas_call | solution.py:111
  79.9 11.9 %collective-permute-done.27 = bf16[512,512]{1,0:T(8,128)(2,1)S(1)} collective-permute-done((bf16[512,512]{1,0:T(8,128)(2,1)S(1)}, bf16[512,512]{1,0:T(8,128)(2,1)S(1)}, u32[]{:S(2)}, u32[]{:S(2)}) %collective-permute-start.27) | collective-permute-done | bytes 524320 | tf_op jit(solution)/shard_map/ppermute | solution.py:15
  91.8 1.1 %add_bitcast_fusion = f32[1,512,512]{2,1,0:T(8,128)} fusion(f32[512,512]{1,0:T(8,128)S(1)} %shard_map.54, bf16[512,512]{1,0:T(8,128)(2,1)S(1)} %collective-permute-done.27), kind=kLoop, calls=%fused_computation | loop fusion | flops 524288 | bytes 2621440 | tf_op jit(solution)/shard_map/broadcast_in_dim | solution.py:190
  (47 shorter events, 3.8 us)
Async XLA Ops:
  0.0 4.3 %copy-start = (bf16[1,512,1024]{2,1,0:T(8,128)(2,1)S(1)}, bf16[1,512,1024]{2,1,0:T(8,128)(2,1)}, u32[]{:S(2)}) copy-start(bf16[1,512,1024]{2,1,0:T(8,128)(2,1)} %param.4) | copy-start | bytes 3145732
  0.0 43.9 %collective-permute-start.26 = (bf16[512,1024]{1,0:T(8,128)(2,1)}, bf16[512,1024]{1,0:T(8,128)(2,1)}, u32[]{:S(2)}, u32[]{:S(2)}) collective-permute-start(bf16[512,1024]{1,0:T(8,128)(2,1)} %bitcast.11), channel_id=1, source_target_pairs={{0,2},{2,0},{4,6},{6,4},{8,10},{10,8},{12,14},{14,12},{16,18},{18,... | collective-permute-start | bytes 3145736 | tf_op jit(solution)/shard_map/ppermute | solution.py:15
  1.5 4.7 %copy-start.3 = (s32[4]{0:T(128)S(1)}, s32[4]{0:T(128)}, u32[]{:S(2)}) copy-start(s32[4]{0:T(128)} %param.7) | copy-start | bytes 52
  1.5 10.8 %collective-permute-start.22 = (bf16[128,1024]{1,0:T(8,128)(2,1)S(1)}, bf16[128,1024]{1,0:T(8,128)(2,1)S(1)}, u32[]{:S(2)}, u32[]{:S(2)}) collective-permute-start(bf16[128,1024]{1,0:T(8,128)(2,1)S(1)} %get-tuple-element.21), channel_id=1, source_target_pairs={{0,8},{2,10},{4,12},{6,14},{8,0},{10,2},{12,4},{14,6},{16,24},{18,... | collective-permute-start | bytes 786440 | tf_op jit(solution)/shard_map/ppermute | solution.py:15
  4.3 47.5 %collective-permute-start.6 = (bf16[512,1024]{1,0:T(8,128)(2,1)S(1)}, bf16[512,1024]{1,0:T(8,128)(2,1)S(1)}, u32[]{:S(2)}, u32[]{:S(2)}) collective-permute-start(bf16[512,1024]{1,0:T(8,128)(2,1)S(1)} %bitcast.12), channel_id=1, source_target_pairs={{0,4},{2,6},{4,0},{6,2},{8,12},{10,14},{12,8},{14,10},{16,20},{18,... | collective-permute-start | bytes 3145736 | tf_op jit(solution)/shard_map/ppermute | solution.py:15
  5.8 18.2 %collective-permute-start.18 = (bf16[128,1024]{1,0:T(8,128)(2,1)S(1)}, bf16[128,1024]{1,0:T(8,128)(2,1)}, u32[]{:S(2)}, u32[]{:S(2)}) collective-permute-start(bf16[128,1024]{1,0:T(8,128)(2,1)S(1)} %get-tuple-element.22), channel_id=1, source_target_pairs={{0,8},{2,10},{4,12},{6,14},{8,0},{10,2},{12,4},{14,6},{16,24},{18,... | collective-permute-start | bytes 786440 | tf_op jit(solution)/shard_map/ppermute | solution.py:15
  6.2 3.5 %collective-permute-start = (s32[4]{0:T(128)S(1)}, s32[4]{0:T(128)S(1)}, u32[]{:S(2)}, u32[]{:S(2)}) collective-permute-start(s32[4]{0:T(128)S(1)} %copy-done.3), channel_id=1, source_target_pairs={{0,1},{1,0},{2,3},{3,2},{4,5},{5,4},{6,7},{7,6},{8,9},{9,8},{10,11... | collective-permute-start | bytes 56 | tf_op jit(solution)/shard_map/ppermute | solution.py:15
  9.8 21.4 %collective-permute-start.7 = (bf16[128,1024]{1,0:T(8,128)(2,1)S(1)}, bf16[128,1024]{1,0:T(8,128)(2,1)S(1)}, u32[]{:S(2)}, u32[]{:S(2)}) collective-permute-start(bf16[128,1024]{1,0:T(8,128)(2,1)S(1)} %get-tuple-element.21), channel_id=1, source_target_pairs={{0,16},{2,18},{4,20},{6,22},{8,24},{10,26},{12,28},{14,30},{16,0},... | collective-permute-start | bytes 786440 | tf_op jit(solution)/shard_map/ppermute | solution.py:15
  12.3 22.2 %collective-permute-start.1 = (bf16[128,1024]{1,0:T(8,128)(2,1)S(1)}, bf16[128,1024]{1,0:T(8,128)(2,1)S(1)}, u32[]{:S(2)}, u32[]{:S(2)}) collective-permute-start(bf16[128,1024]{1,0:T(8,128)(2,1)S(1)} %get-tuple-element.22), channel_id=1, source_target_pairs={{0,16},{2,18},{4,20},{6,22},{8,24},{10,26},{12,28},{14,30},{16,0},... | collective-permute-start | bytes 786440 | tf_op jit(solution)/shard_map/ppermute | solution.py:15
  23.9 12.1 %collective-permute-start.23 = (bf16[128,1024]{1,0:T(8,128)(2,1)S(1)}, bf16[128,1024]{1,0:T(8,128)(2,1)S(1)}, u32[]{:S(2)}, u32[]{:S(2)}) collective-permute-start(bf16[128,1024]{1,0:T(8,128)(2,1)S(1)} %collective-permute-done.22.refs_1_), channel_id=1, source_target_pairs={{0,1},{1,0},{2,3},{3,2},{4,5},{5,4},{6,7},{7,6},{8,9},{9,8},{10,11... | collective-permute-start | bytes 786440 | tf_op jit(solution)/shard_map/ppermute | solution.py:15
  31.1 5.0 %collective-permute-start.24 = (bf16[128,1024]{1,0:T(8,128)(2,1)S(1)}, bf16[128,1024]{1,0:T(8,128)(2,1)S(1)}, u32[]{:S(2)}, u32[]{:S(2)}) collective-permute-start(bf16[128,1024]{1,0:T(8,128)(2,1)S(1)} %collective-permute-done.22.refs_1_), channel_id=1, source_target_pairs={{0,2},{2,0},{4,6},{6,4},{8,10},{10,8},{12,14},{14,12},{16,18},{18,... | collective-permute-start | bytes 786440 | tf_op jit(solution)/shard_map/ppermute | solution.py:15
  34.5 8.6 %collective-permute-start.19 = (bf16[128,1024]{1,0:T(8,128)(2,1)}, bf16[128,1024]{1,0:T(8,128)(2,1)}, u32[]{:S(2)}, u32[]{:S(2)}) collective-permute-start(bf16[128,1024]{1,0:T(8,128)(2,1)} %collective-permute-done.18.refs_2_), channel_id=1, source_target_pairs={{0,1},{1,0},{2,3},{3,2},{4,5},{5,4},{6,7},{7,6},{8,9},{9,8},{10,11... | collective-permute-start | bytes 786440 | tf_op jit(solution)/shard_map/ppermute | solution.py:15
  36.0 7.1 %collective-permute-start.20 = (bf16[128,1024]{1,0:T(8,128)(2,1)}, bf16[128,1024]{1,0:T(8,128)(2,1)}, u32[]{:S(2)}, u32[]{:S(2)}) collective-permute-start(bf16[128,1024]{1,0:T(8,128)(2,1)} %collective-permute-done.18.refs_2_), channel_id=1, source_target_pairs={{0,2},{2,0},{4,6},{6,4},{8,10},{10,8},{12,14},{14,12},{16,18},{18,... | collective-permute-start | bytes 786440 | tf_op jit(solution)/shard_map/ppermute | solution.py:15
  36.0 8.1 %copy-start.1 = (f32[512]{0:T(512)S(1)}, f32[512]{0:T(512)}, u32[]{:S(2)}) copy-start(f32[512]{0:T(512)} %param.6) | copy-start | bytes 6148
  36.1 11.9 %collective-permute-start.15 = (bf16[128,1024]{1,0:T(8,128)(2,1)S(1)}, bf16[128,1024]{1,0:T(8,128)(2,1)S(1)}, u32[]{:S(2)}, u32[]{:S(2)}) collective-permute-start(bf16[128,1024]{1,0:T(8,128)(2,1)S(1)} %collective-permute-done.7.refs_2_), channel_id=1, source_target_pairs={{0,1},{1,0},{2,3},{3,2},{4,5},{5,4},{6,7},{7,6},{8,9},{9,8},{10,11... | collective-permute-start | bytes 786440 | tf_op jit(solution)/shard_map/ppermute | solution.py:15
  43.1 7.4 %collective-permute-start.16 = (bf16[128,1024]{1,0:T(8,128)(2,1)S(1)}, bf16[128,1024]{1,0:T(8,128)(2,1)S(1)}, u32[]{:S(2)}, u32[]{:S(2)}) collective-permute-start(bf16[128,1024]{1,0:T(8,128)(2,1)S(1)} %collective-permute-done.7.refs_2_), channel_id=1, source_target_pairs={{0,2},{2,0},{4,6},{6,4},{8,10},{10,8},{12,14},{14,12},{16,18},{18,... | collective-permute-start | bytes 786440 | tf_op jit(solution)/shard_map/ppermute | solution.py:15
  43.1 11.7 %collective-permute-start.8 = (bf16[128,1024]{1,0:T(8,128)(2,1)S(1)}, bf16[128,1024]{1,0:T(8,128)(2,1)S(1)}, u32[]{:S(2)}, u32[]{:S(2)}) collective-permute-start(bf16[128,1024]{1,0:T(8,128)(2,1)S(1)} %collective-permute-done.7.refs_2_), channel_id=1, source_target_pairs={{0,8},{2,10},{4,12},{6,14},{8,0},{10,2},{12,4},{14,6},{16,24},{18,... | collective-permute-start | bytes 786440 | tf_op jit(solution)/shard_map/ppermute | solution.py:15
  43.9 11.5 %collective-permute-start.25 = (bf16[128,1024]{1,0:T(8,128)(2,1)S(1)}, bf16[128,1024]{1,0:T(8,128)(2,1)S(1)}, u32[]{:S(2)}, u32[]{:S(2)}) collective-permute-start(bf16[128,1024]{1,0:T(8,128)(2,1)S(1)} %collective-permute-done.23.refs_2_), channel_id=1, source_target_pairs={{0,2},{2,0},{4,6},{6,4},{8,10},{10,8},{12,14},{14,12},{16,18},{18,... | collective-permute-start | bytes 786440 | tf_op jit(solution)/shard_map/ppermute | solution.py:15
  44.3 0.7 copy-start.2
  48.0 11.1 %collective-permute-start.12 = (bf16[128,1024]{1,0:T(8,128)(2,1)S(1)}, bf16[128,1024]{1,0:T(8,128)(2,1)S(1)}, u32[]{:S(2)}, u32[]{:S(2)}) collective-permute-start(bf16[128,1024]{1,0:T(8,128)(2,1)S(1)} %collective-permute-done.1.refs_2_), channel_id=1, source_target_pairs={{0,1},{1,0},{2,3},{3,2},{4,5},{5,4},{6,7},{7,6},{8,9},{9,8},{10,11... | collective-permute-start | bytes 786440 | tf_op jit(solution)/shard_map/ppermute | solution.py:15
  50.5 8.8 %collective-permute-start.2 = (bf16[128,1024]{1,0:T(8,128)(2,1)S(1)}, bf16[128,1024]{1,0:T(8,128)(2,1)S(1)}, u32[]{:S(2)}, u32[]{:S(2)}) collective-permute-start(bf16[128,1024]{1,0:T(8,128)(2,1)S(1)} %collective-permute-done.1.refs_2_), channel_id=1, source_target_pairs={{0,8},{2,10},{4,12},{6,14},{8,0},{10,2},{12,4},{14,6},{16,24},{18,... | collective-permute-start | bytes 786440 | tf_op jit(solution)/shard_map/ppermute | solution.py:15
  51.8 8.0 %collective-permute-start.21 = (bf16[128,1024]{1,0:T(8,128)(2,1)}, bf16[128,1024]{1,0:T(8,128)(2,1)S(1)}, u32[]{:S(2)}, u32[]{:S(2)}) collective-permute-start(bf16[128,1024]{1,0:T(8,128)(2,1)} %collective-permute-done.19.refs_3_), channel_id=1, source_target_pairs={{0,2},{2,0},{4,6},{6,4},{8,10},{10,8},{12,14},{14,12},{16,18},{18,... | collective-permute-start | bytes 786440 | tf_op jit(solution)/shard_map/ppermute | solution.py:15
  54.9 10.4 %collective-permute-start.17 = (bf16[128,1024]{1,0:T(8,128)(2,1)S(1)}, bf16[128,1024]{1,0:T(8,128)(2,1)S(1)}, u32[]{:S(2)}, u32[]{:S(2)}) collective-permute-start(bf16[128,1024]{1,0:T(8,128)(2,1)S(1)} %collective-permute-done.15.refs_3_), channel_id=1, source_target_pairs={{0,2},{2,0},{4,6},{6,4},{8,10},{10,8},{12,14},{14,12},{16,18},{18,... | collective-permute-start | bytes 786440 | tf_op jit(solution)/shard_map/ppermute | solution.py:15
  55.4 10.0 %collective-permute-start.9 = (bf16[128,1024]{1,0:T(8,128)(2,1)S(1)}, bf16[128,1024]{1,0:T(8,128)(2,1)S(1)}, u32[]{:S(2)}, u32[]{:S(2)}) collective-permute-start(bf16[128,1024]{1,0:T(8,128)(2,1)S(1)} %collective-permute-done.8.refs_2_), channel_id=1, source_target_pairs={{0,1},{1,0},{2,3},{3,2},{4,5},{5,4},{6,7},{7,6},{8,9},{9,8},{10,11... | collective-permute-start | bytes 786440 | tf_op jit(solution)/shard_map/ppermute | solution.py:15
  59.2 9.7 %collective-permute-start.13 = (bf16[128,1024]{1,0:T(8,128)(2,1)S(1)}, bf16[128,1024]{1,0:T(8,128)(2,1)S(1)}, u32[]{:S(2)}, u32[]{:S(2)}) collective-permute-start(bf16[128,1024]{1,0:T(8,128)(2,1)S(1)} %collective-permute-done.1.refs_2_), channel_id=1, source_target_pairs={{0,2},{2,0},{4,6},{6,4},{8,10},{10,8},{12,14},{14,12},{16,18},{18,... | collective-permute-start | bytes 786440 | tf_op jit(solution)/shard_map/ppermute | solution.py:15
  59.3 10.2 %collective-permute-start.14 = (bf16[128,1024]{1,0:T(8,128)(2,1)S(1)}, bf16[128,1024]{1,0:T(8,128)(2,1)S(1)}, u32[]{:S(2)}, u32[]{:S(2)}) collective-permute-start(bf16[128,1024]{1,0:T(8,128)(2,1)S(1)} %collective-permute-done.12.refs_3_), channel_id=1, source_target_pairs={{0,2},{2,0},{4,6},{6,4},{8,10},{10,8},{12,14},{14,12},{16,18},{18,... | collective-permute-start | bytes 786440 | tf_op jit(solution)/shard_map/ppermute | solution.py:15
  59.8 9.6 %collective-permute-start.3 = (bf16[128,1024]{1,0:T(8,128)(2,1)S(1)}, bf16[128,1024]{1,0:T(8,128)(2,1)S(1)}, u32[]{:S(2)}, u32[]{:S(2)}) collective-permute-start(bf16[128,1024]{1,0:T(8,128)(2,1)S(1)} %collective-permute-done.2.refs_1_), channel_id=1, source_target_pairs={{0,1},{1,0},{2,3},{3,2},{4,5},{5,4},{6,7},{7,6},{8,9},{9,8},{10,11... | collective-permute-start | bytes 786440 | tf_op jit(solution)/shard_map/ppermute | solution.py:15
  65.3 7.4 %collective-permute-start.10 = (bf16[128,1024]{1,0:T(8,128)(2,1)S(1)}, bf16[128,1024]{1,0:T(8,128)(2,1)S(1)}, u32[]{:S(2)}, u32[]{:S(2)}) collective-permute-start(bf16[128,1024]{1,0:T(8,128)(2,1)S(1)} %collective-permute-done.8.refs_2_), channel_id=1, source_target_pairs={{0,2},{2,0},{4,6},{6,4},{8,10},{10,8},{12,14},{14,12},{16,18},{18,... | collective-permute-start | bytes 786440 | tf_op jit(solution)/shard_map/ppermute | solution.py:15
  65.4 7.3 %collective-permute-start.11 = (bf16[128,1024]{1,0:T(8,128)(2,1)S(1)}, bf16[128,1024]{1,0:T(8,128)(2,1)S(1)}, u32[]{:S(2)}, u32[]{:S(2)}) collective-permute-start(bf16[128,1024]{1,0:T(8,128)(2,1)S(1)} %collective-permute-done.9.refs_3_), channel_id=1, source_target_pairs={{0,2},{2,0},{4,6},{6,4},{8,10},{10,8},{12,14},{14,12},{16,18},{18,... | collective-permute-start | bytes 786440 | tf_op jit(solution)/shard_map/ppermute | solution.py:15
  68.9 6.9 %collective-permute-start.4 = (bf16[128,1024]{1,0:T(8,128)(2,1)S(1)}, bf16[128,1024]{1,0:T(8,128)(2,1)S(1)}, u32[]{:S(2)}, u32[]{:S(2)}) collective-permute-start(bf16[128,1024]{1,0:T(8,128)(2,1)S(1)} %collective-permute-done.2.refs_1_), channel_id=1, source_target_pairs={{0,2},{2,0},{4,6},{6,4},{8,10},{10,8},{12,14},{14,12},{16,18},{18,... | collective-permute-start | bytes 786440 | tf_op jit(solution)/shard_map/ppermute | solution.py:15
  69.3 6.5 %collective-permute-start.5 = (bf16[128,1024]{1,0:T(8,128)(2,1)S(1)}, bf16[128,1024]{1,0:T(8,128)(2,1)S(1)}, u32[]{:S(2)}, u32[]{:S(2)}) collective-permute-start(bf16[128,1024]{1,0:T(8,128)(2,1)S(1)} %collective-permute-done.3.refs_2_), channel_id=1, source_target_pairs={{0,2},{2,0},{4,6},{6,4},{8,10},{10,8},{12,14},{14,12},{16,18},{18,... | collective-permute-start | bytes 786440 | tf_op jit(solution)/shard_map/ppermute | solution.py:15
  77.5 14.2 %collective-permute-start.27 = (bf16[512,512]{1,0:T(8,128)(2,1)S(1)}, bf16[512,512]{1,0:T(8,128)(2,1)S(1)}, u32[]{:S(2)}, u32[]{:S(2)}) collective-permute-start(bf16[512,512]{1,0:T(8,128)(2,1)S(1)} %shard_map.55), channel_id=1, source_target_pairs={{0,4},{2,6},{4,0},{6,2},{8,12},{10,14},{12,8},{14,10},{16,20},{18,... | collective-permute-start | bytes 1572872 | tf_op jit(solution)/shard_map/ppermute | solution.py:15

commit v2 on v0

v2 whole, which is shorter than its diff:
```python
import functools

import jax
import jax.numpy as jnp
from jax import lax
from jax.experimental import pallas as pl
from jax.experimental.pallas import tpu as pltpu
from jax.sharding import PartitionSpec as P

CHUNK = 256
MIB = 1024 * 1024


def exchange(block, axis, mask):
    devices = range(lax.axis_size(axis))
    return lax.ppermute(block, axis, [(i, i ^ mask) for i in devices])


def gate(blocks, after):
    anywhere = pl.BlockSpec(memory_space=pl.ANY)
    return pl.pallas_call(
        lambda *refs: None,
        out_shape=[jax.ShapeDtypeStruct(b.shape, b.dtype) for b in blocks],
        in_specs=[anywhere] * (len(blocks) + len(after)),
        out_specs=[anywhere] * len(blocks),
        input_output_aliases={i: i for i in range(len(blocks))},
        compiler_params=pltpu.CompilerParams(vmem_limit_bytes=MIB),
        cost_estimate=pl.CostEstimate(flops=0, bytes_accessed=0, transcendentals=0),
    )(*blocks, *after)


def absorb_kernel(plan, sizes, place, table, e_occ, e_half, e_col, *refs):
    left_masks, block_plan, fresh = plan
    occupied, width, parts = sizes
    n_left, n_block = len(left_masks), len(block_plan)
    n_total = n_left * parts
    lefts, refs = refs[:n_left], refs[n_left:]
    blocks, refs = refs[:n_block], refs[n_block:]
    olds = None if fresh else refs[:n_total]
    news = refs[-n_total:]
    here, slot = place[0], place[1]

    for i, (left, mask_k) in enumerate(zip(lefts, left_masks)):
        k = here ^ mask_k

        def weight(l):
            ahead = (k - l) & (occupied - 1)
            back = (l - k) & (occupied - 1)
            total = jnp.int32(0)
            for n in range(table.shape[0]):
                d = table[n] & (occupied - 1)
                total = total - (d == ahead).astype(jnp.int32) - (d == back).astype(jnp.int32)
            return total.astype(jnp.float32)

        for at in range(0, left.shape[0], CHUNK):
            column = e_col[at : at + CHUNK, :1] - e_occ[k]
            amps = []
            for block, runs in zip(blocks, block_plan):
                pair = lax.dot_general(
                    left[at : at + CHUNK], block[...], (((1,), (1,)), ((), ())),
                    preferred_element_type=jnp.float32,
                )
                rows = []
                for mask, first, count in runs:
                    pieces = [e_half[pl.ds(slot * 2 + first + j, 1), :] for j in range(count)]
                    rows += [piece - e_occ[here ^ mask] for piece in pieces]
                row = jnp.concatenate(rows, axis=1) if len(rows) > 1 else rows[0]
                amps.append((pair / (column + row)).astype(jnp.bfloat16))
            for q in range(parts):
                lanes = pl.ds(pl.multiple_of((slot ^ q) * width, width), width)
                total = None if fresh else olds[i * parts + q][at : at + CHUNK]
                for amp, block, runs in zip(amps, blocks, block_plan):
                    start = 0
                    for mask, _, count in runs:
                        stop = start + count * e_half.shape[1]
                        term = weight(here ^ mask) * jnp.dot(
                            amp[:, start:stop], block[start:stop, lanes],
                            preferred_element_type=jnp.float32,
                        )
                        total = term if total is None else total + term
                        start = stop
                new = news[i * parts + q]
                new[at : at + CHUNK] = total.astype(new.dtype)


def in_vmem(array):
    return pltpu.with_memory_space_constraint(array, pltpu.VMEM)


def absorb(context, sizes, lefts, blocks, olds, kinds=None):
    virtuals, aux = lefts[0][0].shape
    _, width, parts = sizes
    plan = (
        tuple(mask for _, mask in lefts),
        tuple(tuple(runs) for _, runs in blocks),
        olds is None,
    )
    n_total = len(lefts) * parts
    kinds = kinds or [jnp.float32] * n_total
    arrays = [in_vmem(a) for a, _ in lefts] + [in_vmem(b) for b, _ in blocks]
    arrays += [] if olds is None else [in_vmem(t) for t in olds]
    scalar = pl.BlockSpec(memory_space=pltpu.SMEM)
    whole = pl.BlockSpec(memory_space=pltpu.VMEM)
    n_in = len(context) + len(arrays)
    aliases = {}
    if olds is not None:
        base = n_in - n_total
        aliases = {base + i: i for i in range(n_total) if kinds[i] == jnp.float32}
    depth = sum(b.shape[0] for b, _ in blocks)
    return pl.pallas_call(
        functools.partial(absorb_kernel, plan, sizes),
        out_shape=[pltpu.VMEM((virtuals, width), kind) for kind in kinds],
        in_specs=[scalar] * 3 + [whole] * (n_in - 3),
        out_specs=[whole] * n_total,
        input_output_aliases=aliases,
        compiler_params=pltpu.CompilerParams(vmem_limit_bytes=24 * MIB),
        cost_estimate=pl.CostEstimate(
            flops=4 * len(lefts) * virtuals * depth * aux, bytes_accessed=0, transcendentals=0
        ),
    )(*context, *arrays)


def per_device(integrals, eps_occ, eps_vir, offsets):
    tile = integrals[0]
    virtuals, aux = tile.shape
    occupied = eps_occ.shape[0]
    reps = lax.axis_size("rep")
    lines = lax.axis_size("blk") // 4
    here = lax.axis_index("blk")
    slot = lax.axis_index("rep")
    part = virtuals // reps
    half = part // 2
    width = aux // reps
    sizes = (occupied, width, reps)

    mine = lax.dynamic_slice_in_dim(tile, slot * part, part, axis=0)
    line = {(0, 0): mine[:half], (0, 1): mine[half:]}
    beside = exchange(mine, "blk", 2)
    table = offsets
    bit = 1
    while bit < reps:
        table = jnp.concatenate([table, exchange(table, "rep", bit)])
        bit *= 2
    twin = exchange(tile, "blk", 1)
    lefts = [(tile, 0), (twin, 1)]
    context = [
        jnp.stack([here, slot]).astype(jnp.int32),
        table,
        eps_occ,
        eps_vir.reshape(virtuals // half, half),
        jnp.broadcast_to(eps_vir[:, None], (virtuals, 128)),
    ]
    totals = absorb(context, sizes, lefts, [(mine, [(0, 0, 2)])], None)

    steps = []
    for level in range(1, lines.bit_length()):
        members = [m for m in range(1, lines) if m.bit_count() == level]
        steps += [(members, h) for h in range(2)]
    sides = [(beside, [(2, 0, 2)]), None]
    for members, h in steps:
        for m in members:
            low = m & -m
            line[m, h] = exchange(line[m ^ low, h], "blk", 4 * low)
        blocks = gate([line[m, h] for m in members], [totals[0]])
        for m, block in zip(members, blocks):
            line[m, h] = block
        group = jnp.concatenate(blocks, axis=0) if len(blocks) > 1 else blocks[0]
        sides.append((exchange(group, "blk", 2), [(4 * m + 2, h, 1) for m in members]))
        arrived = sides.pop(0)
        blocks = [] if arrived is None else [arrived]
        blocks.append((group, [(4 * m, h, 1) for m in members]))
        totals = absorb(context, sizes, lefts, blocks, totals)
    for arrived in sides[:-1]:
        totals = absorb(context, sizes, lefts, [arrived], totals)
    last = [sides[-1]]
    kinds = [jnp.float32] + [jnp.bfloat16] * (reps - 1)
    theirs = absorb(context, sizes, lefts[1:], last, totals[reps:], kinds)
    ours = absorb(context, sizes, lefts[:1], last, totals[:reps])
    gamma = ours[0] + exchange(theirs[0], "blk", 1)
    for q in range(1, reps):
        sent = ours[q] + exchange(theirs[q], "blk", 1).astype(jnp.float32)
        gamma = gamma + exchange(sent.astype(jnp.bfloat16), "rep", q).astype(jnp.float32)
    return gamma[None]


def solution(mesh):
    in_specs = (P("blk", None, None), P(), P(), P("rep"))
    out_specs = P("blk", None, "rep")
    return jax.shard_map(
        per_device, mesh=mesh, in_specs=in_specs, out_specs=out_specs, check_vma=False
    )
```

time: 436 us -> 76.2 us (0.17)
  waiting for transfers between devices: 304 us -> 28 us
  matrix products: 42.2 us -> 0 us
  between operations: 28.9 us -> 0.16 us
  Pallas kernels: 0 us -> 25.9 us
  other arithmetic: 23.9 us -> 1.55 us
  starting transfers between devices: 33 us -> 17.8 us
    ppermute x18 -> x16, waiting for transfers between devices: 272 us -> 28 us  [exchange(): return lax.ppermute(block, axis, [(i, i ^ mask) for i in devices])]
    dot_general x8 -> x0, matrix products: 42.2 us -> none  [the longest x4 22.3 us: per_device(): own = jnp.dot(amp, other, preferred_element_type=jnp.float32)]
    reduce_scatter x1 -> x0, waiting for transfers between devices: 31.8 us -> none  [per_device(): gamma = lax.psum_scatter(total, 'rep', scatter_dimension=1, tiled=True)]
    pallas_call x0 -> x12, Pallas kernels: none -> 25.9 us  [the longest x8 25.9 us: absorb(): pl.pallas_call(functools.partial(absorb_kernel, plan, sizes), out_shape=[...]
    select_n x9 -> x0, other arithmetic: 17.3 us -> none  [the longest x5 11.7 us: walk_back(): tile = jnp.where(offset // (1 << level) % 2 == 1, moved, tile)]
    ppermute x18 -> x16, starting transfers between devices: 33 us -> 17.8 us  [exchange(): return lax.ppermute(block, axis, [(i, i ^ mask) for i in devices])]
    add x1 -> x0, other arithmetic: 6.61 us -> none  [per_device(): total = total + own + part]
  transfers between devices with their start and end apart: 19 -> 16, of which waited for: 13 -> 11; matrix products, arithmetic and copies ran while one was open for 12% -> 3% of each run, Pallas kernels for 0% -> 31%
where the time goes in v2:
time: 76.2 us; the launch traced here: 76.1 us
  waiting for transfers between devices  28 us (37%)
  Pallas kernels  25.9 us (34%)
  starting transfers between devices  17.8 us (23%)
  local copies, waits for them, and re-layouts  2.66 us (3%)
  other arithmetic  1.55 us (2%)
    ppermute x16, waiting for transfers between devices, exchange(): return lax.ppermute(block, axis, [(i, i ^ mask) for i in devices])  28 us
    pallas_call x8, Pallas kernels, absorb(): pl.pallas_call(functools.partial(absorb_kernel, plan, sizes), out_shape=[...  25.9 us
    ppermute x16, starting transfers between devices, exchange(): return lax.ppermute(block, axis, [(i, i ^ mask) for i in devices])  17.8 us
    slice x1, local copies, waits for them, and re-layouts, per_device(): line = {(0, 0): mine[:half], (0, 1): mine[half:]}  1.76 us
  transfers between devices with their start and end apart: 16, of which 11 were waited for; matrix products, arithmetic and copies ran while one was open for 3% of the time, Pallas kernels for 31%

profile of v2, /device:TPU:0, one launch (start us, length us, event | category | flops | bytes accessed | tf_op | source)
XLA Modules:
  0.0 76.1 jit_solution(4214542224339967474)
XLA Ops:
  0.0 0.5 collective-permute-start.3
  0.5 1.8 %dynamic-slice_bitcast_fusion.1 = (bf16[128,1024]{1,0:T(8,128)(2,1)}, bf16[128,1024]{1,0:T(8,128)(2,1)S(1)}) fusion(bf16[1,512,1024]{2,1,0:T(8,128)(2,1)} %param.4, s32[]{:T(128)S(6)} %select_n.3, s32[]{:T(128)S(6)} %add.18), kind=kLoop, calls=%fused_computation.3 | loop fusion | bytes 1048584 | tf_op jit(solution)/shard_map/slice | solution.py:137
  2.2 2.7 %collective-permute-start.5 = (bf16[128,1024]{1,0:T(8,128)(2,1)}, bf16[128,1024]{1,0:T(8,128)(2,1)S(1)}, u32[]{:S(2)}, u32[]{:S(2)}) collective-permute-start(bf16[128,1024]{1,0:T(8,128)(2,1)} %get-tuple-element.69), channel_id=1, source_target_pairs={{0,8},{2,10},{4,12},{6,14},{8,0},{10,2},{12,4},{14,6},{16,24},{18,... | collective-permute-start | bytes 786440 | tf_op jit(solution)/shard_map/ppermute | solution.py:16
  4.9 2.6 %collective-permute-start.6 = (bf16[128,1024]{1,0:T(8,128)(2,1)}, bf16[128,1024]{1,0:T(8,128)(2,1)S(1)}, u32[]{:S(2)}, u32[]{:S(2)}) collective-permute-start(bf16[128,1024]{1,0:T(8,128)(2,1)} %get-tuple-element.69), channel_id=1, source_target_pairs={{0,16},{2,18},{4,20},{6,22},{8,24},{10,26},{12,28},{14,30},{16,0},... | collective-permute-start | bytes 786440 | tf_op jit(solution)/shard_map/ppermute | solution.py:16
  7.5 1.5 %collective-permute-start = (s32[4]{0:T(128)S(1)}, s32[4]{0:T(128)S(1)}, u32[]{:S(2)}, u32[]{:S(2)}) collective-permute-start(s32[4]{0:T(128)S(1)} %copy-done.3), channel_id=1, source_target_pairs={{0,1},{1,0},{2,3},{3,2},{4,5},{5,4},{6,7},{7,6},{8,9},{9,8},{10,11... | collective-permute-start | bytes 56 | tf_op jit(solution)/shard_map/ppermute | solution.py:16
  9.0 1.6 %collective-permute-start.4 = (bf16[256,1024]{1,0:T(8,128)(2,1)S(1)}, bf16[256,1024]{1,0:T(8,128)(2,1)}, u32[]{:S(2)}, u32[]{:S(2)}) collective-permute-start(bf16[256,1024]{1,0:T(8,128)(2,1)S(1)} %dynamic-slice_bitcast_fusion.refs_2_), channel_id=1, source_target_pairs={{0,4},{2,6},{4,0},{6,2},{8,12},{10,14},{12,8},{14,10},{16,20},{18,... | collective-permute-start | bytes 1572872 | tf_op jit(solution)/shard_map/ppermute | solution.py:16
  11.0 0.4 collective-permute-start.1
  11.9 0.7 copy-done.2
  12.5 2.5 %shard_map.46 = (f32[512,512]{1,0:T(8,128)S(1)}, f32[512,512]{1,0:T(8,128)S(1)}, f32[512,512]{1,0:T(8,128)S(1)}, f32[512,512]{1,0:T(8,128)S(1)}) custom-call(s32[2]{0:T(128)S(1)} %pad_add_fusion.place, s32[8]{0:T(128)S(1)} %pad_add_fusion.1.table, f32[16]{0:T(128)S(1)} %copy-done.2, f32[4,128]{1,0:T(4,128)S(1)} %bitcast.20, ...), custom_call_target="tpu_custom_call" | custom-call | flops 1073741824 | tf_op jit(solution)/shard_map/pallas_call | solution.py:110
  15.0 2.7 %collective-permute-done.5.refs_0_ = bf16[128,1024]{1,0:T(8,128)(2,1)S(1)} collective-permute-done((bf16[128,1024]{1,0:T(8,128)(2,1)}, bf16[128,1024]{1,0:T(8,128)(2,1)S(1)}, u32[]{:S(2)}, u32[]{:S(2)}) %collective-permute-start.5) | collective-permute-done | bytes 262176 | tf_op jit(solution)/shard_map/ppermute | solution.py:16
  17.7 3.0 %collective-permute-done.6.refs_1_ = bf16[128,1024]{1,0:T(8,128)(2,1)S(1)} collective-permute-done((bf16[128,1024]{1,0:T(8,128)(2,1)}, bf16[128,1024]{1,0:T(8,128)(2,1)S(1)}, u32[]{:S(2)}, u32[]{:S(2)}) %collective-permute-start.6) | collective-permute-done | bytes 262176 | tf_op jit(solution)/shard_map/ppermute | solution.py:16
  20.8 1.6 %collective-permute-start.8 = (bf16[256,1024]{1,0:T(8,128)(2,1)S(1)}, bf16[256,1024]{1,0:T(8,128)(2,1)S(1)}, u32[]{:S(2)}, u32[]{:S(2)}) collective-permute-start(bf16[256,1024]{1,0:T(8,128)(2,1)S(1)} %constant_dynamic-update-slice_fusion.refs_3_), channel_id=1, source_target_pairs={{0,4},{2,6},{4,0},{6,2},{8,12},{10,14},{12,8},{14,10},{16,20},{18,... | collective-permute-start | bytes 1572872 | tf_op jit(solution)/shard_map/ppermute | solution.py:16
  22.4 1.7 %collective-permute-done.4.refs_2_ = bf16[256,1024]{1,0:T(8,128)(2,1)} collective-permute-done((bf16[256,1024]{1,0:T(8,128)(2,1)S(1)}, bf16[256,1024]{1,0:T(8,128)(2,1)}, u32[]{:S(2)}, u32[]{:S(2)}) %collective-permute-start.4) | collective-permute-done | bytes 524320 | tf_op jit(solution)/shard_map/ppermute | solution.py:16
  24.1 4.4 %shard_map.48 = (f32[512,512]{1,0:T(8,128)S(1)}, f32[512,512]{1,0:T(8,128)S(1)}, f32[512,512]{1,0:T(8,128)S(1)}, f32[512,512]{1,0:T(8,128)S(1)}) custom-call(s32[2]{0:T(128)S(1)} %pad_add_fusion.place, s32[8]{0:T(128)S(1)} %pad_add_fusion.1.table, f32[16]{0:T(128)S(1)} %copy-done.2, ...), custom_call_target="tpu_custom_call", output_to_operand_aliasing={{0}: (9, {}), {1}: (10, {}), {2}: (11, {}), {3}: (12, {})} | custom-call | flops 2147483648 | tf_op jit(solution)/shard_map/pallas_call | solution.py:110
  28.7 2.6 %collective-permute-done.2.refs_1_ = bf16[128,1024]{1,0:T(8,128)(2,1)S(1)} collective-permute-done((bf16[128,1024]{1,0:T(8,128)(2,1)S(1)}, bf16[128,1024]{1,0:T(8,128)(2,1)S(1)}, u32[]{:S(2)}, u32[]{:S(2)}) %collective-permute-start.2) | collective-permute-done | bytes 262176 | tf_op jit(solution)/shard_map/ppermute | solution.py:16
  31.4 1.6 %collective-permute-start.12 = (bf16[256,1024]{1,0:T(8,128)(2,1)S(1)}, bf16[256,1024]{1,0:T(8,128)(2,1)S(1)}, u32[]{:S(2)}, u32[]{:S(2)}) collective-permute-start(bf16[256,1024]{1,0:T(8,128)(2,1)S(1)} %constant_dynamic-update-slice_fusion.2.refs_2_), channel_id=1, source_target_pairs={{0,4},{2,6},{4,0},{6,2},{8,12},{10,14},{12,8},{14,10},{16,20},{18,... | collective-permute-start | bytes 1572872 | tf_op jit(solution)/shard_map/ppermute | solution.py:16
  33.4 1.6 %collective-permute-start.7 = (bf16[128,1024]{1,0:T(8,128)(2,1)S(1)}, bf16[128,1024]{1,0:T(8,128)(2,1)S(1)}, u32[]{:S(2)}, u32[]{:S(2)}) collective-permute-start(bf16[128,1024]{1,0:T(8,128)(2,1)S(1)} %get-tuple-element.44), channel_id=1, source_target_pairs={{0,8},{2,10},{4,12},{6,14},{8,0},{10,2},{12,4},{14,6},{16,24},{18,... | collective-permute-start | bytes 786440 | tf_op jit(solution)/shard_map/ppermute | solution.py:16
  35.0 4.5 %shard_map.50 = (f32[512,512]{1,0:T(8,128)S(1)}, f32[512,512]{1,0:T(8,128)S(1)}, f32[512,512]{1,0:T(8,128)S(1)}, f32[512,512]{1,0:T(8,128)S(1)}) custom-call(s32[2]{0:T(128)S(1)} %pad_add_fusion.place, s32[8]{0:T(128)S(1)} %pad_add_fusion.1.table, f32[16]{0:T(128)S(1)} %copy-done.2, ...), custom_call_target="tpu_custom_call", output_to_operand_aliasing={{0}: (8, {}), {1}: (9, {}), {2}: (10, {}), {3}: (11, {})} | custom-call | flops 1073741824 | tf_op jit(solution)/shard_map/pallas_call | solution.py:110
  39.4 2.5 %collective-permute-done.9.refs_0_ = bf16[128,1024]{1,0:T(8,128)(2,1)S(1)} collective-permute-done((bf16[128,1024]{1,0:T(8,128)(2,1)S(1)}, bf16[128,1024]{1,0:T(8,128)(2,1)S(1)}, u32[]{:S(2)}, u32[]{:S(2)}) %collective-permute-start.9) | collective-permute-done | bytes 262176 | tf_op jit(solution)/shard_map/ppermute | solution.py:16
  41.9 0.5 collective-permute-start.11
  42.5 4.1 %shard_map.52 = (f32[512,512]{1,0:T(8,128)S(1)}, f32[512,512]{1,0:T(8,128)S(1)}, f32[512,512]{1,0:T(8,128)S(1)}, f32[512,512]{1,0:T(8,128)S(1)}) custom-call(s32[2]{0:T(128)S(1)} %pad_add_fusion.place, s32[8]{0:T(128)S(1)} %pad_add_fusion.1.table, f32[16]{0:T(128)S(1)} %copy-done.2, ...), custom_call_target="tpu_custom_call", output_to_operand_aliasing={{0}: (9, {}), {1}: (10, {}), {2}: (11, {}), {3}: (12, {})} | custom-call | flops 1610612736 | tf_op jit(solution)/shard_map/pallas_call | solution.py:110
  46.6 1.6 %collective-permute-start.10 = (bf16[128,1024]{1,0:T(8,128)(2,1)S(1)}, bf16[128,1024]{1,0:T(8,128)(2,1)S(1)}, u32[]{:S(2)}, u32[]{:S(2)}) collective-permute-start(bf16[128,1024]{1,0:T(8,128)(2,1)S(1)} %shard_map.53.refs_3_), channel_id=1, source_target_pairs={{0,4},{2,6},{4,0},{6,2},{8,12},{10,14},{12,8},{14,10},{16,20},{18,... | collective-permute-start | bytes 786440 | tf_op jit(solution)/shard_map/ppermute | solution.py:16
  48.2 3.9 %shard_map.54 = (f32[512,512]{1,0:T(8,128)S(1)}, f32[512,512]{1,0:T(8,128)S(1)}, f32[512,512]{1,0:T(8,128)S(1)}, f32[512,512]{1,0:T(8,128)S(1)}) custom-call(s32[2]{0:T(128)S(1)} %pad_add_fusion.place, s32[8]{0:T(128)S(1)} %pad_add_fusion.1.table, f32[16]{0:T(128)S(1)} %copy-done.2, ...), custom_call_target="tpu_custom_call", output_to_operand_aliasing={{0}: (9, {}), {1}: (10, {}), {2}: (11, {}), {3}: (12, {})} | custom-call | flops 1610612736 | tf_op jit(solution)/shard_map/pallas_call | solution.py:110
  52.1 0.4 collective-permute-done.11.refs_2_
  52.6 2.6 %shard_map.55 = (f32[512,512]{1,0:T(8,128)S(1)}, f32[512,512]{1,0:T(8,128)S(1)}, f32[512,512]{1,0:T(8,128)S(1)}, f32[512,512]{1,0:T(8,128)S(1)}) custom-call(s32[2]{0:T(128)S(1)} %pad_add_fusion.place, s32[8]{0:T(128)S(1)} %pad_add_fusion.1.table, f32[16]{0:T(128)S(1)} %copy-done.2, ...), custom_call_target="tpu_custom_call", output_to_operand_aliasing={{0}: (8, {}), {1}: (9, {}), {2}: (10, {}), {3}: (11, {})} | custom-call | flops 536870912 | tf_op jit(solution)/shard_map/pallas_call | solution.py:110
  55.2 1.0 %collective-permute-done.10.refs_1_ = bf16[128,1024]{1,0:T(8,128)(2,1)S(1)} collective-permute-done((bf16[128,1024]{1,0:T(8,128)(2,1)S(1)}, bf16[128,1024]{1,0:T(8,128)(2,1)S(1)}, u32[]{:S(2)}, u32[]{:S(2)}) %collective-permute-start.10) | collective-permute-done | bytes 262176 | tf_op jit(solution)/shard_map/ppermute | solution.py:16
  56.2 1.9 %shard_map.57 = (f32[512,512]{1,0:T(8,128)S(1)}, bf16[512,512]{1,0:T(8,128)(2,1)S(1)}) custom-call(s32[2]{0:T(128)S(1)} %pad_add_fusion.place, s32[8]{0:T(128)S(1)} %pad_add_fusion.1.table, f32[16]{0:T(128)S(1)} %copy-done.2, f32[4,128]{1,0:T(4,128)S(1)} %bitcast.26, f32[512,128]{1,0:T(8,128)S(1)} %broadcast_in_dim.4.e_col, ...), custom_call_target="tpu_custom_call", output_to_operand_aliasing={{0}: (7, {})} | custom-call | flops 268435456 | tf_op jit(solution)/shard_map/pallas_call | solution.py:110
  58.2 0.5 collective-permute-start.13
  58.7 1.9 %shard_map.56 = (f32[512,512]{1,0:T(8,128)S(1)}, f32[512,512]{1,0:T(8,128)S(1)}) custom-call(s32[2]{0:T(128)S(1)} %pad_add_fusion.place, s32[8]{0:T(128)S(1)} %pad_add_fusion.1.table, f32[16]{0:T(128)S(1)} %copy-done.2, f32[4,128]{1,0:T(4,128)S(1)} %bitcast.27, f32[512,128]{1,0:T(8,128)S(1)} %broadcast_in_dim.4.e_col, ...), custom_call_target="tpu_custom_call", output_to_operand_aliasing={{0}: (7, {}), {1}: (8, {})} | custom-call | flops 268435456 | tf_op jit(solution)/shard_map/pallas_call | solution.py:110
  60.8 0.6 collective-permute-start.15
  61.6 13.2 %collective-permute-done.15 = bf16[512,512]{1,0:T(8,128)(2,1)S(1)} collective-permute-done((bf16[512,512]{1,0:T(8,128)(2,1)S(1)}, bf16[512,512]{1,0:T(8,128)(2,1)S(1)}, u32[]{:S(2)}, u32[]{:S(2)}) %collective-permute-start.15) | collective-permute-done | bytes 524320 | tf_op jit(solution)/shard_map/ppermute | solution.py:16
  74.8 1.2 %add_bitcast_fusion = f32[1,512,512]{2,1,0:T(8,128)} fusion(bf16[512,512]{1,0:T(8,128)(2,1)S(1)} %collective-permute-done.15, f32[512,512]{1,0:T(8,128)S(1)} %get-tuple-element.63, f32[512,512]{1,0:T(8,128)S(1)} %collective-permute-done.13), kind=kLoop, calls=%fused_computation | loop fusion | flops 786432 | bytes 3670016 | tf_op jit(solution)/shard_map/broadcast_in_dim | solution.py:183
  (31 shorter events, 2.0 us)
Async XLA Ops:
  0.0 9.0 %copy-start = (bf16[1,512,1024]{2,1,0:T(8,128)(2,1)S(1)}, bf16[1,512,1024]{2,1,0:T(8,128)(2,1)}, u32[]{:S(2)}) copy-start(bf16[1,512,1024]{2,1,0:T(8,128)(2,1)} %param.4) | copy-start | bytes 3145732
  0.0 11.5 %collective-permute-start.3 = (bf16[512,1024]{1,0:T(8,128)(2,1)}, bf16[512,1024]{1,0:T(8,128)(2,1)S(1)}, u32[]{:S(2)}, u32[]{:S(2)}) collective-permute-start(bf16[512,1024]{1,0:T(8,128)(2,1)} %bitcast.12), channel_id=1, source_target_pairs={{0,2},{2,0},{4,6},{6,4},{8,10},{10,8},{12,14},{14,12},{16,18},{18,... | collective-permute-start | bytes 3145736 | tf_op jit(solution)/shard_map/ppermute | solution.py:16
  2.2 5.3 %copy-start.3 = (s32[4]{0:T(128)S(1)}, s32[4]{0:T(128)}, u32[]{:S(2)}) copy-start(s32[4]{0:T(128)} %param.7) | copy-start | bytes 52
  2.2 15.5 %collective-permute-start.5 = (bf16[128,1024]{1,0:T(8,128)(2,1)}, bf16[128,1024]{1,0:T(8,128)(2,1)S(1)}, u32[]{:S(2)}, u32[]{:S(2)}) collective-permute-start(bf16[128,1024]{1,0:T(8,128)(2,1)} %get-tuple-element.69), channel_id=1, source_target_pairs={{0,8},{2,10},{4,12},{6,14},{8,0},{10,2},{12,4},{14,6},{16,24},{18,... | collective-permute-start | bytes 786440 | tf_op jit(solution)/shard_map/ppermute | solution.py:16
  4.9 15.9 %collective-permute-start.6 = (bf16[128,1024]{1,0:T(8,128)(2,1)}, bf16[128,1024]{1,0:T(8,128)(2,1)S(1)}, u32[]{:S(2)}, u32[]{:S(2)}) collective-permute-start(bf16[128,1024]{1,0:T(8,128)(2,1)} %get-tuple-element.69), channel_id=1, source_target_pairs={{0,16},{2,18},{4,20},{6,22},{8,24},{10,26},{12,28},{14,30},{16,0},... | collective-permute-start | bytes 786440 | tf_op jit(solution)/shard_map/ppermute | solution.py:16
  7.5 3.5 %collective-permute-start = (s32[4]{0:T(128)S(1)}, s32[4]{0:T(128)S(1)}, u32[]{:S(2)}, u32[]{:S(2)}) collective-permute-start(s32[4]{0:T(128)S(1)} %copy-done.3), channel_id=1, source_target_pairs={{0,1},{1,0},{2,3},{3,2},{4,5},{5,4},{6,7},{7,6},{8,9},{9,8},{10,11... | collective-permute-start | bytes 56 | tf_op jit(solution)/shard_map/ppermute | solution.py:16
  9.0 15.0 %collective-permute-start.4 = (bf16[256,1024]{1,0:T(8,128)(2,1)S(1)}, bf16[256,1024]{1,0:T(8,128)(2,1)}, u32[]{:S(2)}, u32[]{:S(2)}) collective-permute-start(bf16[256,1024]{1,0:T(8,128)(2,1)S(1)} %dynamic-slice_bitcast_fusion.refs_2_), channel_id=1, source_target_pairs={{0,4},{2,6},{4,0},{6,2},{8,12},{10,14},{12,8},{14,10},{16,20},{18,... | collective-permute-start | bytes 1572872 | tf_op jit(solution)/shard_map/ppermute | solution.py:16
  10.7 1.1 %copy-start.1 = (f32[512]{0:T(512)S(1)}, f32[512]{0:T(512)}, u32[]{:S(2)}) copy-start(f32[512]{0:T(512)} %param.6) | copy-start | bytes 6148
  11.0 17.7 %collective-permute-start.1 = (bf16[128,1024]{1,0:T(8,128)(2,1)S(1)}, bf16[128,1024]{1,0:T(8,128)(2,1)S(1)}, u32[]{:S(2)}, u32[]{:S(2)}) collective-permute-start(bf16[128,1024]{1,0:T(8,128)(2,1)S(1)} %get-tuple-element.70), channel_id=1, source_target_pairs={{0,8},{2,10},{4,12},{6,14},{8,0},{10,2},{12,4},{14,6},{16,24},{18,... | collective-permute-start | bytes 786440 | tf_op jit(solution)/shard_map/ppermute | solution.py:16
  11.6 19.8 %collective-permute-start.2 = (bf16[128,1024]{1,0:T(8,128)(2,1)S(1)}, bf16[128,1024]{1,0:T(8,128)(2,1)S(1)}, u32[]{:S(2)}, u32[]{:S(2)}) collective-permute-start(bf16[128,1024]{1,0:T(8,128)(2,1)S(1)} %get-tuple-element.70), channel_id=1, source_target_pairs={{0,16},{2,18},{4,20},{6,22},{8,24},{10,26},{12,28},{14,30},{16,0},... | collective-permute-start | bytes 786440 | tf_op jit(solution)/shard_map/ppermute | solution.py:16
  11.9 0.7 copy-start.2
  20.8 21.7 %collective-permute-start.8 = (bf16[256,1024]{1,0:T(8,128)(2,1)S(1)}, bf16[256,1024]{1,0:T(8,128)(2,1)S(1)}, u32[]{:S(2)}, u32[]{:S(2)}) collective-permute-start(bf16[256,1024]{1,0:T(8,128)(2,1)S(1)} %constant_dynamic-update-slice_fusion.refs_3_), channel_id=1, source_target_pairs={{0,4},{2,6},{4,0},{6,2},{8,12},{10,14},{12,8},{14,10},{16,20},{18,... | collective-permute-start | bytes 1572872 | tf_op jit(solution)/shard_map/ppermute | solution.py:16
  31.4 16.8 %collective-permute-start.12 = (bf16[256,1024]{1,0:T(8,128)(2,1)S(1)}, bf16[256,1024]{1,0:T(8,128)(2,1)S(1)}, u32[]{:S(2)}, u32[]{:S(2)}) collective-permute-start(bf16[256,1024]{1,0:T(8,128)(2,1)S(1)} %constant_dynamic-update-slice_fusion.2.refs_2_), channel_id=1, source_target_pairs={{0,4},{2,6},{4,0},{6,2},{8,12},{10,14},{12,8},{14,10},{16,20},{18,... | collective-permute-start | bytes 1572872 | tf_op jit(solution)/shard_map/ppermute | solution.py:16
  32.9 9.0 %collective-permute-start.9 = (bf16[128,1024]{1,0:T(8,128)(2,1)S(1)}, bf16[128,1024]{1,0:T(8,128)(2,1)S(1)}, u32[]{:S(2)}, u32[]{:S(2)}) collective-permute-start(bf16[128,1024]{1,0:T(8,128)(2,1)S(1)} %get-tuple-element.39), channel_id=1, source_target_pairs={{0,8},{2,10},{4,12},{6,14},{8,0},{10,2},{12,4},{14,6},{16,24},{18,... | collective-permute-start | bytes 786440 | tf_op jit(solution)/shard_map/ppermute | solution.py:16
  33.4 13.3 %collective-permute-start.7 = (bf16[128,1024]{1,0:T(8,128)(2,1)S(1)}, bf16[128,1024]{1,0:T(8,128)(2,1)S(1)}, u32[]{:S(2)}, u32[]{:S(2)}) collective-permute-start(bf16[128,1024]{1,0:T(8,128)(2,1)S(1)} %get-tuple-element.44), channel_id=1, source_target_pairs={{0,8},{2,10},{4,12},{6,14},{8,0},{10,2},{12,4},{14,6},{16,24},{18,... | collective-permute-start | bytes 786440 | tf_op jit(solution)/shard_map/ppermute | solution.py:16
  41.9 10.6 %collective-permute-start.11 = (bf16[128,1024]{1,0:T(8,128)(2,1)S(1)}, bf16[128,1024]{1,0:T(8,128)(2,1)S(1)}, u32[]{:S(2)}, u32[]{:S(2)}) collective-permute-start(bf16[128,1024]{1,0:T(8,128)(2,1)S(1)} %shard_map.51.refs_3_), channel_id=1, source_target_pairs={{0,4},{2,6},{4,0},{6,2},{8,12},{10,14},{12,8},{14,10},{16,20},{18,... | collective-permute-start | bytes 786440 | tf_op jit(solution)/shard_map/ppermute | solution.py:16
  46.6 9.6 %collective-permute-start.10 = (bf16[128,1024]{1,0:T(8,128)(2,1)S(1)}, bf16[128,1024]{1,0:T(8,128)(2,1)S(1)}, u32[]{:S(2)}, u32[]{:S(2)}) collective-permute-start(bf16[128,1024]{1,0:T(8,128)(2,1)S(1)} %shard_map.53.refs_3_), channel_id=1, source_target_pairs={{0,4},{2,6},{4,0},{6,2},{8,12},{10,14},{12,8},{14,10},{16,20},{18,... | collective-permute-start | bytes 786440 | tf_op jit(solution)/shard_map/ppermute | solution.py:16
  58.1 2.5 %collective-permute-start.14 = (bf16[512,512]{1,0:T(8,128)(2,1)S(1)}, bf16[512,512]{1,0:T(8,128)(2,1)S(1)}, u32[]{:S(2)}, u32[]{:S(2)}) collective-permute-start(bf16[512,512]{1,0:T(8,128)(2,1)S(1)} %get-tuple-element.68), channel_id=1, source_target_pairs={{0,2},{2,0},{4,6},{6,4},{8,10},{10,8},{12,14},{14,12},{16,18},{18,... | collective-permute-start | bytes 1572872 | tf_op jit(solution)/shard_map/ppermute | solution.py:16
  58.2 3.4 %collective-permute-start.13 = (f32[512,512]{1,0:T(8,128)S(1)}, f32[512,512]{1,0:T(8,128)S(1)}, u32[]{:S(2)}, u32[]{:S(2)}) collective-permute-start(f32[512,512]{1,0:T(8,128)S(1)} %get-tuple-element.66), channel_id=1, source_target_pairs={{0,2},{2,0},{4,6},{6,4},{8,10},{10,8},{12,14},{14,12},{16,18},{18,... | collective-permute-start | bytes 3145736 | tf_op jit(solution)/shard_map/ppermute | solution.py:16
  60.8 14.0 %collective-permute-start.15 = (bf16[512,512]{1,0:T(8,128)(2,1)S(1)}, bf16[512,512]{1,0:T(8,128)(2,1)S(1)}, u32[]{:S(2)}, u32[]{:S(2)}) collective-permute-start(bf16[512,512]{1,0:T(8,128)(2,1)S(1)} %add_convert_fusion), channel_id=1, source_target_pairs={{0,1},{1,0},{2,3},{3,2},{4,5},{5,4},{6,7},{7,6},{8,9},{9,8},{10,11... | collective-permute-start | bytes 1572872 | tf_op jit(solution)/shard_map/ppermute | solution.py:16

commit v3 on v2

v3 whole, which is shorter than its diff:
```python
import functools

import jax
import jax.numpy as jnp
from jax import lax
from jax.experimental import pallas as pl
from jax.experimental.pallas import tpu as pltpu
from jax.sharding import PartitionSpec as P

CHUNK = 256
SPLIT = 4
MIB = 1024 * 1024


def exchange(block, axis, mask):
    devices = range(lax.axis_size(axis))
    return lax.ppermute(block, axis, [(i, i ^ mask) for i in devices])


def gate(blocks, after):
    anywhere = pl.BlockSpec(memory_space=pl.ANY)
    return pl.pallas_call(
        lambda *refs: None,
        out_shape=[jax.ShapeDtypeStruct(b.shape, b.dtype) for b in blocks],
        in_specs=[anywhere] * (len(blocks) + len(after)),
        out_specs=[anywhere] * len(blocks),
        input_output_aliases={i: i for i in range(len(blocks))},
        compiler_params=pltpu.CompilerParams(vmem_limit_bytes=MIB),
        cost_estimate=pl.CostEstimate(flops=0, bytes_accessed=0, transcendentals=0),
    )(*blocks, *after)


def join_kernel(*refs):
    out, start = refs[-1], 0
    for ref in refs[:-1]:
        out[start : start + ref.shape[0]] = ref[...]
        start += ref.shape[0]


def join(blocks):
    rows = sum(b.shape[0] for b in blocks)
    whole = pl.BlockSpec(memory_space=pltpu.VMEM)
    return pl.pallas_call(
        join_kernel,
        out_shape=pltpu.VMEM((rows, blocks[0].shape[1]), blocks[0].dtype),
        in_specs=[whole] * len(blocks),
        out_specs=whole,
        compiler_params=pltpu.CompilerParams(vmem_limit_bytes=8 * MIB),
        cost_estimate=pl.CostEstimate(flops=0, bytes_accessed=0, transcendentals=0),
    )(*[in_vmem(b) for b in blocks])


def absorb_kernel(plan, sizes, place, table, e_occ, e_half, e_col, *refs):
    left_masks, block_plan, fresh, parts = plan
    occupied, width = sizes
    n_left, n_block = len(left_masks), len(block_plan)
    n_total = n_left * len(parts)
    lefts, refs = refs[:n_left], refs[n_left:]
    blocks, refs = refs[:n_block], refs[n_block:]
    olds = None if fresh else refs[:n_total]
    news = refs[-n_total:]
    here, slot = place[0], place[1]
    half = e_half.shape[1]

    merged = []
    for block, runs in zip(blocks, block_plan):
        if merged and len(merged[-1][1]) + len(runs) <= 2:
            merged[-1][0].append(block)
            merged[-1][1].extend(runs)
        else:
            merged.append(([block], list(runs)))

    def weight(k, l):
        ahead = (k - l) & (occupied - 1)
        back = (l - k) & (occupied - 1)
        total = jnp.int32(0)
        for n in range(table.shape[0]):
            d = table[n] & (occupied - 1)
            total = total - (d == ahead).astype(jnp.int32) - (d == back).astype(jnp.int32)
        return total.astype(jnp.float32)

    masks = {mask for runs in block_plan for mask, _, _ in runs}
    weights = [{m: weight(here ^ k, here ^ m) for m in sorted(masks)} for k in left_masks]

    def amplitudes(i, at):
        column = e_col[at : at + CHUNK, :1] - e_occ[here ^ left_masks[i]]
        groups = {}
        for members, runs in merged:
            block = [member[...] for member in members]
            block = jnp.concatenate(block, axis=0) if len(block) > 1 else block[0]
            pair = lax.dot_general(
                lefts[i][at : at + CHUNK], block, (((1,), (1,)), ((), ())),
                preferred_element_type=jnp.float32,
            )
            rows = [
                e_half[pl.ds((slot ^ r) * 2 + h, 1), :] - e_occ[here ^ mask] for mask, r, h in runs
            ]
            row = jnp.concatenate(rows, axis=1) if len(rows) > 1 else rows[0]
            amp = (pair / (column + row)).astype(jnp.bfloat16)
            places = [(b, s) for b in members for s in range(0, b.shape[0], half)]
            for n, ((mask, _, _), place) in enumerate(zip(runs, places)):
                groups.setdefault(mask, []).append((amp[:, n * half : (n + 1) * half], *place))
        return groups

    tasks = [(i, at) for i in range(n_left) for at in range(0, lefts[0].shape[0], CHUNK)]
    ready = [amplitudes(*task) for task in tasks]
    for (i, at), groups in zip(tasks, ready):
        for j, q in enumerate(parts):
            lanes = pl.ds(pl.multiple_of((slot ^ q) * width, width), width)
            total = None if fresh else olds[i * len(parts) + j][at : at + CHUNK]
            for mask, members in groups.items():
                amps = [amp for amp, _, _ in members]
                sides = [block[s : s + half, lanes] for _, block, s in members]
                term = weights[i][mask] * jnp.dot(
                    jnp.concatenate(amps, axis=1) if len(amps) > 1 else amps[0],
                    jnp.concatenate(sides, axis=0) if len(sides) > 1 else sides[0],
                    preferred_element_type=jnp.float32,
                )
                total = term if total is None else total + term
            news[i * len(parts) + j][at : at + CHUNK] = total


def in_vmem(array):
    return pltpu.with_memory_space_constraint(array, pltpu.VMEM)


def absorb(context, width, lefts, blocks, parts, olds, cost):
    virtuals, aux = lefts[0][0].shape
    keys = [(mask, q) for _, mask in lefts for q in parts]
    fresh = keys[0] not in olds
    plan = (tuple(m for _, m in lefts), tuple(tuple(r) for _, r in blocks), fresh, tuple(parts))
    sizes = (context[2].shape[0], width)
    arrays = [in_vmem(a) for a, _ in lefts] + [in_vmem(b) for b, _ in blocks]
    base = len(context) + len(arrays)
    arrays += [] if fresh else [in_vmem(olds[key]) for key in keys]
    scalar = pl.BlockSpec(memory_space=pltpu.SMEM)
    whole = pl.BlockSpec(memory_space=pltpu.VMEM)
    depth = sum(b.shape[0] for b, _ in blocks)
    news = pl.pallas_call(
        functools.partial(absorb_kernel, plan, sizes),
        out_shape=[pltpu.VMEM((virtuals, width), jnp.float32) for _ in keys],
        in_specs=[scalar] * 3 + [whole] * (len(context) - 3 + len(arrays)),
        out_specs=[whole] * len(keys),
        input_output_aliases={} if fresh else {base + i: i for i in range(len(keys))},
        compiler_params=pltpu.CompilerParams(vmem_limit_bytes=24 * MIB),
        cost_estimate=pl.CostEstimate(
            flops=cost * 2 * len(lefts) * virtuals * depth * (aux + width * len(parts)),
            bytes_accessed=0, transcendentals=0,
        ),
    )(*context, *arrays)
    return {**olds, **dict(zip(keys, news))}


def across(total, pieces):
    return jnp.concatenate([exchange(t, "blk", 1) for t in jnp.split(total, pieces)])


def per_device(integrals, eps_occ, eps_vir, offsets):
    tile = integrals[0]
    virtuals, aux = tile.shape
    reps = lax.axis_size("rep")
    lines = lax.axis_size("blk") // 4
    here = lax.axis_index("blk")
    slot = lax.axis_index("rep")
    part = virtuals // reps
    half = part // 2
    width = aux // reps
    every = list(range(reps))
    rest = every[1:]

    mine = lax.dynamic_slice_in_dim(tile, slot * part, part, axis=0)
    line = {(0, 0): mine[:half], (0, 1): mine[half:]}
    side = {}
    beside = exchange(mine, "blk", 2)
    table = offsets
    bit = 1
    while bit < reps:
        table = jnp.concatenate([table, exchange(table, "rep", bit)])
        bit *= 2
    twin = exchange(tile, "blk", 1)
    own, other = (tile, 0), (twin, 1)
    context = [
        jnp.stack([here, slot]).astype(jnp.int32),
        table,
        eps_occ,
        eps_vir.reshape(2 * reps, half),
        jnp.broadcast_to(eps_vir[:, None], (virtuals, 128)),
    ]

    def add(blocks, totals, parts=every, lefts=(own, other), cost=0):
        return absorb(context, width, lefts, blocks, parts, totals, cost)

    def travel(members, h, after):
        for m in members:
            low = m & -m
            line[m, h] = exchange(line[m ^ low, h], "blk", 4 * low)
        for m, block in zip(members, gate([line[m, h] for m in members], after)):
            line[m, h] = block

    def lines_of(m, h):
        return (line[m, h], [(4 * m, 0, h)])

    def sides_of(m, h):
        return (side[m, h], [(4 * m + 2, 0, h)])

    levels = [[m for m in range(1, lines) if m.bit_count() == n] for n in range(1, lines.bit_length())]
    singles, final = levels[0], lines - 1
    others = [m for level in levels[1:] for m in level]
    by = final & -final
    totals = add([(mine, [(0, 0, 0), (0, 0, 1)])], {})
    travel(singles, 0, [beside, totals[0, 0]])
    group = join([line[m, 0] for m in singles])
    group_side = exchange(group, "blk", 2)
    (line[0, 1],) = gate([line[0, 1]], [twin])
    totals = add([(beside, [(2, 0, 0), (2, 0, 1)])], totals)
    travel(singles, 1, [totals[0, 0]])
    for m in singles[::-1]:
        side[m, 1] = exchange(line[m, 1], "blk", 2)
    blocks = [(group, [(4 * m, 0, 0) for m in singles])] + [lines_of(m, 1) for m in singles]
    late = []
    for m in others:
        travel([m], 0, [line[singles[0], 1]])
        side[m, 0] = exchange(line[m, 0], "blk", 2)
        late.append(lines_of(m, 0))
        if m != final:
            travel([m], 1, [])
            side[m, 1] = exchange(line[m, 1], "blk", 2)
            late.append(lines_of(m, 1))
    totals = add(blocks, totals)
    line[final, 1] = exchange(line[final ^ by, 1], "blk", 4 * by)
    (passed,) = gate([side[final ^ by, 1]], [totals[0, 0]])
    side[final ^ by, 1] = passed
    side[final, 1] = exchange(passed, "blk", 4 * by)
    (group_side,) = gate([group_side], [passed])
    totals = add(late + [(group_side, [(4 * m + 2, 0, 0) for m in singles])], totals)
    blocks = [lines_of(final, 1)] + [sides_of(m, 1) for m in singles[::-1]]
    totals = add(blocks, totals)
    blocks = [sides_of(m, h) for m, h in side if m not in singles]

    came = []
    if rest:
        theirs = add(blocks, totals, rest, [other])
        ours = add(blocks, totals, rest, [own])
        sent = [(ours[0, q] + across(theirs[1, q], 1)).astype(jnp.bfloat16) for q in rest]
        came = [exchange(s, "rep", q) for s, q in zip(sent, rest)]
        held = gate([block for block, _ in blocks], sent)
        blocks = [(block, runs) for block, (_, runs) in zip(held, blocks)]
    totals = add(blocks, totals, [0], cost=0)
    gamma = totals[0, 0] + across(totals[1, 0], SPLIT)
    for c in came:
        gamma = gamma + c.astype(jnp.float32)
    return gamma[None]


def solution(mesh):
    in_specs = (P("blk", None, None), P(), P(), P("rep"))
    out_specs = P("blk", None, "rep")
    return jax.shard_map(
        per_device, mesh=mesh, in_specs=in_specs, out_specs=out_specs, check_vma=False
    )
```

time: 76.2 us -> 70.8 us (0.929)
  Pallas kernels: 25.9 us -> 20 us
  waiting for transfers between devices: 28 us -> 26.6 us
  starting transfers between devices: 17.8 us -> 18.9 us
    pallas_call x8, Pallas kernels: 25.9 us -> 18.9 us  [absorb(): pl.pallas_call(functools.partial(absorb_kernel, plan, sizes), out_shape=[...]
    ppermute x16 -> x20, waiting for transfers between devices: 28 us -> 26.6 us  [exchange(): return lax.ppermute(block, axis, [(i, i ^ mask) for i in devices])]
    ppermute x16 -> x20, starting transfers between devices: 17.8 us -> 18.9 us  [exchange(): return lax.ppermute(block, axis, [(i, i ^ mask) for i in devices])]
    pallas_call x0 -> x1, Pallas kernels: none -> 1.06 us  [join(): pl.pallas_call(join_kernel, out_shape=pltpu.VMEM((rows, blocks[0].shape[1...]
    dynamic_slice x1, local copies, waits for them, and re-layouts: 0.03 us -> 1.08 us  [per_device(): mine = lax.dynamic_slice_in_dim(tile, slot * part, part, axis=0)]
    slice x1, local copies, waits for them, and re-layouts: 1.76 us -> 0.83 us  [per_device(): line = {(0, 0): mine[:half], (0, 1): mine[half:]}]
  transfers between devices with their start and end apart: 16 -> 20, of which waited for: 11 -> 14; matrix products, arithmetic and copies ran while one was open for 3% -> 3% of each run, Pallas kernels for 31% -> 27%
where the time goes in v3:
time: 70.8 us; the launch traced here: 70.6 us
  waiting for transfers between devices  26.6 us (38%)
  Pallas kernels  20 us (28%)
  starting transfers between devices  18.9 us (27%)
  local copies, waits for them, and re-layouts  3.29 us (5%)
  other arithmetic  1.64 us (2%)
    ppermute x20, waiting for transfers between devices, exchange(): return lax.ppermute(block, axis, [(i, i ^ mask) for i in devices])  26.6 us
    pallas_call x8, Pallas kernels, absorb(): pl.pallas_call(functools.partial(absorb_kernel, plan, sizes), out_shape=[...  18.9 us
    ppermute x20, starting transfers between devices, exchange(): return lax.ppermute(block, axis, [(i, i ^ mask) for i in devices])  18.9 us
  transfers between devices with their start and end apart: 20, of which 14 were waited for; matrix products, arithmetic and copies ran while one was open for 3% of the time, Pallas kernels for 27%

profile of v3, /device:TPU:0, one launch (start us, length us, event | category | flops | bytes accessed | tf_op | source)
XLA Modules:
  0.0 70.6 jit_solution(7423404924418715476)
XLA Ops:
  0.5 1.1 %dynamic-slice_bitcast_fusion.refs_2_ = bf16[256,1024]{1,0:T(8,128)(2,1)S(1)} fusion(bf16[1,512,1024]{2,1,0:T(8,128)(2,1)} %param.4, s32[]{:T(128)S(6)} %select_n.3), kind=kLoop, calls=%fused_computation.4 | loop fusion | bytes 1048580 | tf_op jit(solution)/shard_map/dynamic_slice | solution.py:171
  1.5 2.6 %collective-permute-start.4 = (bf16[256,1024]{1,0:T(8,128)(2,1)S(1)}, bf16[256,1024]{1,0:T(8,128)(2,1)S(1)}, u32[]{:S(2)}, u32[]{:S(2)}) collective-permute-start(bf16[256,1024]{1,0:T(8,128)(2,1)S(1)} %dynamic-slice_bitcast_fusion.refs_2_), channel_id=1, source_target_pairs={{0,4},{2,6},{4,0},{6,2},{8,12},{10,14},{12,8},{14,10},{16,20},{18,... | collective-permute-start | bytes 1572872 | tf_op jit(solution)/shard_map/ppermute | solution.py:17
  4.2 0.8 %dynamic-slice_bitcast_fusion.1 = (bf16[128,1024]{1,0:T(8,128)(2,1)}, bf16[128,1024]{1,0:T(8,128)(2,1)}) fusion(bf16[1,512,1024]{2,1,0:T(8,128)(2,1)S(1)} %copy-done, s32[]{:T(128)S(6)} %add.18, s32[]{:T(128)S(6)} %select_n.3), kind=kLoop, calls=%fused_computation.5 | loop fusion | bytes 1048584 | tf_op jit(solution)/shard_map/slice | solution.py:172
  5.0 1.6 %collective-permute-start.2 = (bf16[128,1024]{1,0:T(8,128)(2,1)}, bf16[128,1024]{1,0:T(8,128)(2,1)}, u32[]{:S(2)}, u32[]{:S(2)}) collective-permute-start(bf16[128,1024]{1,0:T(8,128)(2,1)} %get-tuple-element.66), channel_id=1, source_target_pairs={{0,8},{2,10},{4,12},{6,14},{8,0},{10,2},{12,4},{14,6},{16,24},{18,... | collective-permute-start | bytes 786440 | tf_op jit(solution)/shard_map/ppermute | solution.py:17
  6.6 2.6 %collective-permute-start.3 = (bf16[128,1024]{1,0:T(8,128)(2,1)}, bf16[128,1024]{1,0:T(8,128)(2,1)}, u32[]{:S(2)}, u32[]{:S(2)}) collective-permute-start(bf16[128,1024]{1,0:T(8,128)(2,1)} %get-tuple-element.66), channel_id=1, source_target_pairs={{0,16},{2,18},{4,20},{6,22},{8,24},{10,26},{12,28},{14,30},{16,0},... | collective-permute-start | bytes 786440 | tf_op jit(solution)/shard_map/ppermute | solution.py:17
  9.2 1.5 %collective-permute-start = (s32[4]{0:T(128)S(1)}, s32[4]{0:T(128)S(1)}, u32[]{:S(2)}, u32[]{:S(2)}) collective-permute-start(s32[4]{0:T(128)S(1)} %copy-done.3), channel_id=1, source_target_pairs={{0,1},{1,0},{2,3},{3,2},{4,5},{5,4},{6,7},{7,6},{8,9},{9,8},{10,11... | collective-permute-start | bytes 56 | tf_op jit(solution)/shard_map/ppermute | solution.py:17
  11.2 1.6 %collective-permute-done = s32[4]{0:T(128)S(1)} collective-permute-done((s32[4]{0:T(128)S(1)}, s32[4]{0:T(128)S(1)}, u32[]{:S(2)}, u32[]{:S(2)}) %collective-permute-start) | collective-permute-done | bytes 48 | tf_op jit(solution)/shard_map/ppermute | solution.py:17
  13.9 0.7 copy-done.2
  14.5 1.8 %shard_map.46 = (f32[512,512]{1,0:T(8,128)S(1)}, f32[512,512]{1,0:T(8,128)S(1)}, f32[512,512]{1,0:T(8,128)S(1)}, f32[512,512]{1,0:T(8,128)S(1)}) custom-call(s32[2]{0:T(128)S(1)} %pad_add_fusion.place, s32[8]{0:T(128)S(1)} %pad_add_fusion.1.table, f32[16]{0:T(128)S(1)} %copy-done.2, f32[4,128]{1,0:T(4,128)S(1)} %bitcast.20, ...), custom_call_target="tpu_custom_call" | custom-call | tf_op jit(solution)/shard_map/pallas_call | solution.py:139
  16.4 3.6 %collective-permute-done.2.refs_0_ = bf16[128,1024]{1,0:T(8,128)(2,1)} collective-permute-done((bf16[128,1024]{1,0:T(8,128)(2,1)}, bf16[128,1024]{1,0:T(8,128)(2,1)}, u32[]{:S(2)}, u32[]{:S(2)}) %collective-permute-start.2) | collective-permute-done | bytes 262176 | tf_op jit(solution)/shard_map/ppermute | solution.py:17
  20.0 2.4 %collective-permute-done.3.refs_1_ = bf16[128,1024]{1,0:T(8,128)(2,1)} collective-permute-done((bf16[128,1024]{1,0:T(8,128)(2,1)}, bf16[128,1024]{1,0:T(8,128)(2,1)}, u32[]{:S(2)}, u32[]{:S(2)}) %collective-permute-start.3) | collective-permute-done | bytes 262176 | tf_op jit(solution)/shard_map/ppermute | solution.py:17
  22.4 1.1 %shard_map.52.refs_2_ = bf16[256,1024]{1,0:T(8,128)(2,1)S(1)} custom-call(bf16[128,1024]{1,0:T(8,128)(2,1)} %get-tuple-element.41.refs_0_, bf16[128,1024]{1,0:T(8,128)(2,1)} %get-tuple-element.34.refs_1_), custom_call_target="tpu_custom_call" | custom-call | tf_op jit(solution)/shard_map/pallas_call | solution.py:43
  23.5 0.6 collective-permute-start.13
  24.4 2.0 %shard_map.49 = (f32[512,512]{1,0:T(8,128)S(1)}, f32[512,512]{1,0:T(8,128)S(1)}, f32[512,512]{1,0:T(8,128)S(1)}, f32[512,512]{1,0:T(8,128)S(1)}) custom-call(s32[2]{0:T(128)S(1)} %pad_add_fusion.place, s32[8]{0:T(128)S(1)} %pad_add_fusion.1.table, f32[16]{0:T(128)S(1)} %copy-done.2, ...), custom_call_target="tpu_custom_call", output_to_operand_aliasing={{0}: (8, {}), {1}: (9, {}), {2}: (10, {}), {3}: (11, {})} | custom-call | tf_op jit(solution)/shard_map/pallas_call | solution.py:139
  26.4 4.7 %collective-permute-done.6.refs_0_ = bf16[128,1024]{1,0:T(8,128)(2,1)S(1)} collective-permute-done((bf16[128,1024]{1,0:T(8,128)(2,1)}, bf16[128,1024]{1,0:T(8,128)(2,1)S(1)}, u32[]{:S(2)}, u32[]{:S(2)}) %collective-permute-start.6) | collective-permute-done | bytes 262176 | tf_op jit(solution)/shard_map/ppermute | solution.py:17
  31.1 1.2 %collective-permute-done.7.refs_1_ = bf16[128,1024]{1,0:T(8,128)(2,1)} collective-permute-done((bf16[128,1024]{1,0:T(8,128)(2,1)}, bf16[128,1024]{1,0:T(8,128)(2,1)}, u32[]{:S(2)}, u32[]{:S(2)}) %collective-permute-start.7) | collective-permute-done | bytes 262176 | tf_op jit(solution)/shard_map/ppermute | solution.py:17
  32.2 0.5 collective-permute-start.9
  32.8 1.8 %collective-permute-start.11 = (bf16[128,1024]{1,0:T(8,128)(2,1)}, bf16[128,1024]{1,0:T(8,128)(2,1)S(1)}, u32[]{:S(2)}, u32[]{:S(2)}) collective-permute-start(bf16[128,1024]{1,0:T(8,128)(2,1)} %get-tuple-element.40.refs_4_), channel_id=1, source_target_pairs={{0,8},{2,10},{4,12},{6,14},{8,0},{10,2},{12,4},{14,6},{16,24},{18,... | collective-permute-start | bytes 786440 | tf_op jit(solution)/shard_map/ppermute | solution.py:17
  34.5 1.5 %collective-permute-start.12 = (bf16[128,1024]{1,0:T(8,128)(2,1)S(1)}, bf16[128,1024]{1,0:T(8,128)(2,1)S(1)}, u32[]{:S(2)}, u32[]{:S(2)}) collective-permute-start(bf16[128,1024]{1,0:T(8,128)(2,1)S(1)} %get-tuple-element.39.refs_1_.refs_3_), channel_id=1, source_target_pairs={{0,4},{2,6},{4,0},{6,2},{8,12},{10,14},{12,8},{14,10},{16,20},{18,... | collective-permute-start | bytes 786440 | tf_op jit(solution)/shard_map/ppermute | solution.py:17
  36.0 0.8 %collective-permute-done.5.refs_0_ = bf16[128,1024]{1,0:T(8,128)(2,1)S(1)} collective-permute-done((bf16[128,1024]{1,0:T(8,128)(2,1)}, bf16[128,1024]{1,0:T(8,128)(2,1)S(1)}, u32[]{:S(2)}, u32[]{:S(2)}) %collective-permute-start.5) | collective-permute-done | bytes 262176 | tf_op jit(solution)/shard_map/ppermute | solution.py:17
  37.0 3.7 %shard_map.53 = (f32[512,512]{1,0:T(8,128)S(1)}, f32[512,512]{1,0:T(8,128)S(1)}, f32[512,512]{1,0:T(8,128)S(1)}, f32[512,512]{1,0:T(8,128)S(1)}) custom-call(s32[2]{0:T(128)S(1)} %pad_add_fusion.place, s32[8]{0:T(128)S(1)} %pad_add_fusion.1.table, f32[16]{0:T(128)S(1)} %copy-done.2, ...), custom_call_target="tpu_custom_call", output_to_operand_aliasing={{0}: (10, {}), {1}: (11, {}), {2}: (12, {}), {3}: (13, {})} | custom-call | tf_op jit(solution)/shard_map/pallas_call | solution.py:139
  40.7 1.0 %collective-permute-done.9.refs_0_ = bf16[128,1024]{1,0:T(8,128)(2,1)S(1)} collective-permute-done((bf16[128,1024]{1,0:T(8,128)(2,1)}, bf16[128,1024]{1,0:T(8,128)(2,1)S(1)}, u32[]{:S(2)}, u32[]{:S(2)}) %collective-permute-start.9) | collective-permute-done | bytes 262176 | tf_op jit(solution)/shard_map/ppermute | solution.py:17
  41.7 1.8 %collective-permute-start.10 = (bf16[128,1024]{1,0:T(8,128)(2,1)S(1)}, bf16[128,1024]{1,0:T(8,128)(2,1)S(1)}, u32[]{:S(2)}, u32[]{:S(2)}) collective-permute-start(bf16[128,1024]{1,0:T(8,128)(2,1)S(1)} %shard_map.54.refs_1_.refs_3_), channel_id=1, source_target_pairs={{0,8},{2,10},{4,12},{6,14},{8,0},{10,2},{12,4},{14,6},{16,24},{18,... | collective-permute-start | bytes 786440 | tf_op jit(solution)/shard_map/ppermute | solution.py:17
  43.5 3.5 %shard_map.56 = (f32[512,512]{1,0:T(8,128)S(1)}, f32[512,512]{1,0:T(8,128)S(1)}, f32[512,512]{1,0:T(8,128)S(1)}, f32[512,512]{1,0:T(8,128)S(1)}) custom-call(s32[2]{0:T(128)S(1)} %pad_add_fusion.place, s32[8]{0:T(128)S(1)} %pad_add_fusion.1.table, f32[16]{0:T(128)S(1)} %copy-done.2, ...), custom_call_target="tpu_custom_call", output_to_operand_aliasing={{0}: (9, {}), {1}: (10, {}), {2}: (11, {}), {3}: (12, {})} | custom-call | tf_op jit(solution)/shard_map/pallas_call | solution.py:139
  47.3 3.7 %shard_map.57 = (f32[512,512]{1,0:T(8,128)S(1)}, f32[512,512]{1,0:T(8,128)S(1)}, f32[512,512]{1,0:T(8,128)S(1)}, f32[512,512]{1,0:T(8,128)S(1)}) custom-call(s32[2]{0:T(128)S(1)} %pad_add_fusion.place, s32[8]{0:T(128)S(1)} %pad_add_fusion.1.table, f32[16]{0:T(128)S(1)} %copy-done.2, ...), custom_call_target="tpu_custom_call", output_to_operand_aliasing={{0}: (10, {}), {1}: (11, {}), {2}: (12, {}), {3}: (13, {})} | custom-call | tf_op jit(solution)/shard_map/pallas_call | solution.py:139
  51.0 1.3 %shard_map.59 = f32[512,512]{1,0:T(8,128)S(1)} custom-call(s32[2]{0:T(128)S(1)} %pad_add_fusion.place, s32[8]{0:T(128)S(1)} %pad_add_fusion.1.table, f32[16]{0:T(128)S(1)} %copy-done.2, f32[4,128]{1,0:T(4,128)S(1)} %bitcast.25, f32[512,128]{1,0:T(8,128)S(1)} %broadcast_in_dim.4.e_col, ...), custom_call_target="tpu_custom_call", output_to_operand_aliasing={{}: (8, {})} | custom-call | tf_op jit(solution)/shard_map/pallas_call | solution.py:139
  52.4 1.3 %shard_map.58 = f32[512,512]{1,0:T(8,128)S(1)} custom-call(s32[2]{0:T(128)S(1)} %pad_add_fusion.place, s32[8]{0:T(128)S(1)} %pad_add_fusion.1.table, f32[16]{0:T(128)S(1)} %copy-done.2, f32[4,128]{1,0:T(4,128)S(1)} %bitcast.26, f32[512,128]{1,0:T(8,128)S(1)} %broadcast_in_dim.4.e_col, ...), custom_call_target="tpu_custom_call", output_to_operand_aliasing={{}: (8, {})} | custom-call | tf_op jit(solution)/shard_map/pallas_call | solution.py:139
  53.6 1.4 %collective-permute-done.14 = f32[512,512]{1,0:T(8,128)S(1)} collective-permute-done((f32[512,512]{1,0:T(8,128)S(1)}, f32[512,512]{1,0:T(8,128)S(1)}, u32[]{:S(2)}, u32[]{:S(2)}) %collective-permute-start.14) | collective-permute-done | bytes 1048608 | tf_op jit(solution)/shard_map/ppermute | solution.py:17
  55.3 1.6 %collective-permute-start.19 = (bf16[512,512]{1,0:T(8,128)(2,1)S(1)}, bf16[512,512]{1,0:T(8,128)(2,1)S(1)}, u32[]{:S(2)}, u32[]{:S(2)}) collective-permute-start(bf16[512,512]{1,0:T(8,128)(2,1)S(1)} %add_convert_fusion.refs_2_), channel_id=1, source_target_pairs={{0,1},{1,0},{2,3},{3,2},{4,5},{5,4},{6,7},{7,6},{8,9},{9,8},{10,11... | collective-permute-start | bytes 1572872 | tf_op jit(solution)/shard_map/ppermute | solution.py:17
  56.9 1.6 %shard_map.61 = (f32[512,512]{1,0:T(8,128)S(1)}, f32[512,512]{1,0:T(8,128)S(1)}) custom-call(s32[2]{0:T(128)S(1)} %pad_add_fusion.place, s32[8]{0:T(128)S(1)} %pad_add_fusion.1.table, f32[16]{0:T(128)S(1)} %copy-done.2, f32[4,128]{1,0:T(4,128)S(1)} %bitcast.27, f32[512,128]{1,0:T(8,128)S(1)} %broadcast_in_dim.4.e_col, ...), custom_call_target="tpu_custom_call", output_to_operand_aliasing={{0}: (9, {}), {1}: (10, {})} | custom-call | tf_op jit(solution)/shard_map/pallas_call | solution.py:139
  61.3 8.0 %collective-permute-done.19 = bf16[512,512]{1,0:T(8,128)(2,1)S(1)} collective-permute-done((bf16[512,512]{1,0:T(8,128)(2,1)S(1)}, bf16[512,512]{1,0:T(8,128)(2,1)S(1)}, u32[]{:S(2)}, u32[]{:S(2)}) %collective-permute-start.19) | collective-permute-done | bytes 524320 | tf_op jit(solution)/shard_map/ppermute | solution.py:17
  69.3 1.2 %fusion.1 = f32[1,512,512]{2,1,0:T(8,128)} fusion(f32[512,512]{1,0:T(8,128)S(1)} %get-tuple-element.59, f32[128,512]{1,0:T(8,128)S(1)} %collective-permute-done.18, f32[128,512]{1,0:T(8,128)S(1)} %collective-permute-done.17, f32[128,512]{1,0:T(8,128)S(1)} %collective-permute-done.16, f32[128,512]{1,0:T(8,128)S(1)} %collective-permute-done.15, ...), kind=kLoop, calls=%fused_computation.2 | loop fusion | flops 1572864 | bytes 3670016 | tf_op jit(solution)/shard_map/broadcast_in_dim | solution.py:252
  (40 shorter events, 5.9 us)
Async XLA Ops:
  0.0 4.2 %copy-start = (bf16[1,512,1024]{2,1,0:T(8,128)(2,1)S(1)}, bf16[1,512,1024]{2,1,0:T(8,128)(2,1)}, u32[]{:S(2)}) copy-start(bf16[1,512,1024]{2,1,0:T(8,128)(2,1)} %param.4) | copy-start | bytes 3145732
  0.0 10.7 %collective-permute-start.1 = (bf16[512,1024]{1,0:T(8,128)(2,1)}, bf16[512,1024]{1,0:T(8,128)(2,1)S(1)}, u32[]{:S(2)}, u32[]{:S(2)}) collective-permute-start(bf16[512,1024]{1,0:T(8,128)(2,1)} %bitcast.12), channel_id=1, source_target_pairs={{0,2},{2,0},{4,6},{6,4},{8,10},{10,8},{12,14},{14,12},{16,18},{18,... | collective-permute-start | bytes 3145736 | tf_op jit(solution)/shard_map/ppermute | solution.py:17
  1.5 20.9 %collective-permute-start.4 = (bf16[256,1024]{1,0:T(8,128)(2,1)S(1)}, bf16[256,1024]{1,0:T(8,128)(2,1)S(1)}, u32[]{:S(2)}, u32[]{:S(2)}) collective-permute-start(bf16[256,1024]{1,0:T(8,128)(2,1)S(1)} %dynamic-slice_bitcast_fusion.refs_2_), channel_id=1, source_target_pairs={{0,4},{2,6},{4,0},{6,2},{8,12},{10,14},{12,8},{14,10},{16,20},{18,... | collective-permute-start | bytes 1572872 | tf_op jit(solution)/shard_map/ppermute | solution.py:17
  5.0 4.2 %copy-start.3 = (s32[4]{0:T(128)S(1)}, s32[4]{0:T(128)}, u32[]{:S(2)}) copy-start(s32[4]{0:T(128)} %param.7) | copy-start | bytes 52
  5.0 14.9 %collective-permute-start.2 = (bf16[128,1024]{1,0:T(8,128)(2,1)}, bf16[128,1024]{1,0:T(8,128)(2,1)}, u32[]{:S(2)}, u32[]{:S(2)}) collective-permute-start(bf16[128,1024]{1,0:T(8,128)(2,1)} %get-tuple-element.66), channel_id=1, source_target_pairs={{0,8},{2,10},{4,12},{6,14},{8,0},{10,2},{12,4},{14,6},{16,24},{18,... | collective-permute-start | bytes 786440 | tf_op jit(solution)/shard_map/ppermute | solution.py:17
  6.6 15.8 %collective-permute-start.3 = (bf16[128,1024]{1,0:T(8,128)(2,1)}, bf16[128,1024]{1,0:T(8,128)(2,1)}, u32[]{:S(2)}, u32[]{:S(2)}) collective-permute-start(bf16[128,1024]{1,0:T(8,128)(2,1)} %get-tuple-element.66), channel_id=1, source_target_pairs={{0,16},{2,18},{4,20},{6,22},{8,24},{10,26},{12,28},{14,30},{16,0},... | collective-permute-start | bytes 786440 | tf_op jit(solution)/shard_map/ppermute | solution.py:17
  9.2 3.5 %collective-permute-start = (s32[4]{0:T(128)S(1)}, s32[4]{0:T(128)S(1)}, u32[]{:S(2)}, u32[]{:S(2)}) collective-permute-start(s32[4]{0:T(128)S(1)} %copy-done.3), channel_id=1, source_target_pairs={{0,1},{1,0},{2,3},{3,2},{4,5},{5,4},{6,7},{7,6},{8,9},{9,8},{10,11... | collective-permute-start | bytes 56 | tf_op jit(solution)/shard_map/ppermute | solution.py:17
  10.7 20.4 %collective-permute-start.6 = (bf16[128,1024]{1,0:T(8,128)(2,1)}, bf16[128,1024]{1,0:T(8,128)(2,1)S(1)}, u32[]{:S(2)}, u32[]{:S(2)}) collective-permute-start(bf16[128,1024]{1,0:T(8,128)(2,1)} %shard_map.48), channel_id=1, source_target_pairs={{0,8},{2,10},{4,12},{6,14},{8,0},{10,2},{12,4},{14,6},{16,24},{18,... | collective-permute-start | bytes 786440 | tf_op jit(solution)/shard_map/ppermute | solution.py:17
  12.7 19.5 %collective-permute-start.7 = (bf16[128,1024]{1,0:T(8,128)(2,1)}, bf16[128,1024]{1,0:T(8,128)(2,1)}, u32[]{:S(2)}, u32[]{:S(2)}) collective-permute-start(bf16[128,1024]{1,0:T(8,128)(2,1)} %shard_map.48), channel_id=1, source_target_pairs={{0,16},{2,18},{4,20},{6,22},{8,24},{10,26},{12,28},{14,30},{16,0},... | collective-permute-start | bytes 786440 | tf_op jit(solution)/shard_map/ppermute | solution.py:17
  13.1 0.7 copy-start.1
  13.9 0.7 copy-start.2
  23.5 20.0 %collective-permute-start.13 = (bf16[256,1024]{1,0:T(8,128)(2,1)S(1)}, bf16[256,1024]{1,0:T(8,128)(2,1)S(1)}, u32[]{:S(2)}, u32[]{:S(2)}) collective-permute-start(bf16[256,1024]{1,0:T(8,128)(2,1)S(1)} %shard_map.52.refs_2_), channel_id=1, source_target_pairs={{0,4},{2,6},{4,0},{6,2},{8,12},{10,14},{12,8},{14,10},{16,20},{18,... | collective-permute-start | bytes 1572872 | tf_op jit(solution)/shard_map/ppermute | solution.py:17
  24.1 12.8 %collective-permute-start.5 = (bf16[128,1024]{1,0:T(8,128)(2,1)}, bf16[128,1024]{1,0:T(8,128)(2,1)S(1)}, u32[]{:S(2)}, u32[]{:S(2)}) collective-permute-start(bf16[128,1024]{1,0:T(8,128)(2,1)} %get-tuple-element.34.refs_1_), channel_id=1, source_target_pairs={{0,8},{2,10},{4,12},{6,14},{8,0},{10,2},{12,4},{14,6},{16,24},{18,... | collective-permute-start | bytes 786440 | tf_op jit(solution)/shard_map/ppermute | solution.py:17
  32.2 9.5 %collective-permute-start.9 = (bf16[128,1024]{1,0:T(8,128)(2,1)}, bf16[128,1024]{1,0:T(8,128)(2,1)S(1)}, u32[]{:S(2)}, u32[]{:S(2)}) collective-permute-start(bf16[128,1024]{1,0:T(8,128)(2,1)} %get-tuple-element.40.refs_4_), channel_id=1, source_target_pairs={{0,4},{2,6},{4,0},{6,2},{8,12},{10,14},{12,8},{14,10},{16,20},{18,... | collective-permute-start | bytes 786440 | tf_op jit(solution)/shard_map/ppermute | solution.py:17
  32.8 14.2 %collective-permute-start.11 = (bf16[128,1024]{1,0:T(8,128)(2,1)}, bf16[128,1024]{1,0:T(8,128)(2,1)S(1)}, u32[]{:S(2)}, u32[]{:S(2)}) collective-permute-start(bf16[128,1024]{1,0:T(8,128)(2,1)} %get-tuple-element.40.refs_4_), channel_id=1, source_target_pairs={{0,8},{2,10},{4,12},{6,14},{8,0},{10,2},{12,4},{14,6},{16,24},{18,... | collective-permute-start | bytes 786440 | tf_op jit(solution)/shard_map/ppermute | solution.py:17
  34.5 12.8 %collective-permute-start.12 = (bf16[128,1024]{1,0:T(8,128)(2,1)S(1)}, bf16[128,1024]{1,0:T(8,128)(2,1)S(1)}, u32[]{:S(2)}, u32[]{:S(2)}) collective-permute-start(bf16[128,1024]{1,0:T(8,128)(2,1)S(1)} %get-tuple-element.39.refs_1_.refs_3_), channel_id=1, source_target_pairs={{0,4},{2,6},{4,0},{6,2},{8,12},{10,14},{12,8},{14,10},{16,20},{18,... | collective-permute-start | bytes 786440 | tf_op jit(solution)/shard_map/ppermute | solution.py:17
  36.8 14.2 %collective-permute-start.8 = (bf16[128,1024]{1,0:T(8,128)(2,1)S(1)}, bf16[128,1024]{1,0:T(8,128)(2,1)S(1)}, u32[]{:S(2)}, u32[]{:S(2)}) collective-permute-start(bf16[128,1024]{1,0:T(8,128)(2,1)S(1)} %shard_map.51.refs_2_), channel_id=1, source_target_pairs={{0,4},{2,6},{4,0},{6,2},{8,12},{10,14},{12,8},{14,10},{16,20},{18,... | collective-permute-start | bytes 786440 | tf_op jit(solution)/shard_map/ppermute | solution.py:17
  41.7 9.3 %collective-permute-start.10 = (bf16[128,1024]{1,0:T(8,128)(2,1)S(1)}, bf16[128,1024]{1,0:T(8,128)(2,1)S(1)}, u32[]{:S(2)}, u32[]{:S(2)}) collective-permute-start(bf16[128,1024]{1,0:T(8,128)(2,1)S(1)} %shard_map.54.refs_1_.refs_3_), channel_id=1, source_target_pairs={{0,8},{2,10},{4,12},{6,14},{8,0},{10,2},{12,4},{14,6},{16,24},{18,... | collective-permute-start | bytes 786440 | tf_op jit(solution)/shard_map/ppermute | solution.py:17
  52.3 2.7 %collective-permute-start.14 = (f32[512,512]{1,0:T(8,128)S(1)}, f32[512,512]{1,0:T(8,128)S(1)}, u32[]{:S(2)}, u32[]{:S(2)}) collective-permute-start(f32[512,512]{1,0:T(8,128)S(1)} %shard_map.59), channel_id=1, source_target_pairs={{0,2},{2,0},{4,6},{6,4},{8,10},{10,8},{12,14},{14,12},{16,18},{18,... | collective-permute-start | bytes 3145736 | tf_op jit(solution)/shard_map/ppermute | solution.py:17
  55.3 14.0 %collective-permute-start.19 = (bf16[512,512]{1,0:T(8,128)(2,1)S(1)}, bf16[512,512]{1,0:T(8,128)(2,1)S(1)}, u32[]{:S(2)}, u32[]{:S(2)}) collective-permute-start(bf16[512,512]{1,0:T(8,128)(2,1)S(1)} %add_convert_fusion.refs_2_), channel_id=1, source_target_pairs={{0,1},{1,0},{2,3},{3,2},{4,5},{5,4},{6,7},{7,6},{8,9},{9,8},{10,11... | collective-permute-start | bytes 1572872 | tf_op jit(solution)/shard_map/ppermute | solution.py:17
  58.6 1.6 %collective-permute-start.15 = (f32[128,512]{1,0:T(8,128)S(1)}, f32[128,512]{1,0:T(8,128)S(1)}, u32[]{:S(2)}, u32[]{:S(2)}) collective-permute-start(f32[128,512]{1,0:T(8,128)S(1)} %get-tuple-element.61), channel_id=1, source_target_pairs={{0,2},{2,0},{4,6},{6,4},{8,10},{10,8},{12,14},{14,12},{16,18},{18,... | collective-permute-start | bytes 786440 | tf_op jit(solution)/shard_map/ppermute | solution.py:17
  58.7 1.9 %collective-permute-start.16 = (f32[128,512]{1,0:T(8,128)S(1)}, f32[128,512]{1,0:T(8,128)S(1)}, u32[]{:S(2)}, u32[]{:S(2)}) collective-permute-start(f32[128,512]{1,0:T(8,128)S(1)} %get-tuple-element.64), channel_id=1, source_target_pairs={{0,2},{2,0},{4,6},{6,4},{8,10},{10,8},{12,14},{14,12},{16,18},{18,... | collective-permute-start | bytes 786440 | tf_op jit(solution)/shard_map/ppermute | solution.py:17
  59.1 1.8 %collective-permute-start.17 = (f32[128,512]{1,0:T(8,128)S(1)}, f32[128,512]{1,0:T(8,128)S(1)}, u32[]{:S(2)}, u32[]{:S(2)}) collective-permute-start(f32[128,512]{1,0:T(8,128)S(1)} %get-tuple-element.63), channel_id=1, source_target_pairs={{0,2},{2,0},{4,6},{6,4},{8,10},{10,8},{12,14},{14,12},{16,18},{18,... | collective-permute-start | bytes 786440 | tf_op jit(solution)/shard_map/ppermute | solution.py:17
  59.2 2.1 %collective-permute-start.18 = (f32[128,512]{1,0:T(8,128)S(1)}, f32[128,512]{1,0:T(8,128)S(1)}, u32[]{:S(2)}, u32[]{:S(2)}) collective-permute-start(f32[128,512]{1,0:T(8,128)S(1)} %get-tuple-element.62), channel_id=1, source_target_pairs={{0,2},{2,0},{4,6},{6,4},{8,10},{10,8},{12,14},{14,12},{16,18},{18,... | collective-permute-start | bytes 786440 | tf_op jit(solution)/shard_map/ppermute | solution.py:17

commit v4 on v3

--- a/solution.py
+++ b/solution.py
@@ -8,7 +8,6 @@
 from jax.sharding import PartitionSpec as P
 
 CHUNK = 256
-SPLIT = 4
 MIB = 1024 * 1024
 
 
@@ -30,6 +29,33 @@
     )(*blocks, *after)
 
 
+def pieces_kernel(tile, whole, first, second, sems):
+    half = first.shape[0]
+    start = pl.multiple_of(lax.axis_index("rep") * (2 * half), 2 * half)
+    copies = [
+        pltpu.make_async_copy(tile.at[pl.ds(start, half)], first, sems.at[0]),
+        pltpu.make_async_copy(tile.at[pl.ds(start + half, half)], second, sems.at[1]),
+        pltpu.make_async_copy(tile.at[pl.ds(start, 2 * half)], whole, sems.at[2]),
+    ]
+    for copy in copies:
+        copy.start()
+    for copy in copies:
+        copy.wait()
+
+
+def pieces_of(tile, part):
+    columns = tile.shape[1]
+    return pl.pallas_call(
+        pieces_kernel,
+        out_shape=[pltpu.VMEM((n, columns), tile.dtype) for n in (part, part // 2, part // 2)],
+        in_specs=[pl.BlockSpec(memory_space=pl.ANY)],
+        out_specs=[pl.BlockSpec(memory_space=pltpu.VMEM)] * 3,
+        scratch_shapes=[pltpu.SemaphoreType.DMA((3,))],
+        compiler_params=pltpu.CompilerParams(vmem_limit_bytes=8 * MIB),
+        cost_estimate=pl.CostEstimate(flops=0, bytes_accessed=0, transcendentals=0),
+    )(tile)
+
+
 def join_kernel(*refs):
     out, start = refs[-1], 0
     for ref in refs[:-1]:
@@ -51,13 +77,17 @@
 
 
 def absorb_kernel(plan, sizes, place, table, e_occ, e_half, e_col, *refs):
-    left_masks, block_plan, fresh, parts = plan
+    left_masks, block_plan, given, parts, n_addends = plan
     occupied, width = sizes
     n_left, n_block = len(left_masks), len(block_plan)
     n_total = n_left * len(parts)
     lefts, refs = refs[:n_left], refs[n_left:]
     blocks, refs = refs[:n_block], refs[n_block:]
-    olds = None if fresh else refs[:n_total]
+    olds, at_old = [], 0
+    for is_given in given:
+        olds.append(refs[at_old] if is_given else None)
+        at_old += is_given
+    addends = refs[at_old : at_old + n_addends]
     news = refs[-n_total:]
     here, slot = place[0], place[1]
     half = e_half.shape[1]
@@ -93,7 +123,8 @@
                 preferred_element_type=jnp.float32,
             )
             rows = [
-                e_half[pl.ds((slot ^ r) * 2 + h, 1), :] - e_occ[here ^ mask] for mask, r, h in runs
+                e_half[pl.ds(((slot ^ r) if r >= 0 else ~r) * 2 + h, 1), :] - e_occ[here ^ mask]
+                for mask, r, h in runs
             ]
             row = jnp.concatenate(rows, axis=1) if len(rows) > 1 else rows[0]
             amp = (pair / (column + row)).astype(jnp.bfloat16)
@@ -107,7 +138,8 @@
     for (i, at), groups in zip(tasks, ready):
         for j, q in enumerate(parts):
             lanes = pl.ds(pl.multiple_of((slot ^ q) * width, width), width)
-            total = None if fresh else olds[i * len(parts) + j][at : at + CHUNK]
+            n = i * len(parts) + j
+            total = None if olds[n] is None else olds[n][at : at + CHUNK]
             for mask, members in groups.items():
                 amps = [amp for amp, _, _ in members]
                 sides = [block[s : s + half, lanes] for _, block, s in members]
@@ -117,31 +149,39 @@
                     preferred_element_type=jnp.float32,
                 )
                 total = term if total is None else total + term
-            news[i * len(parts) + j][at : at + CHUNK] = total
+            if addends:
+                total = total + addends[n][at : at + CHUNK]
+            news[n][at : at + CHUNK] = total.astype(news[n].dtype)
 
 
 def in_vmem(array):
     return pltpu.with_memory_space_constraint(array, pltpu.VMEM)
 
 
-def absorb(context, width, lefts, blocks, parts, olds, cost):
+def absorb(context, width, lefts, blocks, parts, olds, cost, addends=(), kind=jnp.float32):
     virtuals, aux = lefts[0][0].shape
     keys = [(mask, q) for _, mask in lefts for q in parts]
-    fresh = keys[0] not in olds
-    plan = (tuple(m for _, m in lefts), tuple(tuple(r) for _, r in blocks), fresh, tuple(parts))
+    given = tuple(key in olds for key in keys)
+    plan = (
+        tuple(m for _, m in lefts), tuple(tuple(r) for _, r in blocks), given, tuple(parts), len(addends)
+    )
     sizes = (context[2].shape[0], width)
     arrays = [in_vmem(a) for a, _ in lefts] + [in_vmem(b) for b, _ in blocks]
     base = len(context) + len(arrays)
-    arrays += [] if fresh else [in_vmem(olds[key]) for key in keys]
+    arrays += [in_vmem(olds[key]) for key in keys if key in olds] + [in_vmem(a) for a in addends]
+    aliases = {}
+    for i, is_given in enumerate(given):
+        if is_given and kind == jnp.float32:
+            aliases[base + sum(given[:i])] = i
     scalar = pl.BlockSpec(memory_space=pltpu.SMEM)
     whole = pl.BlockSpec(memory_space=pltpu.VMEM)
     depth = sum(b.shape[0] for b, _ in blocks)
     news = pl.pallas_call(
         functools.partial(absorb_kernel, plan, sizes),
-        out_shape=[pltpu.VMEM((virtuals, width), jnp.float32) for _ in keys],
+        out_shape=[pltpu.VMEM((virtuals, width), kind) for _ in keys],
         in_specs=[scalar] * 3 + [whole] * (len(context) - 3 + len(arrays)),
         out_specs=[whole] * len(keys),
-        input_output_aliases={} if fresh else {base + i: i for i in range(len(keys))},
+        input_output_aliases=aliases,
         compiler_params=pltpu.CompilerParams(vmem_limit_bytes=24 * MIB),
         cost_estimate=pl.CostEstimate(
             flops=cost * 2 * len(lefts) * virtuals * depth * (aux + width * len(parts)),
@@ -168,16 +208,17 @@
     every = list(range(reps))
     rest = every[1:]
 
-    mine = lax.dynamic_slice_in_dim(tile, slot * part, part, axis=0)
-    line = {(0, 0): mine[:half], (0, 1): mine[half:]}
+    mine, *halves = pieces_of(tile, part)
+    line = {(0, h): halves[h] for h in range(2)}
     side = {}
+    twin = exchange(tile, "blk", 1)
+    (mine,) = gate([mine], [twin])
     beside = exchange(mine, "blk", 2)
     table = offsets
     bit = 1
     while bit < reps:
         table = jnp.concatenate([table, exchange(table, "rep", bit)])
         bit *= 2
-    twin = exchange(tile, "blk", 1)
     own, other = (tile, 0), (twin, 1)
     context = [
         jnp.stack([here, slot]).astype(jnp.int32),
@@ -187,8 +228,8 @@
         jnp.broadcast_to(eps_vir[:, None], (virtuals, 128)),
     ]
 
-    def add(blocks, totals, parts=every, lefts=(own, other), cost=0):
-        return absorb(context, width, lefts, blocks, parts, totals, cost)
+    def add(blocks, totals, parts=every, lefts=(own, other), **options):
+        return absorb(context, width, lefts, blocks, parts, totals, options.pop('cost', 0), **options)
 
     def travel(members, h, after):
         for m in members:
@@ -204,49 +245,50 @@
         return (side[m, h], [(4 * m + 2, 0, h)])
 
     levels = [[m for m in range(1, lines) if m.bit_count() == n] for n in range(1, lines.bit_length())]
-    singles, final = levels[0], lines - 1
+    singles, final = levels[0][::-1], lines - 1
     others = [m for level in levels[1:] for m in level]
     by = final & -final
-    totals = add([(mine, [(0, 0, 0), (0, 0, 1)])], {})
-    travel(singles, 0, [beside, totals[0, 0]])
-    group = join([line[m, 0] for m in singles])
-    group_side = exchange(group, "blk", 2)
+    totals = add([(tile, [(0, ~r, h) for r in every for h in range(2)])], {}, [0], cost=1)
+    travel(singles, 0, [totals[0, 0]])
+    for m in singles:
+        side[m, 0] = exchange(line[m, 0], "blk", 2)
     (line[0, 1],) = gate([line[0, 1]], [twin])
-    totals = add([(beside, [(2, 0, 0), (2, 0, 1)])], totals)
+    totals = add([(beside, [(2, 0, 0), (2, 0, 1)])], totals, cost=1)
     travel(singles, 1, [totals[0, 0]])
-    for m in singles[::-1]:
+    for m in singles:
         side[m, 1] = exchange(line[m, 1], "blk", 2)
-    blocks = [(group, [(4 * m, 0, 0) for m in singles])] + [lines_of(m, 1) for m in singles]
+    blocks = [lines_of(m, h) for m in singles for h in range(2)]
+    blocks += [sides_of(m, 0) for m in singles]
+    totals = add(blocks, totals, cost=1)
     late = []
     for m in others:
-        travel([m], 0, [line[singles[0], 1]])
+        travel([m], 0, [totals[0, 0]])
         side[m, 0] = exchange(line[m, 0], "blk", 2)
         late.append(lines_of(m, 0))
         if m != final:
             travel([m], 1, [])
             side[m, 1] = exchange(line[m, 1], "blk", 2)
             late.append(lines_of(m, 1))
-    totals = add(blocks, totals)
     line[final, 1] = exchange(line[final ^ by, 1], "blk", 4 * by)
     (passed,) = gate([side[final ^ by, 1]], [totals[0, 0]])
     side[final ^ by, 1] = passed
     side[final, 1] = exchange(passed, "blk", 4 * by)
-    (group_side,) = gate([group_side], [passed])
-    totals = add(late + [(group_side, [(4 * m + 2, 0, 0) for m in singles])], totals)
-    blocks = [lines_of(final, 1)] + [sides_of(m, 1) for m in singles[::-1]]
+    (line[final, 1],) = gate([line[final, 1]], [passed])
+    blocks = late + [lines_of(final, 1)] + [sides_of(m, 1) for m in singles]
     totals = add(blocks, totals)
     blocks = [sides_of(m, h) for m, h in side if m not in singles]
-
     came = []
     if rest:
-        theirs = add(blocks, totals, rest, [other])
+        theirs = add(blocks, totals, rest, [other], kind=jnp.bfloat16)
         ours = add(blocks, totals, rest, [own])
-        sent = [(ours[0, q] + across(theirs[1, q], 1)).astype(jnp.bfloat16) for q in rest]
-        came = [exchange(s, "rep", q) for s, q in zip(sent, rest)]
-        held = gate([block for block, _ in blocks], sent)
+        for q in rest:
+            sent = ours[0, q] + exchange(theirs[1, q], "blk", 1).astype(jnp.float32)
+            sent = sent.astype(jnp.bfloat16)
+            came.append(exchange(sent, "rep", q))
+        held = gate([block for block, _ in blocks], [sent])
         blocks = [(block, runs) for block, (_, runs) in zip(held, blocks)]
-    totals = add(blocks, totals, [0], cost=0)
-    gamma = totals[0, 0] + across(totals[1, 0], SPLIT)
+    totals = add(blocks, totals, [0])
+    gamma = totals[0, 0] + across(totals[1, 0], 4)
     for c in came:
         gamma = gamma + c.astype(jnp.float32)
     return gamma[None]

time: 70.8 us -> 69 us (0.975)
  waiting for transfers between devices: 26.6 us -> 30.1 us
  Pallas kernels: 20 us -> 16.9 us
  local copies, waits for them, and re-layouts: 3.29 us -> 2.15 us
  starting transfers between devices: 18.9 us -> 18 us
    ppermute x20 -> x21, waiting for transfers between devices: 26.6 us -> 30.1 us  [exchange(): return lax.ppermute(block, axis, [(i, i ^ mask) for i in devices])]
    pallas_call x8 -> x7, Pallas kernels: 18.9 us -> 16.8 us  [absorb(): pl.pallas_call(functools.partial(absorb_kernel, plan, sizes), out_shape=[...]
    dynamic_slice x1 -> x0, local copies, waits for them, and re-layouts: 1.08 us -> none  [per_device(): mine = lax.dynamic_slice_in_dim(tile, slot * part, part, axis=0)]
    pallas_call x1, Pallas kernels: 1.06 us -> 0.1 us  [pieces_of(): pl.pallas_call(pieces_kernel, out_shape=[pltpu.VMEM((n, columns), tile.dt...]
    ppermute x20 -> x21, starting transfers between devices: 18.9 us -> 18 us  [exchange(): return lax.ppermute(block, axis, [(i, i ^ mask) for i in devices])]
    slice x1 -> x0, local copies, waits for them, and re-layouts: 0.83 us -> none  [per_device(): line = {(0, 0): mine[:half], (0, 1): mine[half:]}]
    unnamed x8 -> x10, local copies, waits for them, and re-layouts: 1.19 us -> 1.96 us
  transfers between devices with their start and end apart: 20 -> 21, of which waited for: 14 -> 15; matrix products, arithmetic and copies ran while one was open for 3% -> 0% of each run, Pallas kernels for 27% -> 23%
where the time goes in v4:
time: 69 us; the launch traced here: 68.8 us
  waiting for transfers between devices  30.1 us (44%)
  starting transfers between devices  18 us (26%)
  Pallas kernels  16.9 us (24%)
  local copies, waits for them, and re-layouts  2.15 us (3%)
  other arithmetic  1.55 us (2%)
    ppermute x21, waiting for transfers between devices, exchange(): return lax.ppermute(block, axis, [(i, i ^ mask) for i in devices])  30.1 us
    ppermute x21, starting transfers between devices, exchange(): return lax.ppermute(block, axis, [(i, i ^ mask) for i in devices])  18 us
    pallas_call x7, Pallas kernels, absorb(): pl.pallas_call(functools.partial(absorb_kernel, plan, sizes), out_shape=[...  16.8 us
    unnamed x10, local copies, waits for them, and re-layouts  1.96 us
  transfers between devices with their start and end apart: 21, of which 15 were waited for; matrix products, arithmetic and copies ran while one was open for 0% of the time, Pallas kernels for 23%

profile of v4, /device:TPU:0, one launch (start us, length us, event | category | flops | bytes accessed | tf_op | source)
XLA Modules:
  0.0 68.8 jit_solution(13530120889572637203)
XLA Ops:
  0.5 1.2 %copy-done = bf16[1,512,1024]{2,1,0:T(8,128)(2,1)S(1)} copy-done((bf16[1,512,1024]{2,1,0:T(8,128)(2,1)S(1)}, bf16[1,512,1024]{2,1,0:T(8,128)(2,1)}, u32[]{:S(2)}) %copy-start) | copy-done | bytes 1048600
  1.8 3.7 %collective-permute-start.2 = (bf16[128,1024]{1,0:T(8,128)(2,1)S(1)}, bf16[128,1024]{1,0:T(8,128)(2,1)S(1)}, u32[]{:S(2)}, u32[]{:S(2)}) collective-permute-start(bf16[128,1024]{1,0:T(8,128)(2,1)S(1)} %get-tuple-element.30), channel_id=1, source_target_pairs={{0,16},{2,18},{4,20},{6,22},{8,24},{10,26},{12,28},{14,30},{16,0},... | collective-permute-start | bytes 786440 | tf_op jit(solution)/shard_map/ppermute | solution.py:16
  5.5 1.6 %collective-permute-start.3 = (bf16[128,1024]{1,0:T(8,128)(2,1)S(1)}, bf16[128,1024]{1,0:T(8,128)(2,1)S(1)}, u32[]{:S(2)}, u32[]{:S(2)}) collective-permute-start(bf16[128,1024]{1,0:T(8,128)(2,1)S(1)} %get-tuple-element.30), channel_id=1, source_target_pairs={{0,8},{2,10},{4,12},{6,14},{8,0},{10,2},{12,4},{14,6},{16,24},{18,... | collective-permute-start | bytes 786440 | tf_op jit(solution)/shard_map/ppermute | solution.py:16
  7.0 1.5 %collective-permute-start = (s32[4]{0:T(128)S(1)}, s32[4]{0:T(128)S(1)}, u32[]{:S(2)}, u32[]{:S(2)}) collective-permute-start(s32[4]{0:T(128)S(1)} %copy-done.4), channel_id=1, source_target_pairs={{0,1},{1,0},{2,3},{3,2},{4,5},{5,4},{6,7},{7,6},{8,9},{9,8},{10,11... | collective-permute-start | bytes 56 | tf_op jit(solution)/shard_map/ppermute | solution.py:16
  8.6 1.5 %collective-permute-start.7 = (bf16[256,1024]{1,0:T(8,128)(2,1)S(1)}, bf16[256,1024]{1,0:T(8,128)(2,1)S(1)}, u32[]{:S(2)}, u32[]{:S(2)}) collective-permute-start(bf16[256,1024]{1,0:T(8,128)(2,1)S(1)} %shard_map.50), channel_id=1, source_target_pairs={{0,4},{2,6},{4,0},{6,2},{8,12},{10,14},{12,8},{14,10},{16,20},{18,... | collective-permute-start | bytes 1572872 | tf_op jit(solution)/shard_map/ppermute | solution.py:16
  11.5 0.6 copy-done.3
  12.1 2.4 %shard_map.47 = (f32[512,512]{1,0:T(8,128)S(1)}, f32[512,512]{1,0:T(8,128)S(1)}) custom-call(s32[2]{0:T(128)S(1)} %pad_add_fusion.place, s32[8]{0:T(128)S(1)} %pad_add_fusion.1.table, f32[16]{0:T(128)S(1)} %copy-done.3, f32[4,128]{1,0:T(4,128)S(1)} %bitcast.15, f32[512,128]{1,0:T(8,128)S(1)} %broadcast_in_dim.4.e_col, bf16[512,1024]{1,0:T(8,128)(2,1)S(1)} %bitcast.8, ...), custom_call_target="tpu_custom_call" | custom-call | flops 1610612736 | tf_op jit(solution)/shard_map/pallas_call | solution.py:179
  14.5 3.8 %collective-permute-done.2.refs_0_ = bf16[128,1024]{1,0:T(8,128)(2,1)S(1)} collective-permute-done((bf16[128,1024]{1,0:T(8,128)(2,1)S(1)}, bf16[128,1024]{1,0:T(8,128)(2,1)S(1)}, u32[]{:S(2)}, u32[]{:S(2)}) %collective-permute-start.2) | collective-permute-done | bytes 262176 | tf_op jit(solution)/shard_map/ppermute | solution.py:16
  18.3 1.9 %collective-permute-done.3.refs_1_ = bf16[128,1024]{1,0:T(8,128)(2,1)S(1)} collective-permute-done((bf16[128,1024]{1,0:T(8,128)(2,1)S(1)}, bf16[128,1024]{1,0:T(8,128)(2,1)S(1)}, u32[]{:S(2)}, u32[]{:S(2)}) %collective-permute-start.3) | collective-permute-done | bytes 262176 | tf_op jit(solution)/shard_map/ppermute | solution.py:16
  20.2 1.5 %collective-permute-start.8 = (bf16[128,1024]{1,0:T(8,128)(2,1)S(1)}, bf16[128,1024]{1,0:T(8,128)(2,1)S(1)}, u32[]{:S(2)}, u32[]{:S(2)}) collective-permute-start(bf16[128,1024]{1,0:T(8,128)(2,1)S(1)} %get-tuple-element.32.refs_2_), channel_id=1, source_target_pairs={{0,4},{2,6},{4,0},{6,2},{8,12},{10,14},{12,8},{14,10},{16,20},{18,... | collective-permute-start | bytes 786440 | tf_op jit(solution)/shard_map/ppermute | solution.py:16
  21.7 0.5 collective-permute-start.9
  22.2 1.2 %collective-permute-done.7.refs_2_ = bf16[256,1024]{1,0:T(8,128)(2,1)S(1)} collective-permute-done((bf16[256,1024]{1,0:T(8,128)(2,1)S(1)}, bf16[256,1024]{1,0:T(8,128)(2,1)S(1)}, u32[]{:S(2)}, u32[]{:S(2)}) %collective-permute-start.7) | collective-permute-done | bytes 524320 | tf_op jit(solution)/shard_map/ppermute | solution.py:16
  23.4 1.9 %shard_map.51 = (f32[512,512]{1,0:T(8,128)S(1)}, f32[512,512]{1,0:T(8,128)S(1)}, f32[512,512]{1,0:T(8,128)S(1)}, f32[512,512]{1,0:T(8,128)S(1)}) custom-call(s32[2]{0:T(128)S(1)} %pad_add_fusion.place, s32[8]{0:T(128)S(1)} %pad_add_fusion.1.table, f32[16]{0:T(128)S(1)} %copy-done.3, ...), custom_call_target="tpu_custom_call", output_to_operand_aliasing={{0}: (8, {}), {2}: (9, {})} | custom-call | flops 1073741824 | tf_op jit(solution)/shard_map/pallas_call | solution.py:179
  25.3 4.1 %collective-permute-done.5.refs_0_ = bf16[128,1024]{1,0:T(8,128)(2,1)S(1)} collective-permute-done((bf16[128,1024]{1,0:T(8,128)(2,1)S(1)}, bf16[128,1024]{1,0:T(8,128)(2,1)S(1)}, u32[]{:S(2)}, u32[]{:S(2)}) %collective-permute-start.5) | collective-permute-done | bytes 262176 | tf_op jit(solution)/shard_map/ppermute | solution.py:16
  29.4 0.8 %collective-permute-done.6.refs_1_ = bf16[128,1024]{1,0:T(8,128)(2,1)S(1)} collective-permute-done((bf16[128,1024]{1,0:T(8,128)(2,1)S(1)}, bf16[128,1024]{1,0:T(8,128)(2,1)S(1)}, u32[]{:S(2)}, u32[]{:S(2)}) %collective-permute-start.6) | collective-permute-done | bytes 262176 | tf_op jit(solution)/shard_map/ppermute | solution.py:16
  30.3 1.5 %collective-permute-start.11 = (bf16[128,1024]{1,0:T(8,128)(2,1)S(1)}, bf16[128,1024]{1,0:T(8,128)(2,1)S(1)}, u32[]{:S(2)}, u32[]{:S(2)}) collective-permute-start(bf16[128,1024]{1,0:T(8,128)(2,1)S(1)} %get-tuple-element.37.refs_3_), channel_id=1, source_target_pairs={{0,4},{2,6},{4,0},{6,2},{8,12},{10,14},{12,8},{14,10},{16,20},{18,... | collective-permute-start | bytes 786440 | tf_op jit(solution)/shard_map/ppermute | solution.py:16
  31.8 1.2 %collective-permute-start.13 = (bf16[128,1024]{1,0:T(8,128)(2,1)S(1)}, bf16[128,1024]{1,0:T(8,128)(2,1)S(1)}, u32[]{:S(2)}, u32[]{:S(2)}) collective-permute-start(bf16[128,1024]{1,0:T(8,128)(2,1)S(1)} %get-tuple-element.37.refs_3_), channel_id=1, source_target_pairs={{0,8},{2,10},{4,12},{6,14},{8,0},{10,2},{12,4},{14,6},{16,24},{18,... | collective-permute-start | bytes 786440 | tf_op jit(solution)/shard_map/ppermute | solution.py:16
  33.0 0.5 collective-permute-start.14
  33.5 1.1 %collective-permute-done.9.refs_7_ = bf16[128,1024]{1,0:T(8,128)(2,1)S(1)} collective-permute-done((bf16[128,1024]{1,0:T(8,128)(2,1)S(1)}, bf16[128,1024]{1,0:T(8,128)(2,1)S(1)}, u32[]{:S(2)}, u32[]{:S(2)}) %collective-permute-start.9) | collective-permute-done | bytes 262176 | tf_op jit(solution)/shard_map/ppermute | solution.py:16
  34.6 4.8 %shard_map.53 = (f32[512,512]{1,0:T(8,128)S(1)}, f32[512,512]{1,0:T(8,128)S(1)}, f32[512,512]{1,0:T(8,128)S(1)}, f32[512,512]{1,0:T(8,128)S(1)}) custom-call(s32[2]{0:T(128)S(1)} %pad_add_fusion.place, s32[8]{0:T(128)S(1)} %pad_add_fusion.1.table, f32[16]{0:T(128)S(1)} %copy-done.3, ...), custom_call_target="tpu_custom_call", output_to_operand_aliasing={{0}: (13, {}), {1}: (14, {}), {2}: (15, {}), {3}: (16, {})} | custom-call | flops 3221225472 | tf_op jit(solution)/shard_map/pallas_call | solution.py:179
  39.4 1.7 %collective-permute-start.10 = (bf16[128,1024]{1,0:T(8,128)(2,1)S(1)}, bf16[128,1024]{1,0:T(8,128)(2,1)S(1)}, u32[]{:S(2)}, u32[]{:S(2)}) collective-permute-start(bf16[128,1024]{1,0:T(8,128)(2,1)S(1)} %shard_map.54.refs_2_), channel_id=1, source_target_pairs={{0,4},{2,6},{4,0},{6,2},{8,12},{10,14},{12,8},{14,10},{16,20},{18,... | collective-permute-start | bytes 786440 | tf_op jit(solution)/shard_map/ppermute | solution.py:16
  41.1 4.7 %collective-permute-done.14.refs_5_ = bf16[128,1024]{1,0:T(8,128)(2,1)S(1)} collective-permute-done((bf16[128,1024]{1,0:T(8,128)(2,1)S(1)}, bf16[128,1024]{1,0:T(8,128)(2,1)S(1)}, u32[]{:S(2)}, u32[]{:S(2)}) %collective-permute-start.14) | collective-permute-done | bytes 262176 | tf_op jit(solution)/shard_map/ppermute | solution.py:16
  45.8 3.5 %shard_map.57 = (f32[512,512]{1,0:T(8,128)S(1)}, f32[512,512]{1,0:T(8,128)S(1)}, f32[512,512]{1,0:T(8,128)S(1)}, f32[512,512]{1,0:T(8,128)S(1)}) custom-call(s32[2]{0:T(128)S(1)} %pad_add_fusion.place, s32[8]{0:T(128)S(1)} %pad_add_fusion.1.table, f32[16]{0:T(128)S(1)} %copy-done.3, ...), custom_call_target="tpu_custom_call", output_to_operand_aliasing={{0}: (11, {}), {1}: (12, {}), {2}: (13, {}), {3}: (14, {})} | custom-call | tf_op jit(solution)/shard_map/pallas_call | solution.py:179
  49.4 0.7 %collective-permute-done.10.refs_1_.refs_0_ = bf16[128,1024]{1,0:T(8,128)(2,1)S(1)} collective-permute-done((bf16[128,1024]{1,0:T(8,128)(2,1)S(1)}, bf16[128,1024]{1,0:T(8,128)(2,1)S(1)}, u32[]{:S(2)}, u32[]{:S(2)}) %collective-permute-start.10) | collective-permute-done | bytes 262176 | tf_op jit(solution)/shard_map/ppermute | solution.py:16
  50.1 1.2 %shard_map.59 = bf16[512,512]{1,0:T(8,128)(2,1)S(1)} custom-call(s32[2]{0:T(128)S(1)} %pad_add_fusion.place, s32[8]{0:T(128)S(1)} %pad_add_fusion.1.table, f32[16]{0:T(128)S(1)} %copy-done.3, f32[4,128]{1,0:T(4,128)S(1)} %bitcast.19, f32[512,128]{1,0:T(8,128)S(1)} %broadcast_in_dim.4.e_col, bf16[512,1024]{1,0:T(8,128)(2,1)S(1)} %collective-permute-done.1.refs_1_.refs_0_, ...), custom_call_target="tpu_custom_call" | custom-call | tf_op jit(solution)/shard_map/pallas_call | solution.py:179
  51.5 1.3 %shard_map.58 = f32[512,512]{1,0:T(8,128)S(1)} custom-call(s32[2]{0:T(128)S(1)} %pad_add_fusion.place, s32[8]{0:T(128)S(1)} %pad_add_fusion.1.table, f32[16]{0:T(128)S(1)} %copy-done.3, f32[4,128]{1,0:T(4,128)S(1)} %bitcast.20, f32[512,128]{1,0:T(8,128)S(1)} %broadcast_in_dim.4.e_col, ...), custom_call_target="tpu_custom_call", output_to_operand_aliasing={{}: (8, {})} | custom-call | tf_op jit(solution)/shard_map/pallas_call | solution.py:179
  52.8 0.6 collective-permute-done.15
  53.5 0.6 collective-permute-start.20
  54.1 1.6 %shard_map.61 = (f32[512,512]{1,0:T(8,128)S(1)}, f32[512,512]{1,0:T(8,128)S(1)}) custom-call(s32[2]{0:T(128)S(1)} %pad_add_fusion.place, s32[8]{0:T(128)S(1)} %pad_add_fusion.1.table, f32[16]{0:T(128)S(1)} %copy-done.3, f32[4,128]{1,0:T(4,128)S(1)} %bitcast.21, f32[512,128]{1,0:T(8,128)S(1)} %broadcast_in_dim.4.e_col, ...), custom_call_target="tpu_custom_call", output_to_operand_aliasing={{0}: (9, {}), {1}: (10, {})} | custom-call | tf_op jit(solution)/shard_map/pallas_call | solution.py:179
  56.9 0.5 collective-permute-done.16
  58.6 9.0 %collective-permute-done.20 = bf16[512,512]{1,0:T(8,128)(2,1)S(1)} collective-permute-done((bf16[512,512]{1,0:T(8,128)(2,1)S(1)}, bf16[512,512]{1,0:T(8,128)(2,1)S(1)}, u32[]{:S(2)}, u32[]{:S(2)}) %collective-permute-start.20) | collective-permute-done | bytes 524320 | tf_op jit(solution)/shard_map/ppermute | solution.py:16
  67.6 1.2 %fusion.1 = f32[1,512,512]{2,1,0:T(8,128)} fusion(f32[512,512]{1,0:T(8,128)S(1)} %get-tuple-element.53, f32[128,512]{1,0:T(8,128)S(1)} %collective-permute-done.19, f32[128,512]{1,0:T(8,128)S(1)} %collective-permute-done.18, f32[128,512]{1,0:T(8,128)S(1)} %collective-permute-done.17, f32[128,512]{1,0:T(8,128)S(1)} %collective-permute-done.16, ...), kind=kLoop, calls=%fused_computation.2 | loop fusion | flops 1572864 | bytes 3670016 | tf_op jit(solution)/shard_map/broadcast_in_dim | solution.py:294
  (42 shorter events, 4.5 us)
Async XLA Ops:
  0.0 8.6 %collective-permute-start.1 = (bf16[512,1024]{1,0:T(8,128)(2,1)}, bf16[512,1024]{1,0:T(8,128)(2,1)S(1)}, u32[]{:S(2)}, u32[]{:S(2)}) collective-permute-start(bf16[512,1024]{1,0:T(8,128)(2,1)} %bitcast.6), channel_id=1, source_target_pairs={{0,2},{2,0},{4,6},{6,4},{8,10},{10,8},{12,14},{14,12},{16,18},{18,... | collective-permute-start | bytes 3145736 | tf_op jit(solution)/shard_map/ppermute | solution.py:16
  0.5 1.2 %copy-start = (bf16[1,512,1024]{2,1,0:T(8,128)(2,1)S(1)}, bf16[1,512,1024]{2,1,0:T(8,128)(2,1)}, u32[]{:S(2)}) copy-start(bf16[1,512,1024]{2,1,0:T(8,128)(2,1)} %param.4) | copy-start | bytes 3145732
  1.8 5.2 %copy-start.4 = (s32[4]{0:T(128)S(1)}, s32[4]{0:T(128)}, u32[]{:S(2)}) copy-start(s32[4]{0:T(128)} %param.7) | copy-start | bytes 52
  1.8 16.5 %collective-permute-start.2 = (bf16[128,1024]{1,0:T(8,128)(2,1)S(1)}, bf16[128,1024]{1,0:T(8,128)(2,1)S(1)}, u32[]{:S(2)}, u32[]{:S(2)}) collective-permute-start(bf16[128,1024]{1,0:T(8,128)(2,1)S(1)} %get-tuple-element.30), channel_id=1, source_target_pairs={{0,16},{2,18},{4,20},{6,22},{8,24},{10,26},{12,28},{14,30},{16,0},... | collective-permute-start | bytes 786440 | tf_op jit(solution)/shard_map/ppermute | solution.py:16
  5.5 14.8 %collective-permute-start.3 = (bf16[128,1024]{1,0:T(8,128)(2,1)S(1)}, bf16[128,1024]{1,0:T(8,128)(2,1)S(1)}, u32[]{:S(2)}, u32[]{:S(2)}) collective-permute-start(bf16[128,1024]{1,0:T(8,128)(2,1)S(1)} %get-tuple-element.30), channel_id=1, source_target_pairs={{0,8},{2,10},{4,12},{6,14},{8,0},{10,2},{12,4},{14,6},{16,24},{18,... | collective-permute-start | bytes 786440 | tf_op jit(solution)/shard_map/ppermute | solution.py:16
  7.0 3.5 %collective-permute-start = (s32[4]{0:T(128)S(1)}, s32[4]{0:T(128)S(1)}, u32[]{:S(2)}, u32[]{:S(2)}) collective-permute-start(s32[4]{0:T(128)S(1)} %copy-done.4), channel_id=1, source_target_pairs={{0,1},{1,0},{2,3},{3,2},{4,5},{5,4},{6,7},{7,6},{8,9},{9,8},{10,11... | collective-permute-start | bytes 56 | tf_op jit(solution)/shard_map/ppermute | solution.py:16
  8.6 2.9 %copy-start.1 = (bf16[1,512,1024]{2,1,0:T(8,128)(2,1)S(1)}, bf16[1,512,1024]{2,1,0:T(8,128)(2,1)}, u32[]{:S(2)}) copy-start(bf16[1,512,1024]{2,1,0:T(8,128)(2,1)} %param.4) | copy-start | bytes 3145732
  8.6 14.8 %collective-permute-start.7 = (bf16[256,1024]{1,0:T(8,128)(2,1)S(1)}, bf16[256,1024]{1,0:T(8,128)(2,1)S(1)}, u32[]{:S(2)}, u32[]{:S(2)}) collective-permute-start(bf16[256,1024]{1,0:T(8,128)(2,1)S(1)} %shard_map.50), channel_id=1, source_target_pairs={{0,4},{2,6},{4,0},{6,2},{8,12},{10,14},{12,8},{14,10},{16,20},{18,... | collective-permute-start | bytes 1572872 | tf_op jit(solution)/shard_map/ppermute | solution.py:16
  10.7 0.7 copy-start.2
  10.7 18.8 %collective-permute-start.5 = (bf16[128,1024]{1,0:T(8,128)(2,1)S(1)}, bf16[128,1024]{1,0:T(8,128)(2,1)S(1)}, u32[]{:S(2)}, u32[]{:S(2)}) collective-permute-start(bf16[128,1024]{1,0:T(8,128)(2,1)S(1)} %shard_map.49), channel_id=1, source_target_pairs={{0,16},{2,18},{4,20},{6,22},{8,24},{10,26},{12,28},{14,30},{16,0},... | collective-permute-start | bytes 786440 | tf_op jit(solution)/shard_map/ppermute | solution.py:16
  11.0 19.3 %collective-permute-start.6 = (bf16[128,1024]{1,0:T(8,128)(2,1)S(1)}, bf16[128,1024]{1,0:T(8,128)(2,1)S(1)}, u32[]{:S(2)}, u32[]{:S(2)}) collective-permute-start(bf16[128,1024]{1,0:T(8,128)(2,1)S(1)} %shard_map.49), channel_id=1, source_target_pairs={{0,8},{2,10},{4,12},{6,14},{8,0},{10,2},{12,4},{14,6},{16,24},{18,... | collective-permute-start | bytes 786440 | tf_op jit(solution)/shard_map/ppermute | solution.py:16
  11.5 0.7 copy-start.3
  20.2 12.8 %collective-permute-start.8 = (bf16[128,1024]{1,0:T(8,128)(2,1)S(1)}, bf16[128,1024]{1,0:T(8,128)(2,1)S(1)}, u32[]{:S(2)}, u32[]{:S(2)}) collective-permute-start(bf16[128,1024]{1,0:T(8,128)(2,1)S(1)} %get-tuple-element.32.refs_2_), channel_id=1, source_target_pairs={{0,4},{2,6},{4,0},{6,2},{8,12},{10,14},{12,8},{14,10},{16,20},{18,... | collective-permute-start | bytes 786440 | tf_op jit(solution)/shard_map/ppermute | solution.py:16
  21.7 12.9 %collective-permute-start.9 = (bf16[128,1024]{1,0:T(8,128)(2,1)S(1)}, bf16[128,1024]{1,0:T(8,128)(2,1)S(1)}, u32[]{:S(2)}, u32[]{:S(2)}) collective-permute-start(bf16[128,1024]{1,0:T(8,128)(2,1)S(1)} %get-tuple-element.38.refs_4_), channel_id=1, source_target_pairs={{0,4},{2,6},{4,0},{6,2},{8,12},{10,14},{12,8},{14,10},{16,20},{18,... | collective-permute-start | bytes 786440 | tf_op jit(solution)/shard_map/ppermute | solution.py:16
  23.4 16.0 %collective-permute-start.4 = (bf16[128,1024]{1,0:T(8,128)(2,1)S(1)}, bf16[128,1024]{1,0:T(8,128)(2,1)S(1)}, u32[]{:S(2)}, u32[]{:S(2)}) collective-permute-start(bf16[128,1024]{1,0:T(8,128)(2,1)S(1)} %get-tuple-element.32.refs_2_), channel_id=1, source_target_pairs={{0,8},{2,10},{4,12},{6,14},{8,0},{10,2},{12,4},{14,6},{16,24},{18,... | collective-permute-start | bytes 786440 | tf_op jit(solution)/shard_map/ppermute | solution.py:16
  30.3 10.8 %collective-permute-start.11 = (bf16[128,1024]{1,0:T(8,128)(2,1)S(1)}, bf16[128,1024]{1,0:T(8,128)(2,1)S(1)}, u32[]{:S(2)}, u32[]{:S(2)}) collective-permute-start(bf16[128,1024]{1,0:T(8,128)(2,1)S(1)} %get-tuple-element.37.refs_3_), channel_id=1, source_target_pairs={{0,4},{2,6},{4,0},{6,2},{8,12},{10,14},{12,8},{14,10},{16,20},{18,... | collective-permute-start | bytes 786440 | tf_op jit(solution)/shard_map/ppermute | solution.py:16
  31.8 9.3 %collective-permute-start.13 = (bf16[128,1024]{1,0:T(8,128)(2,1)S(1)}, bf16[128,1024]{1,0:T(8,128)(2,1)S(1)}, u32[]{:S(2)}, u32[]{:S(2)}) collective-permute-start(bf16[128,1024]{1,0:T(8,128)(2,1)S(1)} %get-tuple-element.37.refs_3_), channel_id=1, source_target_pairs={{0,8},{2,10},{4,12},{6,14},{8,0},{10,2},{12,4},{14,6},{16,24},{18,... | collective-permute-start | bytes 786440 | tf_op jit(solution)/shard_map/ppermute | solution.py:16
  33.0 12.9 %collective-permute-start.14 = (bf16[128,1024]{1,0:T(8,128)(2,1)S(1)}, bf16[128,1024]{1,0:T(8,128)(2,1)S(1)}, u32[]{:S(2)}, u32[]{:S(2)}) collective-permute-start(bf16[128,1024]{1,0:T(8,128)(2,1)S(1)} %get-tuple-element.39.refs_5_), channel_id=1, source_target_pairs={{0,4},{2,6},{4,0},{6,2},{8,12},{10,14},{12,8},{14,10},{16,20},{18,... | collective-permute-start | bytes 786440 | tf_op jit(solution)/shard_map/ppermute | solution.py:16
  39.4 10.7 %collective-permute-start.10 = (bf16[128,1024]{1,0:T(8,128)(2,1)S(1)}, bf16[128,1024]{1,0:T(8,128)(2,1)S(1)}, u32[]{:S(2)}, u32[]{:S(2)}) collective-permute-start(bf16[128,1024]{1,0:T(8,128)(2,1)S(1)} %shard_map.54.refs_2_), channel_id=1, source_target_pairs={{0,4},{2,6},{4,0},{6,2},{8,12},{10,14},{12,8},{14,10},{16,20},{18,... | collective-permute-start | bytes 786440 | tf_op jit(solution)/shard_map/ppermute | solution.py:16
  41.1 9.0 %collective-permute-start.12 = (bf16[128,1024]{1,0:T(8,128)(2,1)S(1)}, bf16[128,1024]{1,0:T(8,128)(2,1)S(1)}, u32[]{:S(2)}, u32[]{:S(2)}) collective-permute-start(bf16[128,1024]{1,0:T(8,128)(2,1)S(1)} %shard_map.55.refs_1_.refs_4_), channel_id=1, source_target_pairs={{0,8},{2,10},{4,12},{6,14},{8,0},{10,2},{12,4},{14,6},{16,24},{18,... | collective-permute-start | bytes 786440 | tf_op jit(solution)/shard_map/ppermute | solution.py:16
  51.4 2.0 %collective-permute-start.15 = (bf16[512,512]{1,0:T(8,128)(2,1)S(1)}, bf16[512,512]{1,0:T(8,128)(2,1)S(1)}, u32[]{:S(2)}, u32[]{:S(2)}) collective-permute-start(bf16[512,512]{1,0:T(8,128)(2,1)S(1)} %shard_map.59), channel_id=1, source_target_pairs={{0,2},{2,0},{4,6},{6,4},{8,10},{10,8},{12,14},{14,12},{16,18},{18,... | collective-permute-start | bytes 1572872 | tf_op jit(solution)/shard_map/ppermute | solution.py:16
  53.5 14.0 %collective-permute-start.20 = (bf16[512,512]{1,0:T(8,128)(2,1)S(1)}, bf16[512,512]{1,0:T(8,128)(2,1)S(1)}, u32[]{:S(2)}, u32[]{:S(2)}) collective-permute-start(bf16[512,512]{1,0:T(8,128)(2,1)S(1)} %add_convert_fusion.refs_2_), channel_id=1, source_target_pairs={{0,1},{1,0},{2,3},{3,2},{4,5},{5,4},{6,7},{7,6},{8,9},{9,8},{10,11... | collective-permute-start | bytes 1572872 | tf_op jit(solution)/shard_map/ppermute | solution.py:16
  55.8 1.6 %collective-permute-start.16 = (f32[128,512]{1,0:T(8,128)S(1)}, f32[128,512]{1,0:T(8,128)S(1)}, u32[]{:S(2)}, u32[]{:S(2)}) collective-permute-start(f32[128,512]{1,0:T(8,128)S(1)} %get-tuple-element.55), channel_id=1, source_target_pairs={{0,2},{2,0},{4,6},{6,4},{8,10},{10,8},{12,14},{14,12},{16,18},{18,... | collective-permute-start | bytes 786440 | tf_op jit(solution)/shard_map/ppermute | solution.py:16
  55.9 1.9 %collective-permute-start.17 = (f32[128,512]{1,0:T(8,128)S(1)}, f32[128,512]{1,0:T(8,128)S(1)}, u32[]{:S(2)}, u32[]{:S(2)}) collective-permute-start(f32[128,512]{1,0:T(8,128)S(1)} %get-tuple-element.58), channel_id=1, source_target_pairs={{0,2},{2,0},{4,6},{6,4},{8,10},{10,8},{12,14},{14,12},{16,18},{18,... | collective-permute-start | bytes 786440 | tf_op jit(solution)/shard_map/ppermute | solution.py:16
  56.4 1.8 %collective-permute-start.18 = (f32[128,512]{1,0:T(8,128)S(1)}, f32[128,512]{1,0:T(8,128)S(1)}, u32[]{:S(2)}, u32[]{:S(2)}) collective-permute-start(f32[128,512]{1,0:T(8,128)S(1)} %get-tuple-element.57), channel_id=1, source_target_pairs={{0,2},{2,0},{4,6},{6,4},{8,10},{10,8},{12,14},{14,12},{16,18},{18,... | collective-permute-start | bytes 786440 | tf_op jit(solution)/shard_map/ppermute | solution.py:16
  56.5 2.1 %collective-permute-start.19 = (f32[128,512]{1,0:T(8,128)S(1)}, f32[128,512]{1,0:T(8,128)S(1)}, u32[]{:S(2)}, u32[]{:S(2)}) collective-permute-start(f32[128,512]{1,0:T(8,128)S(1)} %get-tuple-element.56), channel_id=1, source_target_pairs={{0,2},{2,0},{4,6},{6,4},{8,10},{10,8},{12,14},{14,12},{16,18},{18,... | collective-permute-start | bytes 786440 | tf_op jit(solution)/shard_map/ppermute | solution.py:16

commit v5 on v4

--- a/solution.py
+++ b/solution.py
@@ -56,28 +56,8 @@
     )(tile)
 
 
-def join_kernel(*refs):
-    out, start = refs[-1], 0
-    for ref in refs[:-1]:
-        out[start : start + ref.shape[0]] = ref[...]
-        start += ref.shape[0]
-
-
-def join(blocks):
-    rows = sum(b.shape[0] for b in blocks)
-    whole = pl.BlockSpec(memory_space=pltpu.VMEM)
-    return pl.pallas_call(
-        join_kernel,
-        out_shape=pltpu.VMEM((rows, blocks[0].shape[1]), blocks[0].dtype),
-        in_specs=[whole] * len(blocks),
-        out_specs=whole,
-        compiler_params=pltpu.CompilerParams(vmem_limit_bytes=8 * MIB),
-        cost_estimate=pl.CostEstimate(flops=0, bytes_accessed=0, transcendentals=0),
-    )(*[in_vmem(b) for b in blocks])
-
-
 def absorb_kernel(plan, sizes, place, table, e_occ, e_half, e_col, *refs):
-    left_masks, block_plan, given, parts, n_addends = plan
+    left_masks, block_plan, given, parts = plan
     occupied, width = sizes
     n_left, n_block = len(left_masks), len(block_plan)
     n_total = n_left * len(parts)
@@ -87,7 +67,6 @@
     for is_given in given:
         olds.append(refs[at_old] if is_given else None)
         at_old += is_given
-    addends = refs[at_old : at_old + n_addends]
     news = refs[-n_total:]
     here, slot = place[0], place[1]
     half = e_half.shape[1]
@@ -149,8 +128,6 @@
                     preferred_element_type=jnp.float32,
                 )
                 total = term if total is None else total + term
-            if addends:
-                total = total + addends[n][at : at + CHUNK]
             news[n][at : at + CHUNK] = total.astype(news[n].dtype)
 
 
@@ -158,17 +135,17 @@
     return pltpu.with_memory_space_constraint(array, pltpu.VMEM)
 
 
-def absorb(context, width, lefts, blocks, parts, olds, cost, addends=(), kind=jnp.float32):
+def absorb(context, width, lefts, blocks, parts, olds, cost=0, kind=jnp.float32):
     virtuals, aux = lefts[0][0].shape
     keys = [(mask, q) for _, mask in lefts for q in parts]
     given = tuple(key in olds for key in keys)
     plan = (
-        tuple(m for _, m in lefts), tuple(tuple(r) for _, r in blocks), given, tuple(parts), len(addends)
+        tuple(m for _, m in lefts), tuple(tuple(r) for _, r in blocks), given, tuple(parts)
     )
     sizes = (context[2].shape[0], width)
     arrays = [in_vmem(a) for a, _ in lefts] + [in_vmem(b) for b, _ in blocks]
     base = len(context) + len(arrays)
-    arrays += [in_vmem(olds[key]) for key in keys if key in olds] + [in_vmem(a) for a in addends]
+    arrays += [in_vmem(olds[key]) for key in keys if key in olds]
     aliases = {}
     for i, is_given in enumerate(given):
         if is_given and kind == jnp.float32:
@@ -229,7 +206,7 @@
     ]
 
     def add(blocks, totals, parts=every, lefts=(own, other), **options):
-        return absorb(context, width, lefts, blocks, parts, totals, options.pop('cost', 0), **options)
+        return absorb(context, width, lefts, blocks, parts, totals, **options)
 
     def travel(members, h, after):
         for m in members:
@@ -249,14 +226,16 @@
     others = [m for level in levels[1:] for m in level]
     by = final & -final
     totals = add([(tile, [(0, ~r, h) for r in every for h in range(2)])], {}, [0], cost=1)
-    travel(singles, 0, [totals[0, 0]])
+    travel(singles, 0, [twin])
     for m in singles:
         side[m, 0] = exchange(line[m, 0], "blk", 2)
     (line[0, 1],) = gate([line[0, 1]], [twin])
     totals = add([(beside, [(2, 0, 0), (2, 0, 1)])], totals, cost=1)
-    travel(singles, 1, [totals[0, 0]])
+    after = [totals[0, 0]]
     for m in singles:
+        travel([m], 1, after)
         side[m, 1] = exchange(line[m, 1], "blk", 2)
+        after = [line[m, 1]]
     blocks = [lines_of(m, h) for m in singles for h in range(2)]
     blocks += [sides_of(m, 0) for m in singles]
     totals = add(blocks, totals, cost=1)

time: 69 us -> 68 us (0.986)
  waiting for transfers between devices: 30.1 us -> 25.9 us
  starting transfers between devices: 18 us -> 21.3 us
    ppermute x21, waiting for transfers between devices: 30.1 us -> 25.9 us  [exchange(): return lax.ppermute(block, axis, [(i, i ^ mask) for i in devices])]
    ppermute x21, starting transfers between devices: 18 us -> 21.3 us  [exchange(): return lax.ppermute(block, axis, [(i, i ^ mask) for i in devices])]
  transfers between devices with their start and end apart: 21 -> 21, of which waited for: 15 -> 13; matrix products, arithmetic and copies ran while one was open for 0% -> 1% of each run, Pallas kernels for 23% -> 23%
where the time goes in v5:
time: 68 us; the launch traced here: 67.8 us
  waiting for transfers between devices  25.9 us (38%)
  starting transfers between devices  21.3 us (31%)
  Pallas kernels  16.8 us (25%)
  local copies, waits for them, and re-layouts  2.09 us (3%)
  other arithmetic  1.55 us (2%)
    ppermute x21, waiting for transfers between devices, exchange(): return lax.ppermute(block, axis, [(i, i ^ mask) for i in devices])  25.9 us
    ppermute x21, starting transfers between devices, exchange(): return lax.ppermute(block, axis, [(i, i ^ mask) for i in devices])  21.3 us
    pallas_call x7, Pallas kernels, absorb(): pl.pallas_call(functools.partial(absorb_kernel, plan, sizes), out_shape=[...  16.7 us
    unnamed x10, local copies, waits for them, and re-layouts  1.88 us
  transfers between devices with their start and end apart: 21, of which 13 were waited for; matrix products, arithmetic and copies ran while one was open for 1% of the time, Pallas kernels for 23%

profile of v5, /device:TPU:0, one launch (start us, length us, event | category | flops | bytes accessed | tf_op | source)
XLA Modules:
  0.0 67.8 jit_solution(5778957992282294934)
XLA Ops:
  0.5 1.2 %copy-done = bf16[1,512,1024]{2,1,0:T(8,128)(2,1)S(1)} copy-done((bf16[1,512,1024]{2,1,0:T(8,128)(2,1)S(1)}, bf16[1,512,1024]{2,1,0:T(8,128)(2,1)}, u32[]{:S(2)}) %copy-start) | copy-done | bytes 1048600
  1.8 3.7 %collective-permute-start.2 = (bf16[128,1024]{1,0:T(8,128)(2,1)S(1)}, bf16[128,1024]{1,0:T(8,128)(2,1)S(1)}, u32[]{:S(2)}, u32[]{:S(2)}) collective-permute-start(bf16[128,1024]{1,0:T(8,128)(2,1)S(1)} %get-tuple-element.28), channel_id=1, source_target_pairs={{0,16},{2,18},{4,20},{6,22},{8,24},{10,26},{12,28},{14,30},{16,0},... | collective-permute-start | bytes 786440 | tf_op jit(solution)/shard_map/ppermute | solution.py:16
  5.4 1.6 %collective-permute-start.3 = (bf16[128,1024]{1,0:T(8,128)(2,1)S(1)}, bf16[128,1024]{1,0:T(8,128)(2,1)S(1)}, u32[]{:S(2)}, u32[]{:S(2)}) collective-permute-start(bf16[128,1024]{1,0:T(8,128)(2,1)S(1)} %get-tuple-element.28), channel_id=1, source_target_pairs={{0,8},{2,10},{4,12},{6,14},{8,0},{10,2},{12,4},{14,6},{16,24},{18,... | collective-permute-start | bytes 786440 | tf_op jit(solution)/shard_map/ppermute | solution.py:16
  7.0 1.5 %collective-permute-start.6 = (bf16[256,1024]{1,0:T(8,128)(2,1)S(1)}, bf16[256,1024]{1,0:T(8,128)(2,1)S(1)}, u32[]{:S(2)}, u32[]{:S(2)}) collective-permute-start(bf16[256,1024]{1,0:T(8,128)(2,1)S(1)} %shard_map.49), channel_id=1, source_target_pairs={{0,4},{2,6},{4,0},{6,2},{8,12},{10,14},{12,8},{14,10},{16,20},{18,... | collective-permute-start | bytes 1572872 | tf_op jit(solution)/shard_map/ppermute | solution.py:16
  8.5 1.5 %collective-permute-start = (s32[4]{0:T(128)S(1)}, s32[4]{0:T(128)S(1)}, u32[]{:S(2)}, u32[]{:S(2)}) collective-permute-start(s32[4]{0:T(128)S(1)} %copy-done.4), channel_id=1, source_target_pairs={{0,1},{1,0},{2,3},{3,2},{4,5},{5,4},{6,7},{7,6},{8,9},{9,8},{10,11... | collective-permute-start | bytes 56 | tf_op jit(solution)/shard_map/ppermute | solution.py:16
  10.5 7.9 %collective-permute-done.2.refs_0_ = bf16[128,1024]{1,0:T(8,128)(2,1)S(1)} collective-permute-done((bf16[128,1024]{1,0:T(8,128)(2,1)S(1)}, bf16[128,1024]{1,0:T(8,128)(2,1)S(1)}, u32[]{:S(2)}, u32[]{:S(2)}) %collective-permute-start.2) | collective-permute-done | bytes 262176 | tf_op jit(solution)/shard_map/ppermute | solution.py:16
  18.3 0.6 collective-permute-start.7
  19.3 1.5 %collective-permute-start.8 = (bf16[128,1024]{1,0:T(8,128)(2,1)S(1)}, bf16[128,1024]{1,0:T(8,128)(2,1)S(1)}, u32[]{:S(2)}, u32[]{:S(2)}) collective-permute-start(bf16[128,1024]{1,0:T(8,128)(2,1)S(1)} %get-tuple-element.29.refs_2_), channel_id=1, source_target_pairs={{0,4},{2,6},{4,0},{6,2},{8,12},{10,14},{12,8},{14,10},{16,20},{18,... | collective-permute-start | bytes 786440 | tf_op jit(solution)/shard_map/ppermute | solution.py:16
  20.8 0.5 collective-permute-start.9
  21.5 0.6 copy-done.3
  22.2 2.4 %shard_map.50 = (f32[512,512]{1,0:T(8,128)S(1)}, f32[512,512]{1,0:T(8,128)S(1)}) custom-call(s32[2]{0:T(128)S(1)} %pad_add_fusion.place, s32[8]{0:T(128)S(1)} %pad_add_fusion.1.table, f32[16]{0:T(128)S(1)} %copy-done.3, f32[4,128]{1,0:T(4,128)S(1)} %bitcast.15, f32[512,128]{1,0:T(8,128)S(1)} %broadcast_in_dim.4.e_col, bf16[512,1024]{1,0:T(8,128)(2,1)S(1)} %bitcast.8, ...), custom_call_target="tpu_custom_call" | custom-call | flops 1610612736 | tf_op jit(solution)/shard_map/pallas_call | solution.py:156
  24.6 1.2 %collective-permute-start.4 = (bf16[128,1024]{1,0:T(8,128)(2,1)S(1)}, bf16[128,1024]{1,0:T(8,128)(2,1)S(1)}, u32[]{:S(2)}, u32[]{:S(2)}) collective-permute-start(bf16[128,1024]{1,0:T(8,128)(2,1)S(1)} %get-tuple-element.29.refs_2_), channel_id=1, source_target_pairs={{0,8},{2,10},{4,12},{6,14},{8,0},{10,2},{12,4},{14,6},{16,24},{18,... | collective-permute-start | bytes 786440 | tf_op jit(solution)/shard_map/ppermute | solution.py:16
  25.7 1.9 %shard_map.51 = (f32[512,512]{1,0:T(8,128)S(1)}, f32[512,512]{1,0:T(8,128)S(1)}, f32[512,512]{1,0:T(8,128)S(1)}, f32[512,512]{1,0:T(8,128)S(1)}) custom-call(s32[2]{0:T(128)S(1)} %pad_add_fusion.place, s32[8]{0:T(128)S(1)} %pad_add_fusion.1.table, f32[16]{0:T(128)S(1)} %copy-done.3, ...), custom_call_target="tpu_custom_call", output_to_operand_aliasing={{0}: (8, {}), {2}: (9, {})} | custom-call | flops 1073741824 | tf_op jit(solution)/shard_map/pallas_call | solution.py:156
  27.7 1.8 %collective-permute-done.5.refs_0_ = bf16[128,1024]{1,0:T(8,128)(2,1)S(1)} collective-permute-done((bf16[128,1024]{1,0:T(8,128)(2,1)S(1)}, bf16[128,1024]{1,0:T(8,128)(2,1)S(1)}, u32[]{:S(2)}, u32[]{:S(2)}) %collective-permute-start.5) | collective-permute-done | bytes 262176 | tf_op jit(solution)/shard_map/ppermute | solution.py:16
  29.4 1.5 %collective-permute-start.11 = (bf16[128,1024]{1,0:T(8,128)(2,1)S(1)}, bf16[128,1024]{1,0:T(8,128)(2,1)S(1)}, u32[]{:S(2)}, u32[]{:S(2)}) collective-permute-start(bf16[128,1024]{1,0:T(8,128)(2,1)S(1)} %shard_map.52.refs_1_.refs_3_), channel_id=1, source_target_pairs={{0,4},{2,6},{4,0},{6,2},{8,12},{10,14},{12,8},{14,10},{16,20},{18,... | collective-permute-start | bytes 786440 | tf_op jit(solution)/shard_map/ppermute | solution.py:16
  31.0 0.9 %collective-permute-done.7.refs_0_ = bf16[128,1024]{1,0:T(8,128)(2,1)S(1)} collective-permute-done((bf16[128,1024]{1,0:T(8,128)(2,1)S(1)}, bf16[128,1024]{1,0:T(8,128)(2,1)S(1)}, u32[]{:S(2)}, u32[]{:S(2)}) %collective-permute-start.7) | collective-permute-done | bytes 262176 | tf_op jit(solution)/shard_map/ppermute | solution.py:16
  31.9 1.3 %collective-permute-start.14 = (bf16[128,1024]{1,0:T(8,128)(2,1)S(1)}, bf16[128,1024]{1,0:T(8,128)(2,1)S(1)}, u32[]{:S(2)}, u32[]{:S(2)}) collective-permute-start(bf16[128,1024]{1,0:T(8,128)(2,1)S(1)} %shard_map.53.refs_5_), channel_id=1, source_target_pairs={{0,4},{2,6},{4,0},{6,2},{8,12},{10,14},{12,8},{14,10},{16,20},{18,... | collective-permute-start | bytes 786440 | tf_op jit(solution)/shard_map/ppermute | solution.py:16
  33.2 4.7 %shard_map.54 = (f32[512,512]{1,0:T(8,128)S(1)}, f32[512,512]{1,0:T(8,128)S(1)}, f32[512,512]{1,0:T(8,128)S(1)}, f32[512,512]{1,0:T(8,128)S(1)}) custom-call(s32[2]{0:T(128)S(1)} %pad_add_fusion.place, s32[8]{0:T(128)S(1)} %pad_add_fusion.1.table, f32[16]{0:T(128)S(1)} %copy-done.3, ...), custom_call_target="tpu_custom_call", output_to_operand_aliasing={{0}: (13, {}), {1}: (14, {}), {2}: (15, {}), {3}: (16, {})} | custom-call | flops 3221225472 | tf_op jit(solution)/shard_map/pallas_call | solution.py:156
  37.9 1.2 %collective-permute-start.10 = (bf16[128,1024]{1,0:T(8,128)(2,1)S(1)}, bf16[128,1024]{1,0:T(8,128)(2,1)S(1)}, u32[]{:S(2)}, u32[]{:S(2)}) collective-permute-start(bf16[128,1024]{1,0:T(8,128)(2,1)S(1)} %shard_map.55.refs_2_), channel_id=1, source_target_pairs={{0,4},{2,6},{4,0},{6,2},{8,12},{10,14},{12,8},{14,10},{16,20},{18,... | collective-permute-start | bytes 786440 | tf_op jit(solution)/shard_map/ppermute | solution.py:16
  39.1 1.6 %collective-permute-start.12 = (bf16[128,1024]{1,0:T(8,128)(2,1)S(1)}, bf16[128,1024]{1,0:T(8,128)(2,1)S(1)}, u32[]{:S(2)}, u32[]{:S(2)}) collective-permute-start(bf16[128,1024]{1,0:T(8,128)(2,1)S(1)} %shard_map.56.refs_1_.refs_4_), channel_id=1, source_target_pairs={{0,8},{2,10},{4,12},{6,14},{8,0},{10,2},{12,4},{14,6},{16,24},{18,... | collective-permute-start | bytes 786440 | tf_op jit(solution)/shard_map/ppermute | solution.py:16
  40.8 2.3 %collective-permute-done.13.refs_0_ = bf16[128,1024]{1,0:T(8,128)(2,1)S(1)} collective-permute-done((bf16[128,1024]{1,0:T(8,128)(2,1)S(1)}, bf16[128,1024]{1,0:T(8,128)(2,1)S(1)}, u32[]{:S(2)}, u32[]{:S(2)}) %collective-permute-start.13) | collective-permute-done | bytes 262176 | tf_op jit(solution)/shard_map/ppermute | solution.py:16
  43.1 1.1 %collective-permute-done.14.refs_5_ = bf16[128,1024]{1,0:T(8,128)(2,1)S(1)} collective-permute-done((bf16[128,1024]{1,0:T(8,128)(2,1)S(1)}, bf16[128,1024]{1,0:T(8,128)(2,1)S(1)}, u32[]{:S(2)}, u32[]{:S(2)}) %collective-permute-start.14) | collective-permute-done | bytes 262176 | tf_op jit(solution)/shard_map/ppermute | solution.py:16
  44.2 3.5 %shard_map.58 = (f32[512,512]{1,0:T(8,128)S(1)}, f32[512,512]{1,0:T(8,128)S(1)}, f32[512,512]{1,0:T(8,128)S(1)}, f32[512,512]{1,0:T(8,128)S(1)}) custom-call(s32[2]{0:T(128)S(1)} %pad_add_fusion.place, s32[8]{0:T(128)S(1)} %pad_add_fusion.1.table, f32[16]{0:T(128)S(1)} %copy-done.3, ...), custom_call_target="tpu_custom_call", output_to_operand_aliasing={{0}: (11, {}), {1}: (12, {}), {2}: (13, {}), {3}: (14, {})} | custom-call | tf_op jit(solution)/shard_map/pallas_call | solution.py:156
  47.8 1.4 %collective-permute-done.10.refs_1_.refs_0_ = bf16[128,1024]{1,0:T(8,128)(2,1)S(1)} collective-permute-done((bf16[128,1024]{1,0:T(8,128)(2,1)S(1)}, bf16[128,1024]{1,0:T(8,128)(2,1)S(1)}, u32[]{:S(2)}, u32[]{:S(2)}) %collective-permute-start.10) | collective-permute-done | bytes 262176 | tf_op jit(solution)/shard_map/ppermute | solution.py:16
  49.2 1.2 %shard_map.60 = bf16[512,512]{1,0:T(8,128)(2,1)S(1)} custom-call(s32[2]{0:T(128)S(1)} %pad_add_fusion.place, s32[8]{0:T(128)S(1)} %pad_add_fusion.1.table, f32[16]{0:T(128)S(1)} %copy-done.3, f32[4,128]{1,0:T(4,128)S(1)} %bitcast.19, f32[512,128]{1,0:T(8,128)S(1)} %broadcast_in_dim.4.e_col, ...), custom_call_target="tpu_custom_call" | custom-call | tf_op jit(solution)/shard_map/pallas_call | solution.py:156
  50.5 1.3 %shard_map.59 = f32[512,512]{1,0:T(8,128)S(1)} custom-call(s32[2]{0:T(128)S(1)} %pad_add_fusion.place, s32[8]{0:T(128)S(1)} %pad_add_fusion.1.table, f32[16]{0:T(128)S(1)} %copy-done.3, f32[4,128]{1,0:T(4,128)S(1)} %bitcast.20, f32[512,128]{1,0:T(8,128)S(1)} %broadcast_in_dim.4.e_col, ...), custom_call_target="tpu_custom_call", output_to_operand_aliasing={{}: (8, {})} | custom-call | tf_op jit(solution)/shard_map/pallas_call | solution.py:156
  51.8 0.6 collective-permute-done.15
  52.6 1.6 %collective-permute-start.20 = (bf16[512,512]{1,0:T(8,128)(2,1)S(1)}, bf16[512,512]{1,0:T(8,128)(2,1)S(1)}, u32[]{:S(2)}, u32[]{:S(2)}) collective-permute-start(bf16[512,512]{1,0:T(8,128)(2,1)S(1)} %add_convert_fusion.refs_2_), channel_id=1, source_target_pairs={{0,1},{1,0},{2,3},{3,2},{4,5},{5,4},{6,7},{7,6},{8,9},{9,8},{10,11... | collective-permute-start | bytes 1572872 | tf_op jit(solution)/shard_map/ppermute | solution.py:16
  54.1 1.6 %shard_map.62 = (f32[512,512]{1,0:T(8,128)S(1)}, f32[512,512]{1,0:T(8,128)S(1)}) custom-call(s32[2]{0:T(128)S(1)} %pad_add_fusion.place, s32[8]{0:T(128)S(1)} %pad_add_fusion.1.table, f32[16]{0:T(128)S(1)} %copy-done.3, f32[4,128]{1,0:T(4,128)S(1)} %bitcast.21, f32[512,128]{1,0:T(8,128)S(1)} %broadcast_in_dim.4.e_col, ...), custom_call_target="tpu_custom_call", output_to_operand_aliasing={{0}: (9, {}), {1}: (10, {})} | custom-call | tf_op jit(solution)/shard_map/pallas_call | solution.py:156
  56.9 0.5 collective-permute-done.16
  58.6 8.0 %collective-permute-done.20 = bf16[512,512]{1,0:T(8,128)(2,1)S(1)} collective-permute-done((bf16[512,512]{1,0:T(8,128)(2,1)S(1)}, bf16[512,512]{1,0:T(8,128)(2,1)S(1)}, u32[]{:S(2)}, u32[]{:S(2)}) %collective-permute-start.20) | collective-permute-done | bytes 524320 | tf_op jit(solution)/shard_map/ppermute | solution.py:16
  66.6 1.2 %fusion.1 = f32[1,512,512]{2,1,0:T(8,128)} fusion(f32[512,512]{1,0:T(8,128)S(1)} %get-tuple-element.49, f32[128,512]{1,0:T(8,128)S(1)} %collective-permute-done.19, f32[128,512]{1,0:T(8,128)S(1)} %collective-permute-done.18, f32[128,512]{1,0:T(8,128)S(1)} %collective-permute-done.17, f32[128,512]{1,0:T(8,128)S(1)} %collective-permute-done.16, ...), kind=kLoop, calls=%fused_computation.2 | loop fusion | flops 1572864 | bytes 3670016 | tf_op jit(solution)/shard_map/broadcast_in_dim | solution.py:273
  (43 shorter events, 4.0 us)
Async XLA Ops:
  0.0 7.0 %collective-permute-start.1 = (bf16[512,1024]{1,0:T(8,128)(2,1)}, bf16[512,1024]{1,0:T(8,128)(2,1)S(1)}, u32[]{:S(2)}, u32[]{:S(2)}) collective-permute-start(bf16[512,1024]{1,0:T(8,128)(2,1)} %bitcast.6), channel_id=1, source_target_pairs={{0,2},{2,0},{4,6},{6,4},{8,10},{10,8},{12,14},{14,12},{16,18},{18,... | collective-permute-start | bytes 3145736 | tf_op jit(solution)/shard_map/ppermute | solution.py:16
  0.5 1.2 %copy-start = (bf16[1,512,1024]{2,1,0:T(8,128)(2,1)S(1)}, bf16[1,512,1024]{2,1,0:T(8,128)(2,1)}, u32[]{:S(2)}) copy-start(bf16[1,512,1024]{2,1,0:T(8,128)(2,1)} %param.4) | copy-start | bytes 3145732
  1.8 16.5 %collective-permute-start.2 = (bf16[128,1024]{1,0:T(8,128)(2,1)S(1)}, bf16[128,1024]{1,0:T(8,128)(2,1)S(1)}, u32[]{:S(2)}, u32[]{:S(2)}) collective-permute-start(bf16[128,1024]{1,0:T(8,128)(2,1)S(1)} %get-tuple-element.28), channel_id=1, source_target_pairs={{0,16},{2,18},{4,20},{6,22},{8,24},{10,26},{12,28},{14,30},{16,0},... | collective-permute-start | bytes 786440 | tf_op jit(solution)/shard_map/ppermute | solution.py:16
  5.4 13.8 %collective-permute-start.3 = (bf16[128,1024]{1,0:T(8,128)(2,1)S(1)}, bf16[128,1024]{1,0:T(8,128)(2,1)S(1)}, u32[]{:S(2)}, u32[]{:S(2)}) collective-permute-start(bf16[128,1024]{1,0:T(8,128)(2,1)S(1)} %get-tuple-element.28), channel_id=1, source_target_pairs={{0,8},{2,10},{4,12},{6,14},{8,0},{10,2},{12,4},{14,6},{16,24},{18,... | collective-permute-start | bytes 786440 | tf_op jit(solution)/shard_map/ppermute | solution.py:16
  7.0 1.5 %copy-start.4 = (s32[4]{0:T(128)S(1)}, s32[4]{0:T(128)}, u32[]{:S(2)}) copy-start(s32[4]{0:T(128)} %param.7) | copy-start | bytes 52
  7.0 17.5 %collective-permute-start.6 = (bf16[256,1024]{1,0:T(8,128)(2,1)S(1)}, bf16[256,1024]{1,0:T(8,128)(2,1)S(1)}, u32[]{:S(2)}, u32[]{:S(2)}) collective-permute-start(bf16[256,1024]{1,0:T(8,128)(2,1)S(1)} %shard_map.49), channel_id=1, source_target_pairs={{0,4},{2,6},{4,0},{6,2},{8,12},{10,14},{12,8},{14,10},{16,20},{18,... | collective-permute-start | bytes 1572872 | tf_op jit(solution)/shard_map/ppermute | solution.py:16
  8.5 12.2 %collective-permute-start = (s32[4]{0:T(128)S(1)}, s32[4]{0:T(128)S(1)}, u32[]{:S(2)}, u32[]{:S(2)}) collective-permute-start(s32[4]{0:T(128)S(1)} %copy-done.4), channel_id=1, source_target_pairs={{0,1},{1,0},{2,3},{3,2},{4,5},{5,4},{6,7},{7,6},{8,9},{9,8},{10,11... | collective-permute-start | bytes 56 | tf_op jit(solution)/shard_map/ppermute | solution.py:16
  10.1 11.4 %copy-start.1 = (bf16[1,512,1024]{2,1,0:T(8,128)(2,1)S(1)}, bf16[1,512,1024]{2,1,0:T(8,128)(2,1)}, u32[]{:S(2)}) copy-start(bf16[1,512,1024]{2,1,0:T(8,128)(2,1)} %param.4) | copy-start | bytes 3145732
  10.1 19.3 %collective-permute-start.5 = (bf16[128,1024]{1,0:T(8,128)(2,1)S(1)}, bf16[128,1024]{1,0:T(8,128)(2,1)S(1)}, u32[]{:S(2)}, u32[]{:S(2)}) collective-permute-start(bf16[128,1024]{1,0:T(8,128)(2,1)S(1)} %shard_map.48), channel_id=1, source_target_pairs={{0,16},{2,18},{4,20},{6,22},{8,24},{10,26},{12,28},{14,30},{16,0},... | collective-permute-start | bytes 786440 | tf_op jit(solution)/shard_map/ppermute | solution.py:16
  18.3 13.5 %collective-permute-start.7 = (bf16[128,1024]{1,0:T(8,128)(2,1)S(1)}, bf16[128,1024]{1,0:T(8,128)(2,1)S(1)}, u32[]{:S(2)}, u32[]{:S(2)}) collective-permute-start(bf16[128,1024]{1,0:T(8,128)(2,1)S(1)} %shard_map.48), channel_id=1, source_target_pairs={{0,8},{2,10},{4,12},{6,14},{8,0},{10,2},{12,4},{14,6},{16,24},{18,... | collective-permute-start | bytes 786440 | tf_op jit(solution)/shard_map/ppermute | solution.py:16
  19.3 2.1 %copy-start.2 = (f32[512]{0:T(512)S(1)}, f32[512]{0:T(512)}, u32[]{:S(2)}) copy-start(f32[512]{0:T(512)} %param.6) | copy-start | bytes 6148
  19.3 12.6 %collective-permute-start.8 = (bf16[128,1024]{1,0:T(8,128)(2,1)S(1)}, bf16[128,1024]{1,0:T(8,128)(2,1)S(1)}, u32[]{:S(2)}, u32[]{:S(2)}) collective-permute-start(bf16[128,1024]{1,0:T(8,128)(2,1)S(1)} %get-tuple-element.29.refs_2_), channel_id=1, source_target_pairs={{0,4},{2,6},{4,0},{6,2},{8,12},{10,14},{12,8},{14,10},{16,20},{18,... | collective-permute-start | bytes 786440 | tf_op jit(solution)/shard_map/ppermute | solution.py:16
  20.8 12.4 %collective-permute-start.9 = (bf16[128,1024]{1,0:T(8,128)(2,1)S(1)}, bf16[128,1024]{1,0:T(8,128)(2,1)S(1)}, u32[]{:S(2)}, u32[]{:S(2)}) collective-permute-start(bf16[128,1024]{1,0:T(8,128)(2,1)S(1)} %get-tuple-element.35.refs_4_), channel_id=1, source_target_pairs={{0,4},{2,6},{4,0},{6,2},{8,12},{10,14},{12,8},{14,10},{16,20},{18,... | collective-permute-start | bytes 786440 | tf_op jit(solution)/shard_map/ppermute | solution.py:16
  21.5 0.7 copy-start.3
  24.6 13.4 %collective-permute-start.4 = (bf16[128,1024]{1,0:T(8,128)(2,1)S(1)}, bf16[128,1024]{1,0:T(8,128)(2,1)S(1)}, u32[]{:S(2)}, u32[]{:S(2)}) collective-permute-start(bf16[128,1024]{1,0:T(8,128)(2,1)S(1)} %get-tuple-element.29.refs_2_), channel_id=1, source_target_pairs={{0,8},{2,10},{4,12},{6,14},{8,0},{10,2},{12,4},{14,6},{16,24},{18,... | collective-permute-start | bytes 786440 | tf_op jit(solution)/shard_map/ppermute | solution.py:16
  29.4 9.7 %collective-permute-start.11 = (bf16[128,1024]{1,0:T(8,128)(2,1)S(1)}, bf16[128,1024]{1,0:T(8,128)(2,1)S(1)}, u32[]{:S(2)}, u32[]{:S(2)}) collective-permute-start(bf16[128,1024]{1,0:T(8,128)(2,1)S(1)} %shard_map.52.refs_1_.refs_3_), channel_id=1, source_target_pairs={{0,4},{2,6},{4,0},{6,2},{8,12},{10,14},{12,8},{14,10},{16,20},{18,... | collective-permute-start | bytes 786440 | tf_op jit(solution)/shard_map/ppermute | solution.py:16
  31.9 11.2 %collective-permute-start.13 = (bf16[128,1024]{1,0:T(8,128)(2,1)S(1)}, bf16[128,1024]{1,0:T(8,128)(2,1)S(1)}, u32[]{:S(2)}, u32[]{:S(2)}) collective-permute-start(bf16[128,1024]{1,0:T(8,128)(2,1)S(1)} %shard_map.52.refs_1_.refs_3_), channel_id=1, source_target_pairs={{0,8},{2,10},{4,12},{6,14},{8,0},{10,2},{12,4},{14,6},{16,24},{18,... | collective-permute-start | bytes 786440 | tf_op jit(solution)/shard_map/ppermute | solution.py:16
  31.9 12.4 %collective-permute-start.14 = (bf16[128,1024]{1,0:T(8,128)(2,1)S(1)}, bf16[128,1024]{1,0:T(8,128)(2,1)S(1)}, u32[]{:S(2)}, u32[]{:S(2)}) collective-permute-start(bf16[128,1024]{1,0:T(8,128)(2,1)S(1)} %shard_map.53.refs_5_), channel_id=1, source_target_pairs={{0,4},{2,6},{4,0},{6,2},{8,12},{10,14},{12,8},{14,10},{16,20},{18,... | collective-permute-start | bytes 786440 | tf_op jit(solution)/shard_map/ppermute | solution.py:16
  37.9 11.2 %collective-permute-start.10 = (bf16[128,1024]{1,0:T(8,128)(2,1)S(1)}, bf16[128,1024]{1,0:T(8,128)(2,1)S(1)}, u32[]{:S(2)}, u32[]{:S(2)}) collective-permute-start(bf16[128,1024]{1,0:T(8,128)(2,1)S(1)} %shard_map.55.refs_2_), channel_id=1, source_target_pairs={{0,4},{2,6},{4,0},{6,2},{8,12},{10,14},{12,8},{14,10},{16,20},{18,... | collective-permute-start | bytes 786440 | tf_op jit(solution)/shard_map/ppermute | solution.py:16
  39.1 10.0 %collective-permute-start.12 = (bf16[128,1024]{1,0:T(8,128)(2,1)S(1)}, bf16[128,1024]{1,0:T(8,128)(2,1)S(1)}, u32[]{:S(2)}, u32[]{:S(2)}) collective-permute-start(bf16[128,1024]{1,0:T(8,128)(2,1)S(1)} %shard_map.56.refs_1_.refs_4_), channel_id=1, source_target_pairs={{0,8},{2,10},{4,12},{6,14},{8,0},{10,2},{12,4},{14,6},{16,24},{18,... | collective-permute-start | bytes 786440 | tf_op jit(solution)/shard_map/ppermute | solution.py:16
  50.4 2.0 %collective-permute-start.15 = (bf16[512,512]{1,0:T(8,128)(2,1)S(1)}, bf16[512,512]{1,0:T(8,128)(2,1)S(1)}, u32[]{:S(2)}, u32[]{:S(2)}) collective-permute-start(bf16[512,512]{1,0:T(8,128)(2,1)S(1)} %shard_map.60), channel_id=1, source_target_pairs={{0,2},{2,0},{4,6},{6,4},{8,10},{10,8},{12,14},{14,12},{16,18},{18,... | collective-permute-start | bytes 1572872 | tf_op jit(solution)/shard_map/ppermute | solution.py:16
  52.6 14.0 %collective-permute-start.20 = (bf16[512,512]{1,0:T(8,128)(2,1)S(1)}, bf16[512,512]{1,0:T(8,128)(2,1)S(1)}, u32[]{:S(2)}, u32[]{:S(2)}) collective-permute-start(bf16[512,512]{1,0:T(8,128)(2,1)S(1)} %add_convert_fusion.refs_2_), channel_id=1, source_target_pairs={{0,1},{1,0},{2,3},{3,2},{4,5},{5,4},{6,7},{7,6},{8,9},{9,8},{10,11... | collective-permute-start | bytes 1572872 | tf_op jit(solution)/shard_map/ppermute | solution.py:16
  55.8 1.6 %collective-permute-start.16 = (f32[128,512]{1,0:T(8,128)S(1)}, f32[128,512]{1,0:T(8,128)S(1)}, u32[]{:S(2)}, u32[]{:S(2)}) collective-permute-start(f32[128,512]{1,0:T(8,128)S(1)} %get-tuple-element.51), channel_id=1, source_target_pairs={{0,2},{2,0},{4,6},{6,4},{8,10},{10,8},{12,14},{14,12},{16,18},{18,... | collective-permute-start | bytes 786440 | tf_op jit(solution)/shard_map/ppermute | solution.py:16
  55.9 1.9 %collective-permute-start.17 = (f32[128,512]{1,0:T(8,128)S(1)}, f32[128,512]{1,0:T(8,128)S(1)}, u32[]{:S(2)}, u32[]{:S(2)}) collective-permute-start(f32[128,512]{1,0:T(8,128)S(1)} %get-tuple-element.54), channel_id=1, source_target_pairs={{0,2},{2,0},{4,6},{6,4},{8,10},{10,8},{12,14},{14,12},{16,18},{18,... | collective-permute-start | bytes 786440 | tf_op jit(solution)/shard_map/ppermute | solution.py:16
  56.4 1.8 %collective-permute-start.18 = (f32[128,512]{1,0:T(8,128)S(1)}, f32[128,512]{1,0:T(8,128)S(1)}, u32[]{:S(2)}, u32[]{:S(2)}) collective-permute-start(f32[128,512]{1,0:T(8,128)S(1)} %get-tuple-element.53), channel_id=1, source_target_pairs={{0,2},{2,0},{4,6},{6,4},{8,10},{10,8},{12,14},{14,12},{16,18},{18,... | collective-permute-start | bytes 786440 | tf_op jit(solution)/shard_map/ppermute | solution.py:16
  56.5 2.1 %collective-permute-start.19 = (f32[128,512]{1,0:T(8,128)S(1)}, f32[128,512]{1,0:T(8,128)S(1)}, u32[]{:S(2)}, u32[]{:S(2)}) collective-permute-start(f32[128,512]{1,0:T(8,128)S(1)} %get-tuple-element.52), channel_id=1, source_target_pairs={{0,2},{2,0},{4,6},{6,4},{8,10},{10,8},{12,14},{14,12},{16,18},{18,... | collective-permute-start | bytes 786440 | tf_op jit(solution)/shard_map/ppermute | solution.py:16
